TPU v7x, 128 devices: a whole 4x4x4 slice. The times are simulated.
128 devices in a mesh: lat: 8 (over z, x_hi), lon: 16 (over y, x_lo, core).
Axes of the slice: x: 4 (x_hi: 2, x_lo: 2; x = x_hi * 2 + x_lo), y: 4, z: 4, core: 2. Of those that a mesh axis runs over, the one named last changes fastest.
Arguments:
- grid_inputs: bfloat16 [8, 16, 1024, 474], P('lat', 'lon'), may hold values from -6 to 6
- mesh_state: bfloat16 [8, 16, 128, 512], P('lat', 'lon'), may hold values from -6 to 6
- embed_in: bfloat16 [474, 512], replicated, may hold values from -0.25 to 0.25
- embed_out: bfloat16 [512, 512], replicated, may hold values from -0.25 to 0.25
- edge_square: bfloat16 [3, 3, 512, 512], replicated, may hold values from -0.25 to 0.25
- edge_geom_weight: float32 [3, 4, 512], replicated, may hold values from -3 to 3
- node_first: bfloat16 [3, 1024, 512], replicated, may hold values from -0.1875 to 0.1875
- node_second: bfloat16 [2, 512, 512], replicated, may hold values from -0.25 to 0.25
- head: bfloat16 [512, 227], replicated, may hold values from -0.25 to 0.25
- g2m_senders: int32 [8, 16, 2048], P('lat', 'lon'), may hold values from 0 to 9215, as said below
- g2m_receivers: int32 [8, 16, 2048], P('lat', 'lon'), may hold values from 0 to 127
- g2m_counts: int32 [8, 16], P('lat', 'lon'), may hold values from 1024 to 2048, as said below
- g2m_geom: float32 [8, 16, 4, 2048], P('lat', 'lon'), may hold values from -6 to 6
- mesh_senders: int32 [8, 16, 768], P('lat', 'lon'), may hold values from 0 to 1151, as said below
- mesh_geom: float32 [8, 16, 4, 768], P('lat', 'lon'), may hold values from -6 to 6
- coarse_senders: int32 [8, 16, 256], P('lat', 'lon'), may hold values from 0 to 2047
- coarse_receivers: int32 [8, 16, 256], P('lat', 'lon'), may hold values from 0 to 2047, as said below
- coarse_geom: float32 [8, 16, 4, 256], P('lat', 'lon'), may hold values from -6 to 6
- m2g_senders: int32 [8, 16, 3072], P('lat', 'lon'), may hold values from 0 to 1151, as said below
- m2g_geom: float32 [8, 16, 4, 3072], P('lat', 'lon'), may hold values from -6 to 6
Outputs:
- grid_outputs: bfloat16 [8, 16, 1024, 227], P('lat', 'lon')
Inputs may be any that keep to these rules, and one draw needn't show every extreme that they name: `g2m_senders`: index s names node s % 1024 of neighbour s // 1024 of the tile; never a neighbour beyond the first or last band. `mesh_senders`: index s names node s % 128 of neighbour s // 128 of the tile; never a neighbour beyond the first or last band. `m2g_senders`: index s names node s % 128 of neighbour s // 128 of the tile; never a neighbour beyond the first or last band. `g2m_counts`: sector 0 of the first and last bands uses all 2048 slots; sector 0 of the band or bands farthest from both ends uses 2048 // 2. `coarse_receivers`: an edge of a tile enters a coarse node of that tile, of the tile before it in the numbering (counted round), or of the tile half the numbering away.
All inputs are finite; a program needn't handle non-finite values.
Results may differ from a plain program's by a relative error of at most 0.019.
Values may be sent and summed in bfloat16 or wider, within the bound.
No kernel may reach another device: no remote copies, remote signals or barrier semaphores. Data moves between devices by JAX's collectives and lax.ppermute only.
A program may use at most 128 MiB of HBM per device.

v0:
```python
import jax
import jax.numpy as jnp
from jax import lax
from jax.sharding import PartitionSpec as P

MESH_DEGREE = 6
GRID_DEGREE = 3
COARSE_DEV = 16


def extended(block, sides, width, periodic):
    for axis, dim in sides:
        count = lax.axis_size(axis)
        forward = [(i, i + 1) for i in range(count - 1)]
        if periodic:
            forward.append((count - 1, 0))
        backward = [(target, source) for source, target in forward]
        low = lax.ppermute(
            lax.slice_in_dim(block, block.shape[dim] - width, None, axis=dim), axis, forward
        )
        high = lax.ppermute(lax.slice_in_dim(block, 0, width, axis=dim), axis, backward)
        block = jnp.concatenate([low, block, high], axis=dim)
    return block


def product(left, right):
    return jnp.dot(left, right, preferred_element_type=jnp.float32)


def messages(sender_rows, receiver_rows, geometry, geom_weight, second):
    embedded = jnp.einsum("ce,cd->ed", geometry, geom_weight, precision=lax.Precision.HIGHEST)
    pre = embedded + sender_rows.astype(jnp.float32) + receiver_rows.astype(jnp.float32)
    hidden = jax.nn.silu(pre).astype(jnp.bfloat16)
    return product(hidden, second).astype(jnp.bfloat16)


def node_update(node_rows, summed, first_layer, second_layer):
    latent_width = node_rows.shape[1]
    inner = product(node_rows, first_layer[:latent_width]) + product(
        summed.astype(jnp.bfloat16), first_layer[latent_width:]
    )
    hidden = jax.nn.silu(inner).astype(jnp.bfloat16)
    return (node_rows.astype(jnp.float32) + product(hidden, second_layer)).astype(jnp.bfloat16)


def neighbourhood(field):
    widened = extended(field, (("lon", 1),), 1, True)
    filled = extended(widened, (("lat", 0),), 1, False)
    return filled.reshape(-1, field.shape[3])


def per_device(
    grid_inputs,
    mesh_state,
    embed_in,
    embed_out,
    edge_square,
    edge_geom_weight,
    node_first,
    node_second,
    head,
    g2m_senders,
    g2m_receivers,
    g2m_counts,
    g2m_geom,
    mesh_senders,
    mesh_geom,
    coarse_senders,
    coarse_receivers,
    coarse_geom,
    m2g_senders,
    m2g_geom,
):
    latent_width = mesh_state.shape[3]
    grid_nodes = grid_inputs.shape[2]
    mesh_nodes = mesh_state.shape[2]
    slot_total = g2m_senders.shape[2]
    hidden_in = jax.nn.silu(product(grid_inputs[0, 0], embed_in)).astype(jnp.bfloat16)
    grid_latent = product(hidden_in, embed_out).astype(jnp.bfloat16)
    grid_send = product(grid_latent, edge_square[0, 0]).astype(jnp.bfloat16)
    grid_recv = product(grid_latent, edge_square[2, 1]).astype(jnp.bfloat16)
    nearby = neighbourhood(grid_send[None, None])
    mesh_node = mesh_state[0, 0]
    receivers = g2m_receivers[0, 0]
    mesh_recv = product(mesh_node, edge_square[0, 1]).astype(jnp.bfloat16)
    message = messages(
        jnp.take(nearby, g2m_senders[0, 0], axis=0),
        jnp.take(mesh_recv, receivers, axis=0),
        g2m_geom[0, 0],
        edge_geom_weight[0],
        edge_square[0, 2],
    )
    active = jnp.arange(slot_total, dtype=jnp.int32) < g2m_counts[0, 0]
    selector = (
        (receivers[None, :] == jnp.arange(mesh_nodes, dtype=jnp.int32)[:, None]) & active[None, :]
    ).astype(jnp.bfloat16)
    summed = product(selector, message)
    mesh_one = node_update(mesh_node, summed, node_first[0], node_second[0])
    proc_send = product(mesh_one, edge_square[1, 0]).astype(jnp.bfloat16)
    proc_recv = product(mesh_one, edge_square[1, 1]).astype(jnp.bfloat16)
    coarse_send, coarse_recv = (
        lax.all_gather(proc_send[:COARSE_DEV], ("lat", "lon"), axis=0, tiled=True),
        lax.all_gather(proc_recv[:COARSE_DEV], ("lat", "lon"), axis=0, tiled=True),
    )
    coarse_target = coarse_receivers[0, 0]
    coarse_message = messages(
        jnp.take(coarse_send, coarse_senders[0, 0], axis=0),
        jnp.take(coarse_recv, coarse_target, axis=0),
        coarse_geom[0, 0],
        edge_geom_weight[1],
        edge_square[1, 2],
    )
    targets = jnp.arange(COARSE_DEV * lax.axis_size(("lat", "lon")), dtype=jnp.int32)
    picker = (coarse_target[None, :] == targets[:, None]).astype(jnp.bfloat16)
    coarse_sum = lax.psum_scatter(
        product(picker, coarse_message), ("lat", "lon"), scatter_dimension=0, tiled=True
    )
    nearby = neighbourhood(proc_send[None, None])
    message = messages(
        jnp.take(nearby, mesh_senders[0, 0], axis=0),
        jnp.repeat(proc_recv, MESH_DEGREE, axis=0),
        mesh_geom[0, 0],
        edge_geom_weight[1],
        edge_square[1, 2],
    )
    summed = message.astype(jnp.float32).reshape(mesh_nodes, MESH_DEGREE, latent_width).sum(axis=1)
    summed = summed + jnp.pad(coarse_sum, ((0, mesh_nodes - COARSE_DEV), (0, 0)))
    mesh_two = node_update(mesh_one, summed, node_first[1], node_second[1])
    dec_send = product(mesh_two, edge_square[2, 0]).astype(jnp.bfloat16)
    nearby = neighbourhood(dec_send[None, None])
    message = messages(
        jnp.take(nearby, m2g_senders[0, 0], axis=0),
        jnp.repeat(grid_recv, GRID_DEGREE, axis=0),
        m2g_geom[0, 0],
        edge_geom_weight[2],
        edge_square[2, 2],
    )
    summed = message.astype(jnp.float32).reshape(grid_nodes, GRID_DEGREE, latent_width).sum(axis=1)
    inner = product(grid_latent, node_first[2][:latent_width]) + product(
        summed.astype(jnp.bfloat16), node_first[2][latent_width:]
    )
    hidden = jax.nn.silu(inner).astype(jnp.bfloat16)
    return product(hidden, head).astype(jnp.bfloat16)[None, None]


def solution(mesh):
    return jax.shard_map(
        per_device,
        mesh=mesh,
        in_specs=(
            P("lat", "lon", None, None),
            P("lat", "lon", None, None),
            P(),
            P(),
            P(),
            P(),
            P(),
            P(),
            P(),
            P("lat", "lon", None),
            P("lat", "lon", None),
            P("lat", "lon"),
            P("lat", "lon", None, None),
            P("lat", "lon", None),
            P("lat", "lon", None, None),
            P("lat", "lon", None),
            P("lat", "lon", None),
            P("lat", "lon", None, None),
            P("lat", "lon", None),
            P("lat", "lon", None, None),
        ),
        out_specs=P("lat", "lon", None, None),
        check_vma=False,
    )
```

profile of v0, /device:TPU:4, one launch (start us, length us, event | category | flops | bytes accessed | tf_op | source)
XLA Modules:
  0.0 1345.4 jit_solution(18118269073526020485)
XLA Ops:
  12.2 3.8 collective-permute-start.1
  16.1 21.8 %collective-permute-done = bf16[1,1,1024,512]{3,2,1,0:T(8,128)(2,1)S(1)} collective-permute-done((bf16[1,1,1024,512]{3,2,1,0:T(8,128)(2,1)S(1)}, bf16[1,1,1024,512]{3,2,1,0:T(8,128)(2,1)S(1)}, u32[]{:S(2)}, u32[]{:S(2)}) %collective-permute-start) | collective-permute-done | bytes 1048608 | tf_op jit(solution)/shard_map/ppermute | solution.py:18
  40.2 3.5 collective-permute-start.2
  43.7 5.5 collective-permute-start.3
  51.2 9.2 gather_fusion.1
  61.9 5.1 fusion.89
  67.0 47.2 %collective-permute-done.2 = bf16[1,3,1024,512]{3,2,1,0:T(8,128)(2,1)} collective-permute-done((bf16[1,3,1024,512]{3,2,1,0:T(8,128)(2,1)}, bf16[1,3,1024,512]{3,2,1,0:T(8,128)(2,1)}, u32[]{:S(2)}, u32[]{:S(2)}) %collective-permute-start.2) | collective-permute-done | bytes 3145760 | tf_op jit(solution)/shard_map/ppermute | solution.py:18
  114.2 68.8 %collective-permute-done.3 = bf16[1,3,1024,512]{3,2,1,0:T(8,128)(2,1)} collective-permute-done((bf16[1,3,1024,512]{3,2,1,0:T(8,128)(2,1)}, bf16[1,3,1024,512]{3,2,1,0:T(8,128)(2,1)}, u32[]{:S(2)}, u32[]{:S(2)}) %collective-permute-start.3) | collective-permute-done | bytes 3145760 | tf_op jit(solution)/shard_map/ppermute | solution.py:21
  183.0 7.8 pad_maximum_fusion
  190.8 14.1 %gather_fusion = bf16[2048,512]{1,0:T(8,128)(2,1)} fusion(bf16[9216,512]{1,0:T(8,128)(2,1)} %bitcast.141, s32[2048]{0:T(1024)S(1)} %broadcast_clamp_fusion.2), kind=kCustom, calls=%fused_computation.2 | custom fusion | bytes 4202496 | tf_op jit(solution)/shard_map/jit(_take)/gather | solution.py:87
  204.9 5.4 fusion.12
  216.2 193.1 %all-gather.5.cloned.1.call-done = bf16[2048,512]{1,0:T(8,128)(2,1)} async-done(((bf16[16,512]{1,0:T(8,128)(2,1)}), bf16[2048,512]{1,0:T(8,128)(2,1)}) %all-gather.5.cloned.1.call-update) | async-done | bytes 2097168 | tf_op jit(solution)/shard_map/all_gather | solution.py:103
  412.3 191.5 %all-gather.3.cloned.1.call-done = bf16[2048,512]{1,0:T(8,128)(2,1)} async-done(((bf16[16,512]{1,0:T(8,128)(2,1)}), bf16[2048,512]{1,0:T(8,128)(2,1)}) %all-gather.3.cloned.1.call-update) | async-done | bytes 2097168 | tf_op jit(solution)/shard_map/all_gather | solution.py:102
  607.7 4.1 fusion
  615.0 3.1 fusion.2
  618.1 3.1 fusion.50
  621.4 3.8 collective-permute-start.5
  625.2 4.0 collective-permute-done.4
  630.0 3.6 collective-permute-start.6
  633.6 3.7 collective-permute-start.7
  643.8 9.3 collective-permute-done.7
  662.8 542.7 %reduce-scatter.2.cloned.1.call-done = f32[16,512]{1,0:T(8,128)} async-done(((f32[2048,512]{1,0:T(8,128)}), f32[16,512]{1,0:T(8,128)}) %reduce-scatter.2.cloned.1.call-update) | async-done | bytes 32784 | tf_op jit(solution)/shard_map/reduce_scatter | solution.py:115
  1208.6 3.8 collective-permute-start.9
  1219.0 54.4 %collective-permute-start.11 = (bf16[1,3,128,512]{3,2,1,0:T(8,128)(2,1)}, bf16[1,3,128,512]{3,2,1,0:T(8,128)(2,1)S(1)}, u32[]{:S(2)}, u32[]{:S(2)}) collective-permute-start(bf16[1,3,128,512]{3,2,1,0:T(8,128)(2,1)} %pad_maximum_fusion.5), channel_id=1, source_target_pairs={{16,0},{32,16},{48,32},{64,48},{80,64},{96,80},{112,96},{17,1},{33... | collective-permute-start | bytes 1179656 | tf_op jit(solution)/shard_map/ppermute | solution.py:21
  1273.5 4.7 broadcast_in_dim.79
  1278.2 10.8 convert_element_type.150
  1288.9 7.0 fusion.87
  1296.1 13.2 gather_fusion.3
  1309.3 8.6 convolution_convert_fusion
  1317.9 9.1 reshape.183
  1327.0 8.4 reduce
  1335.4 3.5 fusion.9
  (116 shorter events, 53.4 us)
Async XLA Ops:
  6.5 402.7 %all-gather.5.cloned.1.call-start = ((), (), s32[]{:S(2)}) async-start(), calls=%async_computation.2 | async-start | bytes 2113536 | tf_op jit(solution)/shard_map/all_gather | solution.py:103
  12.1 37.8 %copy-start.18 = (s32[1,1,2048]{2,1,0:T(1,128)S(1)}, s32[1,1,2048]{2,1,0:T(1,128)}, u32[]{:S(2)}) copy-start(s32[1,1,2048]{2,1,0:T(1,128)} %param.32) | copy-start | bytes 24580
  12.1 37.8 %copy-start.11 = (bf16[1,1,128,512]{3,2,1,0:T(8,128)(2,1)S(1)}, bf16[1,1,128,512]{3,2,1,0:T(8,128)(2,1)}, u32[]{:S(2)}) copy-start(bf16[1,1,128,512]{3,2,1,0:T(8,128)(2,1)} %param.23) | copy-start | bytes 393220
  12.1 25.7 %collective-permute-start = (bf16[1,1,1024,512]{3,2,1,0:T(8,128)(2,1)S(1)}, bf16[1,1,1024,512]{3,2,1,0:T(8,128)(2,1)S(1)}, u32[]{:S(2)}, u32[]{:S(2)}) collective-permute-start(bf16[1,1,1024,512]{3,2,1,0:T(8,128)(2,1)S(1)} %fusion.4), channel_id=1, source_target_pairs={{0,1},{1,2},{2,3},{3,4},{4,5},{5,6},{6,7},{7,8},{8,9},{9,10},{10,1... | collective-permute-start | bytes 3145736 | tf_op jit(solution)/shard_map/ppermute | solution.py:18
  12.2 25.7 %collective-permute-start.1 = (bf16[1,1,1024,512]{3,2,1,0:T(8,128)(2,1)S(1)}, bf16[1,1,1024,512]{3,2,1,0:T(8,128)(2,1)S(1)}, u32[]{:S(2)}, u32[]{:S(2)}) collective-permute-start(bf16[1,1,1024,512]{3,2,1,0:T(8,128)(2,1)S(1)} %fusion.4), channel_id=1, source_target_pairs={{1,0},{2,1},{3,2},{4,3},{5,4},{6,5},{7,6},{8,7},{9,8},{10,9},{11,1... | collective-permute-start | bytes 3145736 | tf_op jit(solution)/shard_map/ppermute | solution.py:21
  40.2 74.0 %collective-permute-start.2 = (bf16[1,3,1024,512]{3,2,1,0:T(8,128)(2,1)}, bf16[1,3,1024,512]{3,2,1,0:T(8,128)(2,1)}, u32[]{:S(2)}, u32[]{:S(2)}) collective-permute-start(bf16[1,3,1024,512]{3,2,1,0:T(8,128)(2,1)} %pad_maximum_fusion.1), channel_id=1, source_target_pairs={{0,16},{16,32},{32,48},{48,64},{64,80},{80,96},{96,112},{1,17},{17... | collective-permute-start | bytes 9437192 | tf_op jit(solution)/shard_map/ppermute | solution.py:18
  43.7 139.3 %collective-permute-start.3 = (bf16[1,3,1024,512]{3,2,1,0:T(8,128)(2,1)}, bf16[1,3,1024,512]{3,2,1,0:T(8,128)(2,1)}, u32[]{:S(2)}, u32[]{:S(2)}) collective-permute-start(bf16[1,3,1024,512]{3,2,1,0:T(8,128)(2,1)} %pad_maximum_fusion.1), channel_id=1, source_target_pairs={{16,0},{32,16},{48,32},{64,48},{80,64},{96,80},{112,96},{17,1},{33... | collective-permute-start | bytes 9437192 | tf_op jit(solution)/shard_map/ppermute | solution.py:21
  51.2 9.2 copy-start.17
  51.2 10.7 copy-start.16
  51.2 10.7 copy-start.19
  60.4 122.6 %copy-start.4 = (bf16[1,1,1024,512]{3,2,1,0:T(8,128)(2,1)S(1)}, bf16[1,1,1024,512]{3,2,1,0:T(8,128)(2,1)}, u32[]{:S(2)}) copy-start(bf16[1,1,1024,512]{3,2,1,0:T(8,128)(2,1)} %copy-done.3) | copy-start | bytes 3145732
  60.4 122.6 %copy-start.6 = (bf16[1,1,1024,512]{3,2,1,0:T(8,128)(2,1)S(1)}, bf16[1,1,1024,512]{3,2,1,0:T(8,128)(2,1)}, u32[]{:S(2)}) copy-start(bf16[1,1,1024,512]{3,2,1,0:T(8,128)(2,1)} %copy-done.5) | copy-start | bytes 3145732
  211.9 200.4 %copy-start.12 = (bf16[128,512]{1,0:T(8,128)(2,1)}, bf16[128,512]{1,0:T(8,128)(2,1)S(1)}, u32[]{:S(2)}) copy-start(bf16[128,512]{1,0:T(8,128)(2,1)S(1)} %fusion.10) | copy-start | bytes 393220
  211.9 395.0 %copy-start.26 = (f32[1,1,4,256]{3,2,1,0:T(4,128)S(1)}, f32[1,1,4,256]{3,2,1,0:T(4,128)}, u32[]{:S(2)}) copy-start(f32[1,1,4,256]{3,2,1,0:T(4,128)} %param.39) | copy-start | bytes 12292
  213.9 389.9 %all-gather.3.cloned.1.call-start = ((), (), s32[]{:S(2)}) async-start(), calls=%async_computation.1 | async-start | bytes 2113536 | tf_op jit(solution)/shard_map/all_gather | solution.py:102
  215.9 989.7 %reduce-scatter.2.cloned.1.call-start = ((), (), s32[]{:S(2)}) async-start(), calls=%async_computation.3 | async-start | bytes 4227072 | tf_op jit(solution)/shard_map/reduce_scatter | solution.py:115
  615.0 6.2 copy-start.15
  618.1 19.3 %copy-start.10 = (bf16[128,512]{1,0:T(8,128)(2,1)S(1)}, bf16[128,512]{1,0:T(8,128)(2,1)}, u32[]{:S(2)}) copy-start(bf16[128,512]{1,0:T(8,128)(2,1)} %copy-done.9) | copy-start | bytes 393220
  621.3 7.9 collective-permute-start.4
  621.4 7.9 collective-permute-start.5
  630.0 13.8 %collective-permute-start.6 = (bf16[1,3,128,512]{3,2,1,0:T(8,128)(2,1)}, bf16[1,3,128,512]{3,2,1,0:T(8,128)(2,1)S(1)}, u32[]{:S(2)}, u32[]{:S(2)}) collective-permute-start(bf16[1,3,128,512]{3,2,1,0:T(8,128)(2,1)} %pad_maximum_fusion.4), channel_id=1, source_target_pairs={{0,16},{16,32},{32,48},{48,64},{64,80},{80,96},{96,112},{1,17},{17... | collective-permute-start | bytes 1179656 | tf_op jit(solution)/shard_map/ppermute | solution.py:18
  633.6 19.5 %collective-permute-start.7 = (bf16[1,3,128,512]{3,2,1,0:T(8,128)(2,1)}, bf16[1,3,128,512]{3,2,1,0:T(8,128)(2,1)S(1)}, u32[]{:S(2)}, u32[]{:S(2)}) collective-permute-start(bf16[1,3,128,512]{3,2,1,0:T(8,128)(2,1)} %pad_maximum_fusion.4), channel_id=1, source_target_pairs={{16,0},{32,16},{48,32},{64,48},{80,64},{96,80},{112,96},{17,1},{33... | collective-permute-start | bytes 1179656 | tf_op jit(solution)/shard_map/ppermute | solution.py:21
  658.8 546.7 %copy-start.8 = (f32[128,512]{1,0:T(8,128)S(1)}, f32[128,512]{1,0:T(8,128)}, u32[]{:S(2)}) copy-start(f32[128,512]{1,0:T(8,128)} %fusion.40) | copy-start | bytes 786436
  658.9 548.1 %copy-start.13 = (bf16[128,512]{1,0:T(8,128)(2,1)S(1)}, bf16[128,512]{1,0:T(8,128)(2,1)}, u32[]{:S(2)}) copy-start(bf16[128,512]{1,0:T(8,128)(2,1)} %copy-done.12) | copy-start | bytes 393220
  660.4 613.0 %copy-start.2 = (f32[1024,512]{1,0:T(8,128)S(1)}, f32[1024,512]{1,0:T(8,128)}, u32[]{:S(2)}) copy-start(f32[1024,512]{1,0:T(8,128)} %fusion.2) | copy-start | bytes 6291460
  1208.5 6.6 collective-permute-start.8
  1208.6 7.7 collective-permute-start.9
  1217.1 78.8 %collective-permute-start.10 = (bf16[1,3,128,512]{3,2,1,0:T(8,128)(2,1)}, bf16[1,3,128,512]{3,2,1,0:T(8,128)(2,1)S(1)}, u32[]{:S(2)}, u32[]{:S(2)}) collective-permute-start(bf16[1,3,128,512]{3,2,1,0:T(8,128)(2,1)} %pad_maximum_fusion.5), channel_id=1, source_target_pairs={{0,16},{16,32},{32,48},{48,64},{64,80},{80,96},{96,112},{1,17},{17... | collective-permute-start | bytes 1179656 | tf_op jit(solution)/shard_map/ppermute | solution.py:18
  1219.0 76.9 %collective-permute-start.11 = (bf16[1,3,128,512]{3,2,1,0:T(8,128)(2,1)}, bf16[1,3,128,512]{3,2,1,0:T(8,128)(2,1)S(1)}, u32[]{:S(2)}, u32[]{:S(2)}) collective-permute-start(bf16[1,3,128,512]{3,2,1,0:T(8,128)(2,1)} %pad_maximum_fusion.5), channel_id=1, source_target_pairs={{16,0},{32,16},{48,32},{64,48},{80,64},{96,80},{112,96},{17,1},{33... | collective-permute-start | bytes 1179656 | tf_op jit(solution)/shard_map/ppermute | solution.py:21
  1278.2 10.8 copy-start.14
  1327.0 8.4 copy-start.7
  1327.0 8.4 copy-start.25
  (10 other events, 28.3 us)
Sparse Core Ops, SparseCore 0:
  214.0 195.1 all-gather.4
  411.0 192.7 all-gather.2
  611.9 593.6 reduce-scatter.1
where the time goes:
time: 1350 us
  waiting for transfers between devices  1090 us (81%)
  starting transfers between devices  84.7 us (6%)
  local copies, waits for them, and re-layouts  76.4 us (6%)
  matrix products  62.2 us (5%)
  other arithmetic  22.8 us (2%)
  between operations  14.3 us (1%)
    reduce_scatter x1, waiting for transfers between devices, per_device(): lax.psum_scatter(product(picker, coarse_message), ('lat', 'lon'), scatter...  543 us
    all_gather x1, waiting for transfers between devices, per_device(): lax.all_gather(proc_recv[:COARSE_DEV], ('lat', 'lon'), axis=0, tiled=True)  193 us
    all_gather x1, waiting for transfers between devices, per_device(): lax.all_gather(proc_send[:COARSE_DEV], ('lat', 'lon'), axis=0, tiled=True)  191 us
    ppermute x6, waiting for transfers between devices, extended(): lax.ppermute(lax.slice_in_dim(block, 0, width, axis=dim), axis, backward)  79.3 us
    ppermute x6, waiting for transfers between devices, extended(): lax.ppermute(lax.slice_in_dim(block, block.shape[dim] - width, None, axis...  78.4 us
    ppermute x6, starting transfers between devices, extended(): lax.ppermute(lax.slice_in_dim(block, 0, width, axis=dim), axis, backward)  75.2 us
    dot_general x17, matrix products, product(): return jnp.dot(left, right, preferred_element_type=jnp.float32)  46.7 us
  transfers between devices with their start and end apart: 15, of which 11 were waited for; matrix products, arithmetic and copies ran while one was open for 5% of the time, Pallas kernels for 0%

commit v1 on v0

v1 whole, which is shorter than its diff:
```python
import functools

import jax
import jax.numpy as jnp
from jax import lax
from jax.experimental import pallas as pl
from jax.experimental.pallas import tpu as pltpu
from jax.sharding import PartitionSpec as P

BF = jnp.bfloat16
F32 = jnp.float32
I32 = jnp.int32
WIDTH = 512
GRID_NODES = 1024
MESH_NODES = 128
MESH_DEGREE = 6
GRID_DEGREE = 3
COARSE_DEV = 16
SLOTS = 2048
CHUNK = 512
CHUNKS = SLOTS // CHUNK
PAYLOAD = MESH_NODES + 16 * CHUNKS
LON = 16
VMEM_BYTES = 40 * 1024 * 1024


def mm(left, right):
    return jnp.dot(left, right, preferred_element_type=F32)


def mm_t(left, right):
    return lax.dot_general(left, right, (((0,), (0,)), ((), ())), preferred_element_type=F32)


def mm_nt(left, right):
    return lax.dot_general(left, right, (((1,), (1,)), ((), ())), preferred_element_type=F32)


def silu(v):
    half = 0.5 * v
    return half + half * jnp.tanh(half)


def one_hot(column, width):
    spots = lax.broadcasted_iota(I32, (column.shape[0], width), 1)
    return jnp.where(spots == column, 1.0, 0.0).astype(BF)


def whole(shape=None, index=None):
    if shape is None:
        return pl.BlockSpec(memory_space=pltpu.VMEM)
    return pl.BlockSpec(shape, lambda i: index)


SMEM = pl.BlockSpec(memory_space=pltpu.SMEM)


def square(block, kind):
    return whole((None, None, WIDTH, WIDTH), (block, kind, 0, 0))


def first_half(block, half):
    return whole((None, WIDTH, WIDTH), (block, half, 0))


def second_of(block):
    return whole((None, WIDTH, WIDTH), (block, 0, 0))


def kernel_call(body, outs, specs, args, scratch=(), flops=0, moved=0, name=None):
    return pl.pallas_call(
        body,
        grid=(1,),
        out_shape=outs,
        in_specs=specs,
        scratch_shapes=list(scratch),
        compiler_params=pltpu.CompilerParams(vmem_limit_bytes=VMEM_BYTES),
        cost_estimate=pl.CostEstimate(flops=flops, bytes_accessed=moved, transcendentals=0),
        name=name,
    )(*args)


def shaped(shape, dtype):
    return jax.ShapeDtypeStruct(shape, dtype)


def fill_list(scr, width, indices, geometry):
    for row, value in enumerate(indices):
        scr[row : row + 1, 0:width] = value.astype(F32)
    high = geometry.astype(BF).astype(F32)
    scr[4:8, 0:width] = high
    scr[8:12, 0:width] = geometry - high
    scr[12:16, 0:width] = high


def pack_body(count, senders, receivers, geometry, state, c_senders, c_receivers, c_geometry, out, c_out, scr):
    out[0:MESH_NODES, :] = state[...]
    for c in range(CHUNKS):
        cols = slice(c * CHUNK, (c + 1) * CHUNK)
        s = senders[:, cols]
        edge = lax.broadcasted_iota(I32, (1, CHUNK), 1) + c * CHUNK
        code = jnp.where(edge < count[0, 0], lax.shift_right_logical(s, 10) + 1, 0)
        local = s & (GRID_NODES - 1)
        fill_list(
            scr, CHUNK, (code, lax.shift_right_logical(local, 8), local & 255, receivers[:, cols]), geometry[:, cols]
        )
        out[MESH_NODES + 16 * c : MESH_NODES + 16 * (c + 1), :] = scr[...].astype(BF)
    s = c_senders[...]
    r = c_receivers[...]
    n = s.shape[1]
    fill_list(
        scr, n, (lax.shift_right_logical(s, 8), s & 255, lax.shift_right_logical(r, 4), r & 15), c_geometry[...]
    )
    c_out[...] = scr[:, 0:n].astype(BF)


def prep_body(m_senders, m_geometry, d_senders, d_geometry, weight, m_out, d_out, w_out, scr, turned):
    for senders, geometry, degree, out in (
        (m_senders, m_geometry, MESH_DEGREE, m_out),
        (d_senders, d_geometry, GRID_DEGREE, d_out),
    ):
        n = senders.shape[1]
        s = senders[...]
        near = lax.shift_right_logical(s, 7)
        band = lax.shift_right_logical(near * 11, 5)
        spot = ((near - 3 * band) * 3 + band) * MESH_NODES + (s & (MESH_NODES - 1))
        zero = jnp.zeros((1, n), F32)
        fill_list(scr, n, (spot, zero, zero, zero), geometry[...])
        turned[0:n, :] = scr[:, 0:n].T
        for t in range(degree):
            out[t] = turned[pl.ds(t, n // degree, stride=degree), :]
    for k in range(3):
        w = weight[k]
        high = w.astype(BF).astype(F32)
        scr[0:4, 0:WIDTH] = jnp.zeros((4, WIDTH), F32)
        scr[4:8, 0:WIDTH] = high
        scr[8:12, 0:WIDTH] = high
        scr[12:16, 0:WIDTH] = w - high
        w_out[k] = scr[:, 0:WIDTH].astype(BF)


def embed_body(x, w_in, w_out, w_send, latent, send):
    for b in range(4):
        rows = slice(256 * b, 256 * (b + 1))
        hidden = silu(mm(x[rows, :], w_in[...])).astype(BF)
        lat = mm(hidden, w_out[...]).astype(BF)
        latent[rows, :] = lat
        send[rows, :] = mm(lat, w_send[...]).astype(BF)


def grid_body(latent, w_recv, w_first, recv, base):
    for b in range(4):
        rows = slice(256 * b, 256 * (b + 1))
        recv[rows, :] = mm(latent[rows, :], w_recv[...]).astype(BF)
        base[rows, :] = mm(latent[rows, :], w_first[...])


def self_body(payload, send, w_recv, w_geom, out, q):
    q[...] = mm(payload[0:MESH_NODES, :], w_recv[...]).astype(BF)
    out[...] = jnp.zeros_like(out)

    @pl.loop(0, CHUNKS)
    def _(c):
        rows = pl.ds(pl.multiple_of(MESH_NODES + 16 * c, 16), 16)
        d = payload[rows, :].astype(F32).T
        for h in range(2):
            part = d[256 * h : 256 * (h + 1), :]
            s = (part[:, 1:2] * 256.0 + part[:, 2:3]).astype(I32)
            r = jnp.where(part[:, 0:1] == 5.0, part[:, 3:4], -1.0).astype(I32)
            pick = one_hot(r, MESH_NODES)
            pre = mm(one_hot(s, GRID_NODES), send[...]) + mm(pick, q[...]) + mm(part.astype(BF), w_geom[...])
            out[...] += mm_t(pick, silu(pre).astype(BF))


def near_body(left, centre, right, send, w_recv, w_geom, o_left, o_centre, o_right, masks, ranks, q):
    lists = []
    for a in range(3):
        lists.append((left, a, (2 - a) * 3 + 2, o_left, a))
        if a != 1:
            lists.append((centre, a, (2 - a) * 3 + 1, o_centre, a // 2))
        lists.append((right, a, (2 - a) * 3, o_right, a))
    for i, (src, a, bucket, _, _) in enumerate(lists):
        for c in range(CHUNKS):
            code = src[a, MESH_NODES + 16 * c : MESH_NODES + 16 * (c + 1), :].astype(F32)[0:1, :]
            row = i * CHUNKS + c
            masks[row : row + 1, :] = jnp.where(code == float(bucket + 1), 1.0, 0.0)
    n = masks.shape[0]
    mask = masks[...]
    before = lax.broadcasted_iota(I32, (CHUNK, CHUNK), 0) < lax.broadcasted_iota(I32, (CHUNK, CHUNK), 1)
    inside = mm(mask.astype(BF), jnp.where(before, 1.0, 0.0).astype(BF))
    mine = lax.broadcasted_iota(I32, (n, n), 0)
    other = lax.broadcasted_iota(I32, (n, n), 1)
    earlier = jnp.where((other < mine) & (mine // CHUNKS == other // CHUNKS), 1.0, 0.0).astype(BF)
    carried = mm(earlier, mask.astype(BF)).sum(axis=1, keepdims=True)
    ranks[...] = jnp.where(mask > 0.5, inside + carried, -1.0).astype(I32)
    for i, (src, a, _, dst, at) in enumerate(lists):
        q[i] = mm(src[a, 0:MESH_NODES, :], w_recv[...]).astype(BF)

    for i, (src, a, bucket, dst, at) in enumerate(lists):

        def hidden_sum(k, src=src, a=a, bucket=bucket, i=i):
            slot = lax.broadcasted_iota(I32, (128, CHUNK), 0) + k * 128
            d = jnp.zeros((128, 16), F32)
            for c in range(CHUNKS):
                row = i * CHUNKS + c
                chosen = jnp.where(slot == ranks[row : row + 1, :], 1.0, 0.0).astype(BF)
                d += mm_nt(chosen, src[a, MESH_NODES + 16 * c : MESH_NODES + 16 * (c + 1), :])
            s = (d[:, 1:2] * 256.0 + d[:, 2:3]).astype(I32)
            r = jnp.where(d[:, 0:1] == float(bucket + 1), d[:, 3:4], -1.0).astype(I32)
            pick = one_hot(r, MESH_NODES)
            pre = mm(one_hot(s, GRID_NODES), send[...]) + mm(pick, q[i]) + mm(d.astype(BF), w_geom[...])
            return mm_t(pick, silu(pre).astype(BF))

        used = jnp.sum(masks[i * CHUNKS : (i + 1) * CHUNKS, :]).astype(I32)
        blocks = lax.shift_right_logical(used + 127, 7)
        total = lax.fori_loop(1, blocks, lambda k, t, f=hidden_sum: t + f(k), hidden_sum(0))
        dst[at] = total.astype(BF)


def side_sum_body(o_centre, from_left, from_right, out):
    for k, a in ((0, 0), (1, 2)):
        total = o_centre[k].astype(F32) + from_left[a].astype(F32) + from_right[a].astype(F32)
        out[k] = total.astype(BF)


def split_mm(value, weight):
    high = value.astype(BF)
    low = (value - high.astype(F32)).astype(BF)
    return mm(high, weight) + mm(low, weight)


def node_rows(v, hidden_total, w_second, first_node, first_sum, second):
    m = split_mm(hidden_total, w_second).astype(BF)
    u = silu(mm(v, first_node) + mm(m, first_sum)).astype(BF)
    return (v.astype(F32) + mm(u, second)).astype(BF)


def node_body(
    own, from_left, from_right, up, down, state, w_second, first_node, first_sum, second, w_send, w_recv,
    mesh_one, send, recv,
):
    total = own[...] + from_left[...].astype(F32) + from_right[...].astype(F32)
    total = total + up[...].astype(F32) + down[...].astype(F32)
    one = node_rows(state[...], total, w_second[...], first_node[...], first_sum[...], second[...])
    mesh_one[...] = one
    send[...] = mm(one, w_send[...]).astype(BF)
    recv[...] = mm(one, w_recv[...]).astype(BF)


def fine_body(edges, left, centre, right, recv, w_geom, out):
    q = recv[...].astype(F32)
    n = 3 * MESH_NODES
    total = jnp.zeros((MESH_NODES, WIDTH), F32)
    for t in range(MESH_DEGREE):
        d = edges[t]
        spread = one_hot(d[:, 0:1].astype(I32), 3 * n)
        pre = q + mm(d.astype(BF), w_geom[...])
        pre += mm(spread[:, 0:n], left[...]) + mm(spread[:, n : 2 * n], centre[...])
        pre += mm(spread[:, 2 * n :], right[...])
        total += silu(pre)
    out[...] = total


def mesh_body(
    place, fine, list_a, list_b, list_c, coarse_a, coarse_b, recv, mesh_one, w_geom, w_second, first_node, first_sum,
    second, w_send, send,
):
    z, y, x, core, tile = (place[0, k] for k in range(5))
    half = coarse_a.shape[0]
    q = recv[0:COARSE_DEV, :]
    total = jnp.zeros((MESH_NODES, WIDTH), F32)
    for edges in (list_a, list_b, list_c):
        d = edges[...].astype(F32).T
        s = (d[:, 0:1] * 256.0 + d[:, 1:2]).astype(I32)
        t = lax.shift_right_logical(s, 4)
        lat = lax.shift_right_logical(t, 4)
        lon = t & 15
        gz = (z - lax.shift_right_logical(lat, 1)) & 3
        gy = (y - lax.shift_right_logical(lon, 2)) & 3
        gx = (x - ((lat & 1) * 2 + (lax.shift_right_logical(lon, 1) & 1))) & 3
        gc = (core + lon) & 1
        spot = (((gc * 4 + gx) * 4 + gy) * 4 + gz) * 16 + (s & 15)
        mine = d[:, 2:3].astype(I32) == tile
        r = jnp.where(mine, d[:, 3:4].astype(I32), -1)
        pick = one_hot(r, MESH_NODES)
        spread = one_hot(spot, 2 * half)
        pre = mm(spread[:, 0:half], coarse_a[...]) + mm(spread[:, half:], coarse_b[...])
        pre += mm(pick[:, 0:COARSE_DEV], q) + mm(d.astype(BF), w_geom[...])
        total += mm_t(pick, silu(pre).astype(BF))
    two = node_rows(
        mesh_one[...], total + fine[...], w_second[...], first_node[...], first_sum[...], second[...]
    )
    send[...] = mm(two, w_send[...]).astype(BF)


def decode_body(edges, left, centre, right, recv, base, w_geom, w_second, first_sum, head, out):
    n = 3 * MESH_NODES

    @pl.loop(0, 4)
    def _(b):
        rows = pl.ds(pl.multiple_of(256 * b, 256), 256)
        q = recv[rows, :].astype(F32)
        total = jnp.zeros((256, WIDTH), F32)
        for t in range(GRID_DEGREE):
            d = edges[t, rows, :]
            spread = one_hot(d[:, 0:1].astype(I32), 3 * n)
            pre = q + mm(d.astype(BF), w_geom[...])
            pre += mm(spread[:, 0:n], left[...]) + mm(spread[:, n : 2 * n], centre[...])
            pre += mm(spread[:, 2 * n :], right[...])
            total += silu(pre)
        summed = mm(total.astype(BF), w_second[...]).astype(BF)
        hidden = silu(base[rows, :] + mm(summed, first_sum[...])).astype(BF)
        out[rows, :] = mm(hidden, head[...]).astype(BF)


def shift(value, axis, step, periodic):
    n = lax.axis_size(axis)
    pairs = [(i, (i + step) % n) for i in range(n) if periodic or 0 <= i + step < n]
    return lax.ppermute(value, axis, pairs)


def columns(value):
    up = shift(value, "lat", 1, False)
    down = shift(value, "lat", -1, False)
    centre = jnp.stack([up, value, down])
    return shift(centre, "lon", 1, True), centre, shift(centre, "lon", -1, True)


def coarse_gather(rows):
    def joined(value, pairs_of, axis):
        return jnp.concatenate([value] + [lax.ppermute(value, axis, pairs_of(s)) for s in (1, 2, 3)], axis=0)

    def along_z(s):
        return [(i, ((i // 2 + s) % 4) * 2 + i % 2) for i in range(8)]

    def along_y(s):
        return [(i, ((i // 4 + s) % 4) * 4 + i % 4) for i in range(16)]

    def along_x(s):
        pairs = []
        for lat in range(8):
            for lon in range(16):
                x = ((lat % 2) * 2 + (lon // 2) % 2 + s) % 4
                to_lat = lat // 2 * 2 + x // 2
                to_lon = lon // 4 * 4 + (x % 2) * 2 + lon % 2
                pairs.append((lat * 16 + lon, to_lat * 16 + to_lon))
        return pairs

    rows = joined(rows, along_z, "lat")
    rows = joined(rows, along_y, "lon")
    rows = joined(rows, along_x, ("lat", "lon"))
    return rows, lax.ppermute(rows, "lon", [(i, i ^ 1) for i in range(16)])


def per_device(
    grid_inputs,
    mesh_state,
    embed_in,
    embed_out,
    edge_square,
    edge_geom_weight,
    node_first,
    node_second,
    head,
    g2m_senders,
    g2m_receivers,
    g2m_counts,
    g2m_geom,
    mesh_senders,
    mesh_geom,
    coarse_senders,
    coarse_receivers,
    coarse_geom,
    m2g_senders,
    m2g_geom,
):
    v = whole()
    mesh_rows = (MESH_NODES, WIDTH)
    grid_rows = (GRID_NODES, WIDTH)
    grid_flops = 2 * GRID_NODES * WIDTH * WIDTH
    mesh_flops = grid_flops // 8
    state = mesh_state[0, 0]
    payload, coarse_list = kernel_call(
        pack_body,
        (shaped((PAYLOAD, WIDTH), BF), shaped((16, coarse_senders.shape[2]), BF)),
        [SMEM] + [v] * 7,
        (
            g2m_counts, g2m_senders[0], g2m_receivers[0], g2m_geom[0, 0], state,
            coarse_senders[0], coarse_receivers[0], coarse_geom[0, 0],
        ),
        [pltpu.VMEM((16, CHUNK), F32)],
        name="pack",
    )
    near_left, near_centre, near_right = columns(payload)
    tiles = lax.axis_size(("lat", "lon"))
    both = ("lat", "lon")
    list_next = lax.ppermute(coarse_list, both, [(t, (t - 1) % tiles) for t in range(tiles)])
    list_far = lax.ppermute(coarse_list, both, [(t, (t + tiles // 2) % tiles) for t in range(tiles)])

    m_edges, d_edges, geom = kernel_call(
        prep_body,
        (
            shaped((MESH_DEGREE, MESH_NODES, 16), F32),
            shaped((GRID_DEGREE, GRID_NODES, 16), F32),
            shaped((3, 16, WIDTH), BF),
        ),
        [v] * 5,
        (mesh_senders[0], mesh_geom[0, 0], m2g_senders[0], m2g_geom[0, 0], edge_geom_weight),
        [pltpu.VMEM((16, 3072), F32), pltpu.VMEM((3072, 16), F32)],
        flops=grid_flops,
        name="prep",
    )
    latent, grid_send = kernel_call(
        embed_body,
        (shaped(grid_rows, BF), shaped(grid_rows, BF)),
        [v, v, v, square(0, 0)],
        (grid_inputs[0, 0], embed_in, embed_out, edge_square),
        flops=3 * grid_flops,
        moved=5 << 20,
        name="embed",
    )

    def geom_of(k):
        return whole((None, 16, WIDTH), (k, 0, 0))

    own_sum = kernel_call(
        self_body,
        shaped(mesh_rows, F32),
        [v, v, square(0, 1), geom_of(0)],
        (payload, grid_send, edge_square, geom),
        [pltpu.VMEM(mesh_rows, BF)],
        flops=5 * grid_flops,
        moved=3 << 20,
        name="own",
    )
    three = (3,) + mesh_rows
    to_left, to_centre, to_right = kernel_call(
        near_body,
        (shaped(three, BF), shaped((2,) + mesh_rows, BF), shaped(three, BF)),
        [v, v, v, v, square(0, 1), geom_of(0)],
        (near_left, near_centre, near_right, grid_send, edge_square, geom),
        [
            pltpu.VMEM((8 * CHUNKS, CHUNK), F32),
            pltpu.VMEM((8 * CHUNKS, CHUNK), I32),
            pltpu.VMEM((8,) + mesh_rows, BF),
        ],
        flops=4 * grid_flops,
        moved=5 << 20,
        name="near",
    )
    from_right = shift(to_left, "lon", -1, True)
    from_left = shift(to_right, "lon", 1, True)
    grid_recv, grid_base = kernel_call(
        grid_body,
        (shaped(grid_rows, BF), shaped(grid_rows, F32)),
        [v, square(2, 1), first_half(2, 0)],
        (latent, edge_square, node_first),
        flops=2 * grid_flops,
        moved=5 << 20,
        name="grid",
    )
    sides = kernel_call(
        side_sum_body, shaped((2,) + mesh_rows, BF), [v] * 3, (to_centre, from_left, from_right), name="sides"
    )
    down = shift(sides[0], "lat", -1, False)
    up = shift(sides[1], "lat", 1, False)
    middle = whole((None,) + mesh_rows, (1, 0, 0))
    mesh_one, proc_send, proc_recv = kernel_call(
        node_body,
        (shaped(mesh_rows, BF),) * 3,
        [
            v, middle, middle, v, v, v, square(0, 2), first_half(0, 0), first_half(0, 1), second_of(0),
            square(1, 0), square(1, 1),
        ],
        (
            own_sum, from_left, from_right, up, down, state, edge_square, node_first, node_first, node_second,
            edge_square, edge_square,
        ),
        flops=7 * mesh_flops,
        moved=4 << 20,
        name="node",
    )
    coarse_a, coarse_b = coarse_gather(proc_send[:COARSE_DEV])
    joined = (3 * MESH_NODES, WIDTH)
    near = [part.reshape(joined) for part in columns(proc_send)]
    fine = kernel_call(
        fine_body,
        shaped(mesh_rows, F32),
        [v, v, v, v, v, geom_of(1)],
        (m_edges, *near, proc_recv, geom),
        flops=2 * grid_flops,
        moved=3 << 20,
        name="fine",
    )
    lat, lon = lax.axis_index("lat"), lax.axis_index("lon")
    place = jnp.stack([lat // 2, lon // 4, (lat % 2) * 2 + (lon // 2) % 2, lon % 2, lat * LON + lon])[None]
    dec_send = kernel_call(
        mesh_body,
        shaped(mesh_rows, BF),
        [
            SMEM, v, v, v, v, v, v, v, v, geom_of(1), square(1, 2), first_half(1, 0), first_half(1, 1),
            second_of(1), square(2, 0),
        ],
        (
            place.astype(I32), fine, coarse_list, list_next, list_far, coarse_a, coarse_b, proc_recv, mesh_one, geom,
            edge_square, node_first, node_first, node_second, edge_square,
        ),
        flops=4 * grid_flops,
        moved=6 << 20,
        name="mesh",
    )
    near = [part.reshape(joined) for part in columns(dec_send)]
    outputs = kernel_call(
        decode_body,
        shaped((GRID_NODES, head.shape[1]), BF),
        [v, v, v, v, v, v, geom_of(2), square(2, 2), first_half(2, 1), v],
        (d_edges, *near, grid_recv, grid_base, geom, edge_square, node_first, head),
        flops=8 * grid_flops,
        moved=8 << 20,
        name="decode",
    )
    return outputs[None, None]


def solution(mesh):
    return jax.shard_map(
        per_device,
        mesh=mesh,
        in_specs=(
            P("lat", "lon", None, None),
            P("lat", "lon", None, None),
            P(),
            P(),
            P(),
            P(),
            P(),
            P(),
            P(),
            P("lat", "lon", None),
            P("lat", "lon", None),
            P("lat", "lon"),
            P("lat", "lon", None, None),
            P("lat", "lon", None),
            P("lat", "lon", None, None),
            P("lat", "lon", None),
            P("lat", "lon", None),
            P("lat", "lon", None, None),
            P("lat", "lon", None),
            P("lat", "lon", None, None),
        ),
        out_specs=P("lat", "lon", None, None),
        check_vma=False,
    )
```

time: 1350 us -> 190 us (0.14)
  waiting for transfers between devices: 1090 us -> 45.7 us
  matrix products: 62.2 us -> 0 us
  local copies, waits for them, and re-layouts: 76.4 us -> 30.1 us
  Pallas kernels: 0 us -> 43.2 us
  other arithmetic: 22.8 us -> 0.16 us
  starting transfers between devices: 84.7 us -> 67.5 us
    reduce_scatter x1 -> x0, waiting for transfers between devices: 543 us -> none  [per_device(): lax.psum_scatter(product(picker, coarse_message), ('lat', 'lon'), scatter...]
    all_gather x2 -> x0, waiting for transfers between devices: 385 us -> none  [the longest x1 193 us: per_device(): lax.all_gather(proc_recv[:COARSE_DEV], ('lat', 'lon'), axis=0, tiled=True)]
    ppermute x12 -> x28, waiting for transfers between devices: 158 us -> 45.7 us  [the longest x16 38 us: shift(): return lax.ppermute(value, axis, pairs)]
    dot_general x21 -> x0, matrix products: 62.2 us -> none  [the longest x17 46.7 us: product(): return jnp.dot(left, right, preferred_element_type=jnp.float32)]
    gather x6 -> x0, local copies, waits for them, and re-layouts: 45.4 us -> none  [the longest x1 14.1 us: per_device(): jnp.take(nearby, g2m_senders[0, 0], axis=0)]
    pallas_call x0 -> x11, Pallas kernels: none -> 43.2 us  [kernel_call(): pl.pallas_call(body, grid=(1,), out_shape=outs, in_specs=specs, scratch_s...]
    unnamed x54 -> x94, local copies, waits for them, and re-layouts: 2.04 us -> 27.2 us
    ppermute x12 -> x28, starting transfers between devices: 84.4 us -> 67.5 us  [the longest x16 45.5 us: shift(): return lax.ppermute(value, axis, pairs)]
  transfers between devices with their start and end apart: 15 -> 28, of which waited for: 11 -> 14; matrix products, arithmetic and copies ran while one was open for 5% -> 4% of each run, Pallas kernels for 0% -> 8%
where the time goes in v1:
time: 190 us; the launch traced here: 188 us
  starting transfers between devices  67.5 us (36%)
  waiting for transfers between devices  45.7 us (24%)
  Pallas kernels  43.2 us (23%)
  local copies, waits for them, and re-layouts  30.1 us (16%)
    ppermute x16, starting transfers between devices, shift(): return lax.ppermute(value, axis, pairs)  45.5 us
    pallas_call x11, Pallas kernels, kernel_call(): pl.pallas_call(body, grid=(1,), out_shape=outs, in_specs=specs, scratch_s...  43.2 us
    ppermute x16, waiting for transfers between devices, shift(): return lax.ppermute(value, axis, pairs)  38 us
    unnamed x94, local copies, waits for them, and re-layouts  27.2 us
    ppermute x9, starting transfers between devices, joined(): lax.ppermute(value, axis, pairs_of(s))  18.8 us
    ppermute x9, waiting for transfers between devices, joined(): lax.ppermute(value, axis, pairs_of(s))  7.77 us
  transfers between devices with their start and end apart: 28, of which 14 were waited for; matrix products, arithmetic and copies ran while one was open for 4% of the time, Pallas kernels for 8%

profile of v1, /device:TPU:4, one launch (start us, length us, event | category | flops | bytes accessed | tf_op | source)
XLA Modules:
  0.0 187.9 jit_solution(962484744338974009)
XLA Ops:
  5.9 3.9 %collective-permute-start = (bf16[192,512]{1,0:T(8,128)(2,1)S(1)}, bf16[192,512]{1,0:T(8,128)(2,1)S(1)}, u32[]{:S(2)}, u32[]{:S(2)}) collective-permute-start(bf16[192,512]{1,0:T(8,128)(2,1)S(1)} %get-tuple-element.22.payload), channel_id=1, source_target_pairs={{0,16},{16,32},{32,48},{48,64},{64,80},{80,96},{96,112},{1,17},{17... | collective-permute-start | bytes 589832 | tf_op jit(solution)/shard_map/ppermute | solution.py:319
  9.8 3.6 %collective-permute-start.1 = (bf16[192,512]{1,0:T(8,128)(2,1)S(1)}, bf16[192,512]{1,0:T(8,128)(2,1)S(1)}, u32[]{:S(2)}, u32[]{:S(2)}) collective-permute-start(bf16[192,512]{1,0:T(8,128)(2,1)S(1)} %get-tuple-element.22.payload), channel_id=1, source_target_pairs={{16,0},{32,16},{48,32},{64,48},{80,64},{96,80},{112,96},{17,1},{33... | collective-permute-start | bytes 589832 | tf_op jit(solution)/shard_map/ppermute | solution.py:319
  13.4 2.7 %collective-permute-done = bf16[192,512]{1,0:T(8,128)(2,1)S(1)} collective-permute-done((bf16[192,512]{1,0:T(8,128)(2,1)S(1)}, bf16[192,512]{1,0:T(8,128)(2,1)S(1)}, u32[]{:S(2)}, u32[]{:S(2)}) %collective-permute-start) | collective-permute-done | bytes 196640 | tf_op jit(solution)/shard_map/ppermute | solution.py:319
  16.0 5.6 %collective-permute-done.1 = bf16[192,512]{1,0:T(8,128)(2,1)S(1)} collective-permute-done((bf16[192,512]{1,0:T(8,128)(2,1)S(1)}, bf16[192,512]{1,0:T(8,128)(2,1)S(1)}, u32[]{:S(2)}, u32[]{:S(2)}) %collective-permute-start.1) | collective-permute-done | bytes 196640 | tf_op jit(solution)/shard_map/ppermute | solution.py:319
  21.8 3.8 %collective-permute-start.3 = (bf16[3,192,512]{2,1,0:T(8,128)(2,1)S(1)}, bf16[3,192,512]{2,1,0:T(8,128)(2,1)}, u32[]{:S(2)}, u32[]{:S(2)}) collective-permute-start(bf16[3,192,512]{2,1,0:T(8,128)(2,1)S(1)} %pad_maximum_fusion.centre), channel_id=1, source_target_pairs={{0,15},{1,0},{2,1},{3,2},{4,3},{5,4},{6,5},{7,6},{8,7},{9,8},{10,9... | collective-permute-start | bytes 1769480 | tf_op jit(solution)/shard_map/ppermute | solution.py:319
  29.1 2.5 %copy-done = bf16[3,3,512,512]{3,2,1,0:T(8,128)(2,1)S(1)} copy-done((bf16[3,3,512,512]{3,2,1,0:T(8,128)(2,1)S(1)}, bf16[3,3,512,512]{3,2,1,0:T(8,128)(2,1)}, u32[]{:S(2)}) %copy-start) | copy-done | bytes 4718616
  31.6 2.5 %embed.1 = (bf16[1024,512]{1,0:T(8,128)(2,1)S(1)}, bf16[1024,512]{1,0:T(8,128)(2,1)S(1)}) custom-call(bf16[1024,474]{1,0:T(8,128)(2,1)S(1)} %bitcast.40, bf16[474,512]{1,0:T(8,128)(2,1)S(1)} %copy-done.13, bf16[512,512]{1,0:T(8,128)(2,1)S(1)} %copy-done.12, bf16[3,3,512,512]{3,2,1,0:T(8,128)(2,1)S(1)} %copy-done), custom_call_target="tpu_custom_call" | custom-call | flops 1610612736 | bytes 5242880 | tf_op jit(solution)/shard_map/embed/pallas_call | solution.py:71
  35.1 2.6 %collective-permute-done.2.left = bf16[3,192,512]{2,1,0:T(8,128)(2,1)} collective-permute-done((bf16[3,192,512]{2,1,0:T(8,128)(2,1)S(1)}, bf16[3,192,512]{2,1,0:T(8,128)(2,1)}, u32[]{:S(2)}, u32[]{:S(2)}) %collective-permute-start.2) | collective-permute-done | bytes 589856 | tf_op jit(solution)/shard_map/ppermute | solution.py:319
  37.7 11.9 %near.1 = (bf16[3,128,512]{2,1,0:T(8,128)(2,1)S(1)}, bf16[2,128,512]{2,1,0:T(8,128)(2,1)S(1)}, bf16[3,128,512]{2,1,0:T(8,128)(2,1)S(1)}) custom-call(bf16[3,192,512]{2,1,0:T(8,128)(2,1)} %collective-permute-done.2.left, bf16[3,192,512]{2,1,0:T(8,128)(2,1)S(1)} %pad_maximum_fusion.centre, bf16[3,192,512]{2,1,0:T(8,128)(2,1)} %collective-permute-done.3.right, ...), custom_call_target="tpu_custom_call" | custom-call | flops 2147483648 | bytes 5242880 | tf_op jit(solution)/shard_map/near/pallas_call | solution.py:71
  53.5 8.2 %collective-permute-done.4.from_left = bf16[3,128,512]{2,1,0:T(8,128)(2,1)S(1)} collective-permute-done((bf16[3,128,512]{2,1,0:T(8,128)(2,1)S(1)}, bf16[3,128,512]{2,1,0:T(8,128)(2,1)S(1)}, u32[]{:S(2)}, u32[]{:S(2)}) %collective-permute-start.4) | collective-permute-done | bytes 393248 | tf_op jit(solution)/shard_map/ppermute | solution.py:319
  61.8 4.6 %collective-permute-start.6 = (bf16[128,512]{1,0:T(8,128)(2,1)S(1)}, bf16[128,512]{1,0:T(8,128)(2,1)S(1)}, u32[]{:S(2)}, u32[]{:S(2)}) collective-permute-start(bf16[128,512]{1,0:T(8,128)(2,1)S(1)} %get-tuple-element.36), channel_id=1, source_target_pairs={{0,16},{16,32},{32,48},{48,64},{64,80},{80,96},{96,112},{1,17},{17... | collective-permute-start | bytes 393224 | tf_op jit(solution)/shard_map/ppermute | solution.py:319
  66.5 3.0 %collective-permute-start.7 = (bf16[128,512]{1,0:T(8,128)(2,1)S(1)}, bf16[128,512]{1,0:T(8,128)(2,1)S(1)}, u32[]{:S(2)}, u32[]{:S(2)}) collective-permute-start(bf16[128,512]{1,0:T(8,128)(2,1)S(1)} %get-tuple-element.35), channel_id=1, source_target_pairs={{16,0},{32,16},{48,32},{64,48},{80,64},{96,80},{112,96},{17,1},{33... | collective-permute-start | bytes 393224 | tf_op jit(solution)/shard_map/ppermute | solution.py:319
  69.5 7.1 %own.1 = f32[128,512]{1,0:T(8,128)S(1)} custom-call(bf16[192,512]{1,0:T(8,128)(2,1)S(1)} %get-tuple-element.22.payload, bf16[1024,512]{1,0:T(8,128)(2,1)S(1)} %get-tuple-element.23.send, bf16[3,3,512,512]{3,2,1,0:T(8,128)(2,1)S(1)} %copy-done.1, bf16[3,16,512]{2,1,0:T(8,128)(2,1)S(1)} %get-tuple-element.24.w_geom), custom_call_target="tpu_custom_call" | custom-call | flops 2684354560 | bytes 3145728 | tf_op jit(solution)/shard_map/own/pallas_call | solution.py:71
  78.4 3.2 %collective-permute-start.14 = (bf16[16,512]{1,0:T(8,128)(2,1)S(1)}, bf16[16,512]{1,0:T(8,128)(2,1)S(1)}, u32[]{:S(2)}, u32[]{:S(2)}) collective-permute-start(bf16[16,512]{1,0:T(8,128)(2,1)S(1)} %get-tuple-element.39), channel_id=1, source_target_pairs={{0,32},{16,48},{32,64},{48,80},{64,96},{80,112},{96,0},{112,16},{1... | collective-permute-start | bytes 49160 | tf_op jit(solution)/shard_map/ppermute | solution.py:331
  83.5 2.4 %collective-permute-start.16 = (bf16[16,512]{1,0:T(8,128)(2,1)S(1)}, bf16[16,512]{1,0:T(8,128)(2,1)S(1)}, u32[]{:S(2)}, u32[]{:S(2)}) collective-permute-start(bf16[16,512]{1,0:T(8,128)(2,1)S(1)} %get-tuple-element.39), channel_id=1, source_target_pairs={{0,96},{16,112},{32,0},{48,16},{64,32},{80,48},{96,64},{112,80},{1... | collective-permute-start | bytes 49160 | tf_op jit(solution)/shard_map/ppermute | solution.py:331
  87.8 2.9 %collective-permute-start.18 = (bf16[64,512]{1,0:T(8,128)(2,1)S(1)}, bf16[64,512]{1,0:T(8,128)(2,1)S(1)}, u32[]{:S(2)}, u32[]{:S(2)}) collective-permute-start(bf16[64,512]{1,0:T(8,128)(2,1)S(1)} %pad_maximum_fusion.3), channel_id=1, source_target_pairs={{0,8},{1,9},{2,10},{3,11},{4,12},{5,13},{6,14},{7,15},{8,0},{9,1},... | collective-permute-start | bytes 196616 | tf_op jit(solution)/shard_map/ppermute | solution.py:331
  95.7 4.0 %collective-permute-start.21 = (bf16[256,512]{1,0:T(8,128)(2,1)S(1)}, bf16[256,512]{1,0:T(8,128)(2,1)S(1)}, u32[]{:S(2)}, u32[]{:S(2)}) collective-permute-start(bf16[256,512]{1,0:T(8,128)(2,1)S(1)} %get-tuple-element.40), channel_id=1, source_target_pairs={{0,16},{1,17},{2,18},{3,19},{4,20},{5,21},{6,22},{7,23},{8,24},{9,... | collective-permute-start | bytes 786440 | tf_op jit(solution)/shard_map/ppermute | solution.py:331
  99.7 2.6 %collective-permute-start.22 = (bf16[256,512]{1,0:T(8,128)(2,1)S(1)}, bf16[256,512]{1,0:T(8,128)(2,1)S(1)}, u32[]{:S(2)}, u32[]{:S(2)}) collective-permute-start(bf16[256,512]{1,0:T(8,128)(2,1)S(1)} %get-tuple-element.40), channel_id=1, source_target_pairs={{0,18},{1,19},{2,0},{3,1},{4,22},{5,23},{6,4},{7,5},{8,26},{9,27},... | collective-permute-start | bytes 786440 | tf_op jit(solution)/shard_map/ppermute | solution.py:331
  105.2 4.1 %collective-permute-done.21 = bf16[256,512]{1,0:T(8,128)(2,1)S(1)} collective-permute-done((bf16[256,512]{1,0:T(8,128)(2,1)S(1)}, bf16[256,512]{1,0:T(8,128)(2,1)S(1)}, u32[]{:S(2)}, u32[]{:S(2)}) %collective-permute-start.21) | collective-permute-done | bytes 262176 | tf_op jit(solution)/shard_map/ppermute | solution.py:331
  110.8 4.6 %collective-permute-start.8 = (bf16[128,512]{1,0:T(8,128)(2,1)S(1)}, bf16[128,512]{1,0:T(8,128)(2,1)S(1)}, u32[]{:S(2)}, u32[]{:S(2)}) collective-permute-start(bf16[128,512]{1,0:T(8,128)(2,1)S(1)} %get-tuple-element.28), channel_id=1, source_target_pairs={{0,16},{16,32},{32,48},{48,64},{64,80},{80,96},{96,112},{1,17},{17... | collective-permute-start | bytes 393224 | tf_op jit(solution)/shard_map/ppermute | solution.py:319
  115.4 2.7 %collective-permute-start.9 = (bf16[128,512]{1,0:T(8,128)(2,1)S(1)}, bf16[128,512]{1,0:T(8,128)(2,1)S(1)}, u32[]{:S(2)}, u32[]{:S(2)}) collective-permute-start(bf16[128,512]{1,0:T(8,128)(2,1)S(1)} %get-tuple-element.28), channel_id=1, source_target_pairs={{16,0},{32,16},{48,32},{64,48},{80,64},{96,80},{112,96},{17,1},{33... | collective-permute-start | bytes 393224 | tf_op jit(solution)/shard_map/ppermute | solution.py:319
  120.1 5.3 %collective-permute-done.9 = bf16[128,512]{1,0:T(8,128)(2,1)S(1)} collective-permute-done((bf16[128,512]{1,0:T(8,128)(2,1)S(1)}, bf16[128,512]{1,0:T(8,128)(2,1)S(1)}, u32[]{:S(2)}, u32[]{:S(2)}) %collective-permute-start.9) | collective-permute-done | bytes 131104 | tf_op jit(solution)/shard_map/ppermute | solution.py:319
  125.5 3.8 %collective-permute-start.11 = (bf16[3,128,512]{2,1,0:T(8,128)(2,1)S(1)}, bf16[3,128,512]{2,1,0:T(8,128)(2,1)}, u32[]{:S(2)}, u32[]{:S(2)}) collective-permute-start(bf16[3,128,512]{2,1,0:T(8,128)(2,1)S(1)} %pad_maximum_fusion.1), channel_id=1, source_target_pairs={{0,15},{1,0},{2,1},{3,2},{4,3},{5,4},{6,5},{7,6},{8,7},{9,8},{10,9... | collective-permute-start | bytes 1179656 | tf_op jit(solution)/shard_map/ppermute | solution.py:319
  129.3 3.2 %collective-permute-start.13 = (bf16[16,256]{1,0:T(8,128)(2,1)S(1)}, bf16[16,256]{1,0:T(8,128)(2,1)}, u32[]{:S(2)}, u32[]{:S(2)}) collective-permute-start(bf16[16,256]{1,0:T(8,128)(2,1)S(1)} %get-tuple-element.30.list_a), channel_id=1, source_target_pairs={{0,64},{1,65},{2,66},{3,67},{4,68},{5,69},{6,70},{7,71},{8,72},{9,... | collective-permute-start | bytes 24584 | tf_op jit(solution)/shard_map/ppermute | solution.py:398
  133.2 5.4 %collective-permute-done.10 = bf16[3,128,512]{2,1,0:T(8,128)(2,1)} collective-permute-done((bf16[3,128,512]{2,1,0:T(8,128)(2,1)S(1)}, bf16[3,128,512]{2,1,0:T(8,128)(2,1)}, u32[]{:S(2)}, u32[]{:S(2)}) %collective-permute-start.10) | collective-permute-done | bytes 393248 | tf_op jit(solution)/shard_map/ppermute | solution.py:319
  141.3 3.1 %fine.1 = f32[128,512]{1,0:T(8,128)S(1)} custom-call(f32[6,128,16]{2,1,0:T(8,128)S(1)} %copy-done.38, bf16[384,512]{1,0:T(8,128)(2,1)} %bitcast.26.left, bf16[384,512]{1,0:T(8,128)(2,1)S(1)} %bitcast.45, bf16[384,512]{1,0:T(8,128)(2,1)} %bitcast.28.right, bf16[128,512]{1,0:T(8,128)(2,1)S(1)} %copy-done.17, bf16[3,16,512]{2,1,0:T(8,128)(2,1)S(1)} %copy-done.20), custom_call_target="tpu_custom_call" | custom-call | flops 1073741824 | bytes 3145728 | tf_op jit(solution)/shard_map/fine/pallas_call | solution.py:71
  146.8 5.6 %mesh.1 = bf16[128,512]{1,0:T(8,128)(2,1)S(1)} custom-call(s32[1,5]{1,0:T(1,128)S(1)} %bitcast.53, f32[128,512]{1,0:T(8,128)S(1)} %fine.1, bf16[16,256]{1,0:T(8,128)(2,1)S(1)} %get-tuple-element.30.list_a, bf16[16,256]{1,0:T(8,128)(2,1)S(1)} %collective-permute-done.12.list_b, bf16[16,256]{1,0:T(8,128)(2,1)} %collective-permute-done.13.list_c, ...), custom_call_target="tpu_custom_call" | custom-call | flops 2147483648 | bytes 6291456 | tf_op jit(solution)/shard_map/mesh/pallas_call | solution.py:71
  152.4 2.8 %collective-permute-start.24 = (bf16[128,512]{1,0:T(8,128)(2,1)S(1)}, bf16[128,512]{1,0:T(8,128)(2,1)S(1)}, u32[]{:S(2)}, u32[]{:S(2)}) collective-permute-start(bf16[128,512]{1,0:T(8,128)(2,1)S(1)} %mesh.1), channel_id=1, source_target_pairs={{0,16},{16,32},{32,48},{48,64},{64,80},{80,96},{96,112},{1,17},{17... | collective-permute-start | bytes 393224 | tf_op jit(solution)/shard_map/ppermute | solution.py:319
  155.2 4.5 %collective-permute-start.25 = (bf16[128,512]{1,0:T(8,128)(2,1)S(1)}, bf16[128,512]{1,0:T(8,128)(2,1)S(1)}, u32[]{:S(2)}, u32[]{:S(2)}) collective-permute-start(bf16[128,512]{1,0:T(8,128)(2,1)S(1)} %mesh.1), channel_id=1, source_target_pairs={{16,0},{32,16},{48,32},{64,48},{80,64},{96,80},{112,96},{17,1},{33... | collective-permute-start | bytes 393224 | tf_op jit(solution)/shard_map/ppermute | solution.py:319
  160.8 4.1 %collective-permute-done.25 = bf16[128,512]{1,0:T(8,128)(2,1)S(1)} collective-permute-done((bf16[128,512]{1,0:T(8,128)(2,1)S(1)}, bf16[128,512]{1,0:T(8,128)(2,1)S(1)}, u32[]{:S(2)}, u32[]{:S(2)}) %collective-permute-start.25) | collective-permute-done | bytes 131104 | tf_op jit(solution)/shard_map/ppermute | solution.py:319
  164.9 3.8 %collective-permute-start.27 = (bf16[3,128,512]{2,1,0:T(8,128)(2,1)S(1)}, bf16[3,128,512]{2,1,0:T(8,128)(2,1)S(1)}, u32[]{:S(2)}, u32[]{:S(2)}) collective-permute-start(bf16[3,128,512]{2,1,0:T(8,128)(2,1)S(1)} %pad_maximum_fusion.2), channel_id=1, source_target_pairs={{0,15},{1,0},{2,1},{3,2},{4,3},{5,4},{6,5},{7,6},{8,7},{9,8},{10,9... | collective-permute-start | bytes 1179656 | tf_op jit(solution)/shard_map/ppermute | solution.py:319
  177.1 9.8 %decode.1 = bf16[1024,227]{1,0:T(8,128)(2,1)S(1)} custom-call(f32[3,1024,16]{2,1,0:T(8,128)S(1)} %copy-done.36, bf16[384,512]{1,0:T(8,128)(2,1)S(1)} %bitcast.56, bf16[384,512]{1,0:T(8,128)(2,1)S(1)} %bitcast.46, bf16[384,512]{1,0:T(8,128)(2,1)S(1)} %bitcast.57, bf16[1024,512]{1,0:T(8,128)(2,1)S(1)} %get-tuple-element.33.recv, ...), custom_call_target="tpu_custom_call" | custom-call | flops 4294967296 | bytes 8388608 | tf_op jit(solution)/shard_map/decode/pallas_call | solution.py:71
  (139 shorter events, 46.7 us)
Async XLA Ops:
  0.0 27.1 %copy-start.32 = (f32[1,1,4,768]{3,2,1,0:T(4,128)S(1)}, f32[1,1,4,768]{3,2,1,0:T(4,128)}, u32[]{:S(2)}) copy-start(f32[1,1,4,768]{3,2,1,0:T(4,128)} %param.34) | copy-start | bytes 36868
  5.9 10.2 %collective-permute-start = (bf16[192,512]{1,0:T(8,128)(2,1)S(1)}, bf16[192,512]{1,0:T(8,128)(2,1)S(1)}, u32[]{:S(2)}, u32[]{:S(2)}) collective-permute-start(bf16[192,512]{1,0:T(8,128)(2,1)S(1)} %get-tuple-element.22.payload), channel_id=1, source_target_pairs={{0,16},{16,32},{32,48},{48,64},{64,80},{80,96},{96,112},{1,17},{17... | collective-permute-start | bytes 589832 | tf_op jit(solution)/shard_map/ppermute | solution.py:319
  9.8 11.8 %collective-permute-start.1 = (bf16[192,512]{1,0:T(8,128)(2,1)S(1)}, bf16[192,512]{1,0:T(8,128)(2,1)S(1)}, u32[]{:S(2)}, u32[]{:S(2)}) collective-permute-start(bf16[192,512]{1,0:T(8,128)(2,1)S(1)} %get-tuple-element.22.payload), channel_id=1, source_target_pairs={{16,0},{32,16},{48,32},{64,48},{80,64},{96,80},{112,96},{17,1},{33... | collective-permute-start | bytes 589832 | tf_op jit(solution)/shard_map/ppermute | solution.py:319
  21.7 16.0 %collective-permute-start.2 = (bf16[3,192,512]{2,1,0:T(8,128)(2,1)S(1)}, bf16[3,192,512]{2,1,0:T(8,128)(2,1)}, u32[]{:S(2)}, u32[]{:S(2)}) collective-permute-start(bf16[3,192,512]{2,1,0:T(8,128)(2,1)S(1)} %pad_maximum_fusion.centre), channel_id=1, source_target_pairs={{0,1},{1,2},{2,3},{3,4},{4,5},{5,6},{6,7},{7,8},{8,9},{9,10},{10,1... | collective-permute-start | bytes 1769480 | tf_op jit(solution)/shard_map/ppermute | solution.py:319
  21.8 15.9 %collective-permute-start.3 = (bf16[3,192,512]{2,1,0:T(8,128)(2,1)S(1)}, bf16[3,192,512]{2,1,0:T(8,128)(2,1)}, u32[]{:S(2)}, u32[]{:S(2)}) collective-permute-start(bf16[3,192,512]{2,1,0:T(8,128)(2,1)S(1)} %pad_maximum_fusion.centre), channel_id=1, source_target_pairs={{0,15},{1,0},{2,1},{3,2},{4,3},{5,4},{6,5},{7,6},{8,7},{9,8},{10,9... | collective-permute-start | bytes 1769480 | tf_op jit(solution)/shard_map/ppermute | solution.py:319
  29.1 40.5 %copy-start.19 = (bf16[3,16,512]{2,1,0:T(8,128)(2,1)}, bf16[3,16,512]{2,1,0:T(8,128)(2,1)S(1)}, u32[]{:S(2)}) copy-start(bf16[3,16,512]{2,1,0:T(8,128)(2,1)S(1)} %get-tuple-element.24.w_geom) | copy-start | bytes 147460
  49.6 12.1 %collective-permute-start.4 = (bf16[3,128,512]{2,1,0:T(8,128)(2,1)S(1)}, bf16[3,128,512]{2,1,0:T(8,128)(2,1)S(1)}, u32[]{:S(2)}, u32[]{:S(2)}) collective-permute-start(bf16[3,128,512]{2,1,0:T(8,128)(2,1)S(1)} %get-tuple-element.25), channel_id=1, source_target_pairs={{0,1},{1,2},{2,3},{3,4},{4,5},{5,6},{6,7},{7,8},{8,9},{9,10},{10,1... | collective-permute-start | bytes 1179656 | tf_op jit(solution)/shard_map/ppermute | solution.py:319
  51.5 10.2 %collective-permute-start.5 = (bf16[3,128,512]{2,1,0:T(8,128)(2,1)S(1)}, bf16[3,128,512]{2,1,0:T(8,128)(2,1)S(1)}, u32[]{:S(2)}, u32[]{:S(2)}) collective-permute-start(bf16[3,128,512]{2,1,0:T(8,128)(2,1)S(1)} %get-tuple-element.26), channel_id=1, source_target_pairs={{0,15},{1,0},{2,1},{3,2},{4,3},{5,4},{6,5},{7,6},{8,7},{9,8},{10,9... | collective-permute-start | bytes 1179656 | tf_op jit(solution)/shard_map/ppermute | solution.py:319
  61.8 14.8 %collective-permute-start.6 = (bf16[128,512]{1,0:T(8,128)(2,1)S(1)}, bf16[128,512]{1,0:T(8,128)(2,1)S(1)}, u32[]{:S(2)}, u32[]{:S(2)}) collective-permute-start(bf16[128,512]{1,0:T(8,128)(2,1)S(1)} %get-tuple-element.36), channel_id=1, source_target_pairs={{0,16},{16,32},{32,48},{48,64},{64,80},{80,96},{96,112},{1,17},{17... | collective-permute-start | bytes 393224 | tf_op jit(solution)/shard_map/ppermute | solution.py:319
  66.5 10.2 %collective-permute-start.7 = (bf16[128,512]{1,0:T(8,128)(2,1)S(1)}, bf16[128,512]{1,0:T(8,128)(2,1)S(1)}, u32[]{:S(2)}, u32[]{:S(2)}) collective-permute-start(bf16[128,512]{1,0:T(8,128)(2,1)S(1)} %get-tuple-element.35), channel_id=1, source_target_pairs={{16,0},{32,16},{48,32},{64,48},{80,64},{96,80},{112,96},{17,1},{33... | collective-permute-start | bytes 393224 | tf_op jit(solution)/shard_map/ppermute | solution.py:319
  77.7 47.7 %copy-start.14 = (bf16[128,512]{1,0:T(8,128)(2,1)}, bf16[128,512]{1,0:T(8,128)(2,1)S(1)}, u32[]{:S(2)}) copy-start(bf16[128,512]{1,0:T(8,128)(2,1)S(1)} %get-tuple-element.31.mesh_one) | copy-start | bytes 393220
  77.7 47.8 %copy-start.16 = (bf16[128,512]{1,0:T(8,128)(2,1)}, bf16[128,512]{1,0:T(8,128)(2,1)S(1)}, u32[]{:S(2)}) copy-start(bf16[128,512]{1,0:T(8,128)(2,1)S(1)} %get-tuple-element.29.recv) | copy-start | bytes 393220
  78.4 7.5 %collective-permute-start.14 = (bf16[16,512]{1,0:T(8,128)(2,1)S(1)}, bf16[16,512]{1,0:T(8,128)(2,1)S(1)}, u32[]{:S(2)}, u32[]{:S(2)}) collective-permute-start(bf16[16,512]{1,0:T(8,128)(2,1)S(1)} %get-tuple-element.39), channel_id=1, source_target_pairs={{0,32},{16,48},{32,64},{48,80},{64,96},{80,112},{96,0},{112,16},{1... | collective-permute-start | bytes 49160 | tf_op jit(solution)/shard_map/ppermute | solution.py:331
  81.6 5.2 %collective-permute-start.15 = (bf16[16,512]{1,0:T(8,128)(2,1)S(1)}, bf16[16,512]{1,0:T(8,128)(2,1)S(1)}, u32[]{:S(2)}, u32[]{:S(2)}) collective-permute-start(bf16[16,512]{1,0:T(8,128)(2,1)S(1)} %get-tuple-element.39), channel_id=1, source_target_pairs={{0,64},{16,80},{32,96},{48,112},{64,0},{80,16},{96,32},{112,48},{1... | collective-permute-start | bytes 49160 | tf_op jit(solution)/shard_map/ppermute | solution.py:331
  83.5 3.9 %collective-permute-start.16 = (bf16[16,512]{1,0:T(8,128)(2,1)S(1)}, bf16[16,512]{1,0:T(8,128)(2,1)S(1)}, u32[]{:S(2)}, u32[]{:S(2)}) collective-permute-start(bf16[16,512]{1,0:T(8,128)(2,1)S(1)} %get-tuple-element.39), channel_id=1, source_target_pairs={{0,96},{16,112},{32,0},{48,16},{64,32},{80,48},{96,64},{112,80},{1... | collective-permute-start | bytes 49160 | tf_op jit(solution)/shard_map/ppermute | solution.py:331
  87.3 6.5 %collective-permute-start.17 = (bf16[64,512]{1,0:T(8,128)(2,1)S(1)}, bf16[64,512]{1,0:T(8,128)(2,1)S(1)}, u32[]{:S(2)}, u32[]{:S(2)}) collective-permute-start(bf16[64,512]{1,0:T(8,128)(2,1)S(1)} %pad_maximum_fusion.3), channel_id=1, source_target_pairs={{0,4},{1,5},{2,6},{3,7},{4,8},{5,9},{6,10},{7,11},{8,12},{9,13},{1... | collective-permute-start | bytes 196616 | tf_op jit(solution)/shard_map/ppermute | solution.py:331
  87.8 6.7 %collective-permute-start.18 = (bf16[64,512]{1,0:T(8,128)(2,1)S(1)}, bf16[64,512]{1,0:T(8,128)(2,1)S(1)}, u32[]{:S(2)}, u32[]{:S(2)}) collective-permute-start(bf16[64,512]{1,0:T(8,128)(2,1)S(1)} %pad_maximum_fusion.3), channel_id=1, source_target_pairs={{0,8},{1,9},{2,10},{3,11},{4,12},{5,13},{6,14},{7,15},{8,0},{9,1},... | collective-permute-start | bytes 196616 | tf_op jit(solution)/shard_map/ppermute | solution.py:331
  90.7 4.3 %collective-permute-start.19 = (bf16[64,512]{1,0:T(8,128)(2,1)S(1)}, bf16[64,512]{1,0:T(8,128)(2,1)S(1)}, u32[]{:S(2)}, u32[]{:S(2)}) collective-permute-start(bf16[64,512]{1,0:T(8,128)(2,1)S(1)} %pad_maximum_fusion.3), channel_id=1, source_target_pairs={{0,12},{1,13},{2,14},{3,15},{4,0},{5,1},{6,2},{7,3},{8,4},{9,5},{1... | collective-permute-start | bytes 196616 | tf_op jit(solution)/shard_map/ppermute | solution.py:331
  95.7 8.8 %collective-permute-start.20 = (bf16[256,512]{1,0:T(8,128)(2,1)S(1)}, bf16[256,512]{1,0:T(8,128)(2,1)S(1)}, u32[]{:S(2)}, u32[]{:S(2)}) collective-permute-start(bf16[256,512]{1,0:T(8,128)(2,1)S(1)} %get-tuple-element.40), channel_id=1, source_target_pairs={{0,2},{1,3},{2,16},{3,17},{4,6},{5,7},{6,20},{7,21},{8,10},{9,11},... | collective-permute-start | bytes 786440 | tf_op jit(solution)/shard_map/ppermute | solution.py:331
  95.7 13.6 %collective-permute-start.21 = (bf16[256,512]{1,0:T(8,128)(2,1)S(1)}, bf16[256,512]{1,0:T(8,128)(2,1)S(1)}, u32[]{:S(2)}, u32[]{:S(2)}) collective-permute-start(bf16[256,512]{1,0:T(8,128)(2,1)S(1)} %get-tuple-element.40), channel_id=1, source_target_pairs={{0,16},{1,17},{2,18},{3,19},{4,20},{5,21},{6,22},{7,23},{8,24},{9,... | collective-permute-start | bytes 786440 | tf_op jit(solution)/shard_map/ppermute | solution.py:331
  99.7 10.4 %collective-permute-start.22 = (bf16[256,512]{1,0:T(8,128)(2,1)S(1)}, bf16[256,512]{1,0:T(8,128)(2,1)S(1)}, u32[]{:S(2)}, u32[]{:S(2)}) collective-permute-start(bf16[256,512]{1,0:T(8,128)(2,1)S(1)} %get-tuple-element.40), channel_id=1, source_target_pairs={{0,18},{1,19},{2,0},{3,1},{4,22},{5,23},{6,4},{7,5},{8,26},{9,27},... | collective-permute-start | bytes 786440 | tf_op jit(solution)/shard_map/ppermute | solution.py:331
  110.8 33.6 %collective-permute-start.23 = (bf16[1024,512]{1,0:T(8,128)(2,1)}, bf16[1024,512]{1,0:T(8,128)(2,1)}, u32[]{:S(2)}, u32[]{:S(2)}) collective-permute-start(bf16[1024,512]{1,0:T(8,128)(2,1)} %constant_dynamic-update-slice_fusion.7.coarse_a), channel_id=1, source_target_pairs={{0,1},{1,0},{2,3},{3,2},{4,5},{5,4},{6,7},{7,6},{8,9},{9,8},{10,11... | collective-permute-start | bytes 3145736 | tf_op jit(solution)/shard_map/ppermute | solution.py:352
  110.8 9.3 %collective-permute-start.8 = (bf16[128,512]{1,0:T(8,128)(2,1)S(1)}, bf16[128,512]{1,0:T(8,128)(2,1)S(1)}, u32[]{:S(2)}, u32[]{:S(2)}) collective-permute-start(bf16[128,512]{1,0:T(8,128)(2,1)S(1)} %get-tuple-element.28), channel_id=1, source_target_pairs={{0,16},{16,32},{32,48},{48,64},{64,80},{80,96},{96,112},{1,17},{17... | collective-permute-start | bytes 393224 | tf_op jit(solution)/shard_map/ppermute | solution.py:319
  115.4 9.9 %collective-permute-start.9 = (bf16[128,512]{1,0:T(8,128)(2,1)S(1)}, bf16[128,512]{1,0:T(8,128)(2,1)S(1)}, u32[]{:S(2)}, u32[]{:S(2)}) collective-permute-start(bf16[128,512]{1,0:T(8,128)(2,1)S(1)} %get-tuple-element.28), channel_id=1, source_target_pairs={{16,0},{32,16},{48,32},{64,48},{80,64},{96,80},{112,96},{17,1},{33... | collective-permute-start | bytes 393224 | tf_op jit(solution)/shard_map/ppermute | solution.py:319
  125.4 13.2 %collective-permute-start.10 = (bf16[3,128,512]{2,1,0:T(8,128)(2,1)S(1)}, bf16[3,128,512]{2,1,0:T(8,128)(2,1)}, u32[]{:S(2)}, u32[]{:S(2)}) collective-permute-start(bf16[3,128,512]{2,1,0:T(8,128)(2,1)S(1)} %pad_maximum_fusion.1), channel_id=1, source_target_pairs={{0,1},{1,2},{2,3},{3,4},{4,5},{5,6},{6,7},{7,8},{8,9},{9,10},{10,1... | collective-permute-start | bytes 1179656 | tf_op jit(solution)/shard_map/ppermute | solution.py:319
  125.5 13.1 %collective-permute-start.11 = (bf16[3,128,512]{2,1,0:T(8,128)(2,1)S(1)}, bf16[3,128,512]{2,1,0:T(8,128)(2,1)}, u32[]{:S(2)}, u32[]{:S(2)}) collective-permute-start(bf16[3,128,512]{2,1,0:T(8,128)(2,1)S(1)} %pad_maximum_fusion.1), channel_id=1, source_target_pairs={{0,15},{1,0},{2,1},{3,2},{4,3},{5,4},{6,5},{7,6},{8,7},{9,8},{10,9... | collective-permute-start | bytes 1179656 | tf_op jit(solution)/shard_map/ppermute | solution.py:319
  129.3 15.1 %collective-permute-start.12 = (bf16[16,256]{1,0:T(8,128)(2,1)S(1)}, bf16[16,256]{1,0:T(8,128)(2,1)S(1)}, u32[]{:S(2)}, u32[]{:S(2)}) collective-permute-start(bf16[16,256]{1,0:T(8,128)(2,1)S(1)} %get-tuple-element.30.list_a), channel_id=1, source_target_pairs={{0,127},{1,0},{2,1},{3,2},{4,3},{5,4},{6,5},{7,6},{8,7},{9,8},{10,... | collective-permute-start | bytes 24584 | tf_op jit(solution)/shard_map/ppermute | solution.py:397
  129.3 15.1 %collective-permute-start.13 = (bf16[16,256]{1,0:T(8,128)(2,1)S(1)}, bf16[16,256]{1,0:T(8,128)(2,1)}, u32[]{:S(2)}, u32[]{:S(2)}) collective-permute-start(bf16[16,256]{1,0:T(8,128)(2,1)S(1)} %get-tuple-element.30.list_a), channel_id=1, source_target_pairs={{0,64},{1,65},{2,66},{3,67},{4,68},{5,69},{6,70},{7,71},{8,72},{9,... | collective-permute-start | bytes 24584 | tf_op jit(solution)/shard_map/ppermute | solution.py:398
  152.4 8.4 %collective-permute-start.24 = (bf16[128,512]{1,0:T(8,128)(2,1)S(1)}, bf16[128,512]{1,0:T(8,128)(2,1)S(1)}, u32[]{:S(2)}, u32[]{:S(2)}) collective-permute-start(bf16[128,512]{1,0:T(8,128)(2,1)S(1)} %mesh.1), channel_id=1, source_target_pairs={{0,16},{16,32},{32,48},{48,64},{64,80},{80,96},{96,112},{1,17},{17... | collective-permute-start | bytes 393224 | tf_op jit(solution)/shard_map/ppermute | solution.py:319
  155.2 9.6 %collective-permute-start.25 = (bf16[128,512]{1,0:T(8,128)(2,1)S(1)}, bf16[128,512]{1,0:T(8,128)(2,1)S(1)}, u32[]{:S(2)}, u32[]{:S(2)}) collective-permute-start(bf16[128,512]{1,0:T(8,128)(2,1)S(1)} %mesh.1), channel_id=1, source_target_pairs={{16,0},{32,16},{48,32},{64,48},{80,64},{96,80},{112,96},{17,1},{33... | collective-permute-start | bytes 393224 | tf_op jit(solution)/shard_map/ppermute | solution.py:319
  164.9 12.0 %collective-permute-start.26 = (bf16[3,128,512]{2,1,0:T(8,128)(2,1)S(1)}, bf16[3,128,512]{2,1,0:T(8,128)(2,1)S(1)}, u32[]{:S(2)}, u32[]{:S(2)}) collective-permute-start(bf16[3,128,512]{2,1,0:T(8,128)(2,1)S(1)} %pad_maximum_fusion.2), channel_id=1, source_target_pairs={{0,1},{1,2},{2,3},{3,4},{4,5},{5,6},{6,7},{7,8},{8,9},{9,10},{10,1... | collective-permute-start | bytes 1179656 | tf_op jit(solution)/shard_map/ppermute | solution.py:319
  164.9 12.0 %collective-permute-start.27 = (bf16[3,128,512]{2,1,0:T(8,128)(2,1)S(1)}, bf16[3,128,512]{2,1,0:T(8,128)(2,1)S(1)}, u32[]{:S(2)}, u32[]{:S(2)}) collective-permute-start(bf16[3,128,512]{2,1,0:T(8,128)(2,1)S(1)} %pad_maximum_fusion.2), channel_id=1, source_target_pairs={{0,15},{1,0},{2,1},{3,2},{4,3},{5,4},{6,5},{7,6},{8,7},{9,8},{10,9... | collective-permute-start | bytes 1179656 | tf_op jit(solution)/shard_map/ppermute | solution.py:319
  (38 other events, 273.3 us)

commit v2 on v1

v2 whole, which is shorter than its diff:
```python
import functools

import jax
import jax.numpy as jnp
from jax import lax
from jax.experimental import pallas as pl
from jax.experimental.pallas import tpu as pltpu
from jax.sharding import PartitionSpec as P

BF = jnp.bfloat16
F32 = jnp.float32
I32 = jnp.int32
WIDTH = 512
GRID_NODES = 1024
MESH_NODES = 128
MESH_DEGREE = 6
GRID_DEGREE = 3
COARSE_DEV = 16
SLOTS = 2048
CHUNK = 512
CHUNKS = SLOTS // CHUNK
PAYLOAD = MESH_NODES + 16 * CHUNKS
LON = 16
NEAR_SLOTS = 160
COARSE_SLOTS = 320
GROUPS = (5, 3, 7, 0, 1, 2, 6, 4, 8)
VMEM_BYTES = 20 * 1024 * 1024


def mm(left, right):
    return jnp.dot(left, right, preferred_element_type=F32)


def mm_t(left, right):
    return lax.dot_general(left, right, (((0,), (0,)), ((), ())), preferred_element_type=F32)


def mm_nt(left, right):
    return lax.dot_general(left, right, (((1,), (1,)), ((), ())), preferred_element_type=F32)


def silu(v):
    half = 0.5 * v
    return half + half * jnp.tanh(half)


def one_hot(column, width):
    spots = lax.broadcasted_iota(I32, (column.shape[0], width), 1)
    return jnp.where(spots == column, 1.0, 0.0).astype(BF)


class Load:
    def __init__(self, index, shape):
        self.index, self.shape = index, shape


class View:
    def __init__(self, index):
        self.index = index


class Arriving:
    def __init__(self, copy, ref):
        self.copy, self.ref = copy, ref
        self.shape = ref.shape

    def ready(self):
        if self.copy is not None:
            self.copy.wait()
            self.copy = None
        return self.ref

    def __getitem__(self, index):
        return self.ready()[index]


V = pl.BlockSpec(memory_space=pltpu.VMEM)
SMEM = pl.BlockSpec(memory_space=pltpu.SMEM)
ANY = pl.BlockSpec(memory_space=pl.ANY)
HBM = pl.BlockSpec(memory_space=pltpu.HBM)


def square(block, kind):
    return Load((block, kind), (WIDTH, WIDTH))


def first_half(block, half):
    return Load((block, slice(WIDTH * half, WIDTH * (half + 1))), (WIDTH, WIDTH))


def second_of(block):
    return Load((block,), (WIDTH, WIDTH))


def kernel_call(body, outs, specs, args, scratch=(), flops=0, moved=0, name=None, out_specs=None):
    loads = [(k, spec, args[k].dtype) for k, spec in enumerate(specs) if isinstance(spec, Load)]
    n_in, n_loads = len(specs), len(loads)

    def run(*refs):
        given, rest = list(refs[:n_in]), list(refs[n_in:])
        if n_loads:
            sems = rest[-1]
            buffers = rest[-1 - n_loads : -1]
            rest = rest[: -1 - n_loads]
            for at, ((k, spec, _), buffer) in enumerate(zip(loads, buffers)):
                source = given[k].at[spec.index] if spec.index else given[k]
                copy = pltpu.make_async_copy(source, buffer, sems.at[at])
                copy.start()
                given[k] = Arriving(copy, buffer)
        for k, spec in enumerate(specs):
            if isinstance(spec, View):
                given[k] = given[k].at[spec.index]
        body(*given, *rest)
        for part in given:
            if isinstance(part, Arriving):
                part.ready()

    extra = [pltpu.VMEM(spec.shape, dtype) for _, spec, dtype in loads]
    if loads:
        extra.append(pltpu.SemaphoreType.DMA((n_loads,)))
    many = isinstance(outs, tuple)
    args = [
        pltpu.with_memory_space_constraint(arg, pltpu.HBM) if isinstance(spec, Load) else arg
        for spec, arg in zip(specs, args)
    ]
    return pl.pallas_call(
        run,
        out_shape=outs,
        in_specs=[HBM if isinstance(q, Load) else V if isinstance(q, View) else q for q in specs],
        out_specs=out_specs if out_specs is not None else (V,) * len(outs) if many else V,
        scratch_shapes=list(scratch) + extra,
        compiler_params=pltpu.CompilerParams(vmem_limit_bytes=VMEM_BYTES),
        cost_estimate=pl.CostEstimate(flops=flops, bytes_accessed=moved, transcendentals=0),
        name=name,
    )(*args)


def shaped(shape, dtype):
    return jax.ShapeDtypeStruct(shape, dtype)


def fill_list(scr, width, indices, geometry):
    for row, value in enumerate(indices):
        scr[row : row + 1, 0:width] = value.astype(F32)
    high = geometry.astype(BF).astype(F32)
    scr[4:8, 0:width] = high
    scr[8:12, 0:width] = geometry - high
    scr[12:16, 0:width] = high


def pack_body(count, senders, receivers, geometry, state, c_senders, c_receivers, c_geometry, out, c_out, scr):
    out[0:MESH_NODES, :] = state[...]
    for c in range(CHUNKS):
        cols = slice(c * CHUNK, (c + 1) * CHUNK)
        s = senders[:, cols]
        edge = lax.broadcasted_iota(I32, (1, CHUNK), 1) + c * CHUNK
        code = jnp.where(edge < count[0, 0], lax.shift_right_logical(s, 10) + 1, 0)
        local = s & (GRID_NODES - 1)
        fill_list(
            scr, CHUNK, (code, lax.shift_right_logical(local, 8), local & 255, receivers[:, cols]), geometry[:, cols]
        )
        out[MESH_NODES + 16 * c : MESH_NODES + 16 * (c + 1), :] = scr[...].astype(BF)
    s = c_senders[...]
    r = c_receivers[...]
    n = s.shape[1]
    fill_list(
        scr, n, (lax.shift_right_logical(s, 8), s & 255, lax.shift_right_logical(r, 4), r & 15), c_geometry[...]
    )
    c_out[...] = scr[:, 0:n].astype(BF)


def prep_body(m_senders, m_geometry, d_senders, d_geometry, weight, m_out, d_out, w_out, scr, turned):
    for senders, geometry, degree, out in (
        (m_senders, m_geometry, MESH_DEGREE, m_out),
        (d_senders, d_geometry, GRID_DEGREE, d_out),
    ):
        n = senders.shape[1]
        s = senders[...]
        near = lax.shift_right_logical(s, 7)
        spot = jnp.zeros_like(near)
        for place, group in enumerate(GROUPS):
            spot = jnp.where(near == place, group, spot)
        spot = spot * MESH_NODES + (s & (MESH_NODES - 1))
        zero = jnp.zeros((1, n), F32)
        fill_list(scr, n, (spot, zero, zero, zero), geometry[...])
        turned[0:n, :] = scr[:, 0:n].T
        for t in range(degree):
            out[t] = turned[pl.ds(t, n // degree, stride=degree), :]
    for k in range(3):
        w = weight[k]
        high = w.astype(BF).astype(F32)
        scr[0:4, 0:WIDTH] = jnp.zeros((4, WIDTH), F32)
        scr[4:8, 0:WIDTH] = high
        scr[8:12, 0:WIDTH] = high
        scr[12:16, 0:WIDTH] = w - high
        w_out[k] = scr[:, 0:WIDTH].astype(BF)


def embed_body(x, w_in, w_out, w_send, latent, send):
    for b in range(4):
        rows = slice(256 * b, 256 * (b + 1))
        hidden = silu(mm(x[rows, :], w_in[...])).astype(BF)
        lat = mm(hidden, w_out[...]).astype(BF)
        latent[rows, :] = lat
        send[rows, :] = mm(lat, w_send[...]).astype(BF)


def grid_body(latent, w_recv, w_first, recv, base):
    for b in range(4):
        rows = slice(256 * b, 256 * (b + 1))
        recv[rows, :] = mm(latent[rows, :], w_recv[...]).astype(BF)
        base[rows, :] = mm(latent[rows, :], w_first[...])


def self_body(payload, send, w_recv, w_geom, out, q):
    q[...] = mm(payload[0:MESH_NODES, :], w_recv[...]).astype(BF)
    out[...] = jnp.zeros_like(out)

    @pl.loop(0, CHUNKS)
    def _(c):
        rows = pl.ds(pl.multiple_of(MESH_NODES + 16 * c, 16), 16)
        d = payload[rows, :].astype(F32).T
        for h in range(2):
            part = d[256 * h : 256 * (h + 1), :]
            s = (part[:, 1:2] * 256.0 + part[:, 2:3]).astype(I32)
            r = jnp.where(part[:, 0:1] == 5.0, part[:, 3:4], -1.0).astype(I32)
            pick = one_hot(r, MESH_NODES)
            pre = mm(one_hot(s, GRID_NODES), send[...]) + mm(pick, q[...]) + mm(part.astype(BF), w_geom[...])
            out[...] += mm_t(pick, silu(pre).astype(BF))


def near_body(
    left, right, middle, left_pair, right_pair, send, w_recv, w_geom, order,
    o_left, o_right, o_middle, o_left_pair, o_right_pair, masks, ranks, q, edges, sums,
):
    lists = (
        (left, 5, o_left),
        (right, 3, o_right),
        (middle.at[0], 7, o_middle.at[0]),
        (middle.at[1], 1, o_middle.at[1]),
        (left_pair.at[0], 8, o_left_pair.at[0]),
        (left_pair.at[1], 2, o_left_pair.at[1]),
        (right_pair.at[0], 6, o_right_pair.at[0]),
        (right_pair.at[1], 0, o_right_pair.at[1]),
    )
    q[4 * MESH_NODES : 5 * MESH_NODES, :] = jnp.zeros((MESH_NODES, WIDTH), BF)

    def listed(src, c):
        return src[MESH_NODES + 16 * c : MESH_NODES + 16 * (c + 1), :]

    for i, (src, bucket, _) in enumerate(lists):
        q[MESH_NODES * bucket : MESH_NODES * (bucket + 1), :] = mm(src[0:MESH_NODES, :], w_recv[...]).astype(BF)
        for c in range(CHUNKS):
            row = i * CHUNKS + c
            code = listed(src, c).astype(F32)[0:1, :]
            masks[row : row + 1, :] = jnp.where(code == float(bucket + 1), 1.0, 0.0)
    n = masks.shape[0]
    mask = masks[...]
    before = lax.broadcasted_iota(I32, (CHUNK, CHUNK), 0) < lax.broadcasted_iota(I32, (CHUNK, CHUNK), 1)
    inside = mm(mask.astype(BF), jnp.where(before, 1.0, 0.0).astype(BF))
    mine = lax.broadcasted_iota(I32, (n, n), 0)
    other = lax.broadcasted_iota(I32, (n, n), 1)
    same = mine // CHUNKS == other // CHUNKS
    earlier = jnp.where((other < mine) & same, 1.0, 0.0).astype(BF)
    carried = mm(earlier, mask.astype(BF)).sum(axis=1, keepdims=True)
    ranks[...] = jnp.where(mask > 0.5, inside + carried, -1.0).astype(I32)

    slot = lax.broadcasted_iota(I32, (NEAR_SLOTS, CHUNK), 0)
    for i, (src, _, _) in enumerate(lists):
        d = jnp.zeros((NEAR_SLOTS, 16), F32)
        for c in range(CHUNKS):
            row = i * CHUNKS + c
            d += mm_nt(jnp.where(slot == ranks[row : row + 1, :], 1.0, 0.0).astype(BF), listed(src, c))
        edges[NEAR_SLOTS * i : NEAR_SLOTS * (i + 1), :] = d
    for j in range(4):
        d = edges[2 * NEAR_SLOTS * j : 2 * NEAR_SLOTS * (j + 1), :]
        s = (d[:, 1:2] * 256.0 + d[:, 2:3]).astype(I32)
        pre = mm(one_hot(s, GRID_NODES), send[...]) + mm(d.astype(BF), w_geom[...])
        r = jnp.where(d[:, 0:1] > 0.5, d[:, 3:4], -1.0).astype(I32)
        for h in range(2):
            bucket = lists[2 * j + h][1]
            part = slice(NEAR_SLOTS * h, NEAR_SLOTS * (h + 1))
            rows = slice(MESH_NODES * bucket, MESH_NODES * (bucket + 1))
            pick = one_hot(r[part, :], MESH_NODES)
            sums[rows, :] = mm_t(pick, silu(pre[part, :] + mm(pick, q[rows, :])).astype(BF))

    count = mm(jnp.where(same, 1.0, 0.0).astype(BF), mask.astype(BF)).sum(axis=1, keepdims=True)
    over = jnp.maximum(count - NEAR_SLOTS, 0.0)
    total = lax.shift_right_logical(jnp.sum(over).astype(I32), 2)

    @pl.when(total > 0)
    def _():
        across = lax.broadcasted_iota(I32, (n, 1), 0) // CHUNKS
        base = jnp.zeros((n, 1), F32)
        for i in range(len(lists) - 1):
            base += jnp.where(across > i, over[i * CHUNKS : i * CHUNKS + 1, :], 0.0)
        rank = ranks[...]
        ranks[...] = jnp.where(rank >= NEAR_SLOTS, rank - NEAR_SLOTS + base.astype(I32), -1)

        @pl.loop(0, lax.shift_right_logical(total + 127, 7))
        def _(k):
            late = lax.broadcasted_iota(I32, (128, CHUNK), 0) + k * 128
            d = jnp.zeros((128, 16), F32)
            for i, (src, _, _) in enumerate(lists):
                for c in range(CHUNKS):
                    row = i * CHUNKS + c
                    d += mm_nt(jnp.where(late == ranks[row : row + 1, :], 1.0, 0.0).astype(BF), listed(src, c))
            s = (d[:, 1:2] * 256.0 + d[:, 2:3]).astype(I32)
            code = d[:, 0:1]
            r = jnp.where(code > 0.5, (code - 1.0) * float(MESH_NODES) + d[:, 3:4], -1.0).astype(I32)
            pick = one_hot(r, 9 * MESH_NODES)
            pre = mm(one_hot(s, GRID_NODES), send[...]) + mm(pick, q[...]) + mm(d.astype(BF), w_geom[...])
            sums[...] += mm_t(pick, silu(pre).astype(BF))

    for _, bucket, dst in lists:
        dst[...] = sums[MESH_NODES * bucket : MESH_NODES * (bucket + 1), :].astype(BF)


def side_sum_body(middle, from_left, from_right, order, up, down):
    for k, out in ((0, up), (1, down)):
        total = middle[k].astype(F32) + from_left[k].astype(F32) + from_right[k].astype(F32)
        out[...] = total.astype(BF)


def join_body(parts, out):
    n = parts[0].shape[0]
    for k, part in enumerate(parts):
        out[n * k : n * (k + 1), :] = part[...]


def pair_body(up, down, order, out):
    out[0] = up[...]
    out[1] = down[...]


def four_body(a, b, c, d, out):
    join_body((a, b, c, d), out)


def four_pair_body(a, b, c, d, up, down, out, pair):
    join_body((a, b, c, d), out)
    pair[0] = up[...]
    pair[1] = down[...]


def split_mm(value, weight):
    high = value.astype(BF)
    low = (value - high.astype(F32)).astype(BF)
    return mm(high, weight) + mm(low, weight)


def node_rows(v, hidden_total, w_second, first_node, first_sum, second):
    m = split_mm(hidden_total, w_second).astype(BF)
    u = silu(mm(v, first_node) + mm(m, first_sum)).astype(BF)
    return (v.astype(F32) + mm(u, second)).astype(BF)


def node_body(
    own, from_left, from_right, up, down, state, w_second, first_node, first_sum, second, w_send, w_recv, order,
    mesh_one, send, recv,
):
    total = own[...] + from_left[...].astype(F32) + from_right[...].astype(F32)
    total = total + up[...].astype(F32) + down[...].astype(F32)
    one = node_rows(state[...], total, w_second[...], first_node[...], first_sum[...], second[...])
    mesh_one[...] = one
    send[...] = mm(one, w_send[...]).astype(BF)
    recv[...] = mm(one, w_recv[...]).astype(BF)


def near_groups(left, own, right, pair, left_pair, right_pair):
    pairs = (pair.at[0], pair.at[1], left_pair.at[0], left_pair.at[1], right_pair.at[0], right_pair.at[1])
    return (left, own, right) + pairs


def fine_body(edges, left, own, right, pair, left_pair, right_pair, recv, w_geom, out, rows):
    for k, part in enumerate(near_groups(left, own, right, pair, left_pair, right_pair)):
        rows[MESH_NODES * k : MESH_NODES * (k + 1), :] = part[...]
    rows[9 * MESH_NODES :, :] = jnp.zeros((MESH_NODES, WIDTH), BF)
    rows[9 * MESH_NODES : 9 * MESH_NODES + 16, :] = w_geom[...]
    q = recv[...].astype(F32)
    total = jnp.zeros((MESH_NODES, WIDTH), F32)
    for t in range(MESH_DEGREE):
        d = edges[t]
        spread = one_hot(d[:, 0:1].astype(I32), 9 * MESH_NODES)
        pre = q + mm(spread, rows[0 : 9 * MESH_NODES, :]) + mm(d.astype(BF), w_geom[...])
        total += silu(pre)
    out[...] = total


def coarse_prep_body(place, list_a, list_b, list_c, out, count, row):
    z, y, x, core, tile = (place[0, k] for k in range(5))
    n = list_a.shape[1]
    lists = (list_a, list_b, list_c)
    for k, edges in enumerate(lists):
        owner = edges[...].astype(F32)[2:3, :].astype(I32)
        row[k : k + 1, :] = jnp.where(owner == tile, 1.0, 0.0)
    row[3:8, :] = jnp.zeros((5, n), F32)
    mask = row[...]
    before = lax.broadcasted_iota(I32, (n, n), 0) < lax.broadcasted_iota(I32, (n, n), 1)
    inside = mm(mask.astype(BF), jnp.where(before, 1.0, 0.0).astype(BF))
    earlier = lax.broadcasted_iota(I32, (8, 8), 1) < lax.broadcasted_iota(I32, (8, 8), 0)
    carried = mm(jnp.where(earlier, 1.0, 0.0).astype(BF), mask.astype(BF)).sum(axis=1, keepdims=True)
    rank = jnp.where(mask > 0.5, inside + carried, -1.0).astype(I32)
    slot = lax.broadcasted_iota(I32, (3 * n, n), 0)
    d = jnp.zeros((3 * n, 16), F32)
    for k, edges in enumerate(lists):
        d += mm_nt(jnp.where(slot == rank[k : k + 1, :], 1.0, 0.0).astype(BF), edges[...])
    s = (d[:, 0:1] * 256.0 + d[:, 1:2]).astype(I32)
    t = lax.shift_right_logical(s, 4)
    lat = lax.shift_right_logical(t, 4)
    lon = t & 15
    gz = (z - lax.shift_right_logical(lat, 1)) & 3
    gy = (y - lax.shift_right_logical(lon, 2)) & 3
    gx = (x - ((lat & 1) * 2 + (lax.shift_right_logical(lon, 1) & 1))) & 3
    gc = (core + lon) & 1
    spot = (((gc * 4 + gx) * 4 + gy) * 4 + gz) * 16 + (s & 15)
    total = jnp.sum(mask).astype(I32)
    used = lax.broadcasted_iota(I32, (3 * n, 1), 0) < total
    r = jnp.where(used, d[:, 3:4], -1.0)
    lane = lax.broadcasted_iota(I32, (3 * n, 16), 1)
    out[...] = jnp.where(lane == 0, spot.astype(F32), jnp.where(lane == 1, r, d))
    count[0, 0] = total


def mesh_body(
    count, fine, edges, a0, a1, a2, a3, b0, b1, b2, b3, recv, mesh_one, w_geom, w_second, first_node, first_sum,
    second, w_send, send, rows, total,
):
    parts = (a0, a1, a2, a3, b0, b1, b2, b3)
    n = a0.shape[0]
    for k, part in enumerate(parts):
        rows[n * k : n * (k + 1), :] = part[...]
    q = recv[0:COARSE_DEV, :]

    def hidden_sum(d):
        pick = one_hot(d[:, 1:2].astype(I32), MESH_NODES)
        pre = mm(one_hot(d[:, 0:1].astype(I32), len(parts) * n), rows[...])
        pre += mm(pick[:, 0:COARSE_DEV], q) + mm(d.astype(BF), w_geom[...])
        return mm_t(pick, silu(pre).astype(BF))

    total[...] = fine[...] + hidden_sum(edges[0:COARSE_SLOTS, :])

    @pl.loop(COARSE_SLOTS // 64, lax.shift_right_logical(count[0, 0] + 63, 6))
    def _(k):
        total[...] += hidden_sum(edges[pl.ds(pl.multiple_of(64 * k, 64), 64), :])

    two = node_rows(mesh_one[...], total[...], w_second[...], first_node[...], first_sum[...], second[...])
    send[...] = mm(two, w_send[...]).astype(BF)


def decode_early_body(edges, left, own, right, pair, recv, w_geom, out, rows):
    for k, part in enumerate((left, own, right, pair.at[0], pair.at[1])):
        rows[MESH_NODES * k : MESH_NODES * (k + 1), :] = part[...]
    n = 5 * MESH_NODES
    rows[n : n + 128, :] = jnp.zeros((128, WIDTH), BF)
    rows[n : n + 16, :] = w_geom[...]

    @pl.loop(0, 4)
    def _(b):
        span = pl.ds(pl.multiple_of(256 * b, 256), 256)
        q = recv[span, :].astype(F32)
        for t in range(GRID_DEGREE):
            d = edges[t, span, :]
            spread = one_hot(d[:, 0:1].astype(I32), n)
            out[t, span, :] = q + mm(spread, rows[0:n, :]) + mm(d.astype(BF), w_geom[...])


def decode_body(edges, early, left_pair, right_pair, base, w_second, first_sum, head, out, rows):
    w_second, first_sum = w_second.ready(), first_sum.ready()
    for k, part in enumerate((left_pair.at[0], left_pair.at[1], right_pair.at[0], right_pair.at[1])):
        rows[MESH_NODES * k : MESH_NODES * (k + 1), :] = part[...]

    @pl.loop(0, 4)
    def _(b):
        span = pl.ds(pl.multiple_of(256 * b, 256), 256)
        total = jnp.zeros((256, WIDTH), F32)
        for t in range(GRID_DEGREE):
            spot = edges[t, span, :][:, 0:1].astype(I32) - 5 * MESH_NODES
            total += silu(early[t, span, :] + mm(one_hot(spot, 4 * MESH_NODES), rows[...]))
        summed = mm(total.astype(BF), w_second[...]).astype(BF)
        hidden = silu(base[span, :] + mm(summed, first_sum[...])).astype(BF)
        out[:, span] = mm_nt(head[...], hidden).astype(BF)


def shift(value, axis, step, periodic):
    n = lax.axis_size(axis)
    pairs = [(i, (i + step) % n) for i in range(n) if periodic or 0 <= i + step < n]
    return lax.ppermute(value, axis, pairs)


def first_stage(value):
    up = shift(value, "lat", 1, False)
    down = shift(value, "lat", -1, False)
    return up, down, shift(value, "lon", 1, True), shift(value, "lon", -1, True)


def second_stage(pair):
    return shift(pair, "lon", 1, True), shift(pair, "lon", -1, True)


def along_z(s):
    return [(i, ((i // 2 + s) % 4) * 2 + i % 2) for i in range(8)]


def along_y(s):
    return [(i, ((i // 4 + s) % 4) * 4 + i % 4) for i in range(16)]


def along_x(s):
    pairs = []
    for lat in range(8):
        for lon in range(16):
            x = ((lat % 2) * 2 + (lon // 2) % 2 + s) % 4
            to_lat = lat // 2 * 2 + x // 2
            to_lon = lon // 4 * 4 + (x % 2) * 2 + lon % 2
            pairs.append((lat * 16 + lon, to_lat * 16 + to_lon))
    return pairs


def four(value, axis, pairs_of):
    return [value] + [lax.ppermute(value, axis, pairs_of(s)) for s in (1, 2, 3)]


def per_device(
    grid_inputs,
    mesh_state,
    embed_in,
    embed_out,
    edge_square,
    edge_geom_weight,
    node_first,
    node_second,
    head,
    g2m_senders,
    g2m_receivers,
    g2m_counts,
    g2m_geom,
    mesh_senders,
    mesh_geom,
    coarse_senders,
    coarse_receivers,
    coarse_geom,
    m2g_senders,
    m2g_geom,
):
    mesh_rows = (MESH_NODES, WIDTH)
    grid_rows = (GRID_NODES, WIDTH)
    pair_rows = (2,) + mesh_rows
    grid_flops = 2 * GRID_NODES * WIDTH * WIDTH
    mesh_flops = grid_flops // 8
    both = ("lat", "lon")
    tiles = lax.axis_size(both)
    lat, lon = lax.axis_index("lat"), lax.axis_index("lon")
    place = jnp.stack([lat // 2, lon // 4, (lat % 2) * 2 + (lon // 2) % 2, lon % 2, lat * LON + lon])[None]

    pack_args = (
        g2m_senders, g2m_receivers, g2m_geom, mesh_state, coarse_senders, coarse_receivers, coarse_geom
    )

    def part_of(array):
        n = array.ndim - 2
        return Load((0,) if n == 1 else (0, 0), array.shape[1:] if n == 1 else array.shape[2:])

    payload, coarse_list = kernel_call(
        pack_body,
        (shaped((PAYLOAD, WIDTH), BF), shaped((16, coarse_senders.shape[2]), BF)),
        [SMEM] + [part_of(a) for a in pack_args],
        (g2m_counts,) + pack_args,
        [pltpu.VMEM((16, CHUNK), F32)],
        name="pack",
    )
    up, down, near_left, near_right = first_stage(payload)
    prep_args = (mesh_senders, mesh_geom, m2g_senders, m2g_geom)
    m_edges, d_edges, geom = kernel_call(
        prep_body,
        (
            shaped((MESH_DEGREE, MESH_NODES, 16), F32),
            shaped((GRID_DEGREE, GRID_NODES, 16), F32),
            shaped((3, 16, WIDTH), BF),
        ),
        [part_of(a) for a in prep_args] + [Load((), edge_geom_weight.shape)],
        prep_args + (edge_geom_weight,),
        [pltpu.VMEM((16, 3072), F32), pltpu.VMEM((3072, 16), F32)],
        flops=grid_flops,
        name="prep",
    )
    latent, grid_send = kernel_call(
        embed_body,
        (shaped(grid_rows, BF), shaped(grid_rows, BF)),
        [V, Load((), embed_in.shape), Load((), embed_out.shape), square(0, 0)],
        (grid_inputs[0, 0], embed_in, embed_out, edge_square),
        flops=3 * grid_flops,
        moved=5 << 20,
        name="embed",
    )

    def geom_of(k):
        return View(k)

    def paired(up, down, order):
        shape = (2,) + up.shape
        return kernel_call(pair_body, shaped(shape, BF), [V, V, ANY], (up, down, order), name="pair")

    near_middle = paired(up, down, grid_send)
    near_left_pair, near_right_pair = second_stage(near_middle)
    own_sum = kernel_call(
        self_body,
        shaped(mesh_rows, F32),
        [V, V, square(0, 1), geom_of(0)],
        (payload, grid_send, edge_square, geom),
        [pltpu.VMEM(mesh_rows, BF)],
        flops=5 * grid_flops,
        moved=3 << 20,
        name="own",
    )
    to_left, to_right, to_middle, to_left_pair, to_right_pair = kernel_call(
        near_body,
        (shaped(mesh_rows, BF),) * 2 + (shaped(pair_rows, BF),) * 3,
        [V, V, V, V, V, V, square(0, 1), geom_of(0), ANY],
        (near_left, near_right, near_middle, near_left_pair, near_right_pair, grid_send, edge_square, geom, own_sum),
        [
            pltpu.VMEM((8 * CHUNKS, CHUNK), F32),
            pltpu.VMEM((8 * CHUNKS, CHUNK), I32),
            pltpu.VMEM((9 * MESH_NODES, WIDTH), BF),
            pltpu.VMEM((8 * NEAR_SLOTS, 16), F32),
            pltpu.VMEM((9 * MESH_NODES, WIDTH), F32),
        ],
        flops=4 * grid_flops,
        moved=5 << 20,
        name="near",
    )
    pair_left = shift(to_right_pair, "lon", 1, True)
    pair_right = shift(to_left_pair, "lon", -1, True)
    list_next = lax.ppermute(coarse_list, both, [(t, (t - 1) % tiles) for t in range(tiles)])
    list_far = lax.ppermute(coarse_list, both, [(t, (t + tiles // 2) % tiles) for t in range(tiles)])
    grid_recv, grid_base = kernel_call(
        grid_body,
        (shaped(grid_rows, BF), shaped(grid_rows, F32)),
        [V, square(2, 1), first_half(2, 0)],
        (latent, edge_square, node_first),
        flops=2 * grid_flops,
        moved=5 << 20,
        name="grid",
    )
    to_up, to_down = kernel_call(
        side_sum_body,
        (shaped(mesh_rows, BF),) * 2,
        [V, V, V, ANY],
        (to_middle, pair_left, pair_right, grid_recv),
        name="sides",
    )
    from_left = shift(to_right, "lon", 1, True)
    from_right = shift(to_left, "lon", -1, True)
    down = shift(to_up, "lat", -1, False)
    up = shift(to_down, "lat", 1, False)
    edge_total = 3 * coarse_list.shape[1]
    c_edges, c_count = kernel_call(
        coarse_prep_body,
        (shaped((edge_total, 16), F32), shaped((1, 1), I32)),
        [SMEM, V, V, V],
        (place.astype(I32), coarse_list, list_next, list_far),
        [pltpu.VMEM((8, coarse_list.shape[1]), F32)],
        flops=mesh_flops,
        name="coarse_edges",
        out_specs=(V, SMEM),
    )
    mesh_one, proc_send, proc_recv = kernel_call(
        node_body,
        (shaped(mesh_rows, BF),) * 3,
        [
            V, V, V, V, V, part_of(mesh_state), square(0, 2), first_half(0, 0), first_half(0, 1), second_of(0),
            square(1, 0), square(1, 1), ANY,
        ],
        (
            own_sum, from_left, from_right, up, down, mesh_state, edge_square, node_first, node_first, node_second,
            edge_square, edge_square, c_edges,
        ),
        flops=7 * mesh_flops,
        moved=4 << 20,
        name="node",
    )
    quarter = four(proc_send[:COARSE_DEV], "lat", along_z)
    rows = kernel_call(four_body, shaped((4 * COARSE_DEV, WIDTH), BF), [V] * 4, quarter, name="join_z")
    quarter = four(rows, "lon", along_y)
    up, down, left, right = first_stage(proc_send)
    rows, pair = kernel_call(
        four_pair_body,
        (shaped((16 * COARSE_DEV, WIDTH), BF), shaped(pair_rows, BF)),
        [V] * 6,
        (*quarter, up, down),
        name="join_y",
    )
    quarter = four(rows, both, along_x)
    left_pair, right_pair = second_stage(pair)
    across = [lax.ppermute(part, "lon", [(i, i ^ 1) for i in range(LON)]) for part in quarter]
    fine = kernel_call(
        fine_body,
        shaped(mesh_rows, F32),
        [V] * 8 + [geom_of(1)],
        (m_edges, left, proc_send, right, pair, left_pair, right_pair, proc_recv, geom),
        [pltpu.VMEM((10 * MESH_NODES, WIDTH), BF)],
        flops=2 * grid_flops,
        moved=3 << 20,
        name="fine",
    )
    dec_send = kernel_call(
        mesh_body,
        shaped(mesh_rows, BF),
        [SMEM] + [V] * 12
        + [geom_of(1), square(1, 2), first_half(1, 0), first_half(1, 1), second_of(1), square(2, 0)],
        (
            c_count, fine, c_edges, *quarter, *across, proc_recv, mesh_one, geom,
            edge_square, node_first, node_first, node_second, edge_square,
        ),
        [pltpu.VMEM((128 * COARSE_DEV, WIDTH), BF), pltpu.VMEM(mesh_rows, F32)],
        flops=4 * grid_flops,
        moved=6 << 20,
        name="mesh",
    )
    up, down, left, right = first_stage(dec_send)
    pair = paired(up, down, dec_send)
    left_pair, right_pair = second_stage(pair)
    early = kernel_call(
        decode_early_body,
        shaped((GRID_DEGREE,) + grid_rows, F32),
        [V, V, V, V, V, V, geom_of(2)],
        (d_edges, left, dec_send, right, pair, grid_recv, geom),
        [pltpu.VMEM((6 * MESH_NODES, WIDTH), BF)],
        flops=4 * grid_flops,
        moved=8 << 20,
        name="early",
    )
    outputs = kernel_call(
        decode_body,
        shaped((head.shape[1], GRID_NODES), BF),
        [V, V, V, V, V, square(2, 2), first_half(2, 1), V],
        (d_edges, early, left_pair, right_pair, grid_base, edge_square, node_first, head.T),
        [pltpu.VMEM((4 * MESH_NODES, WIDTH), BF)],
        flops=5 * grid_flops,
        moved=8 << 20,
        name="decode",
    )
    return outputs.T[None, None]


def solution(mesh):
    return jax.shard_map(
        per_device,
        mesh=mesh,
        in_specs=(
            P("lat", "lon", None, None),
            P("lat", "lon", None, None),
            P(),
            P(),
            P(),
            P(),
            P(),
            P(),
            P(),
            P("lat", "lon", None),
            P("lat", "lon", None),
            P("lat", "lon"),
            P("lat", "lon", None, None),
            P("lat", "lon", None),
            P("lat", "lon", None, None),
            P("lat", "lon", None),
            P("lat", "lon", None),
            P("lat", "lon", None, None),
            P("lat", "lon", None),
            P("lat", "lon", None, None),
        ),
        out_specs=P("lat", "lon", None, None),
        check_vma=False,
    )
```

time: 190 us -> 163 us (0.86)
  local copies, waits for them, and re-layouts: 30.1 us -> 2.92 us
  waiting for transfers between devices: 45.7 us -> 30.6 us
  starting transfers between devices: 67.5 us -> 78.4 us
  Pallas kernels: 43.2 us -> 48.8 us
    unnamed x94 -> x11, local copies, waits for them, and re-layouts: 27.2 us -> 2.84 us
    ppermute x16 -> x24, waiting for transfers between devices: 38 us -> 21.9 us  [shift(): return lax.ppermute(value, axis, pairs)]
    ppermute x16 -> x24, starting transfers between devices: 45.5 us -> 59.7 us  [shift(): return lax.ppermute(value, axis, pairs)]
    pallas_call x11 -> x17, Pallas kernels: 43.2 us -> 48.8 us  [kernel_call(): pl.pallas_call(run, out_shape=outs, in_specs=[HBM if isinstance(q, Load)...]
    ppermute x10 -> x13, starting transfers between devices: 18.8 us -> 14.1 us  [the longest x9 13.1 us: four(): return [value] + [lax.ppermute(value, axis, pairs_of(s)) for s in (1, 2, 3)]]
    ppermute x10 -> x13, waiting for transfers between devices: 7.77 us -> 5.85 us  [the longest x9 5.84 us: four(): return [value] + [lax.ppermute(value, axis, pairs_of(s)) for s in (1, 2, 3)]]
  transfers between devices with their start and end apart: 28 -> 39, of which waited for: 14 -> 11; matrix products, arithmetic and copies ran while one was open for 4% -> 1% of each run, Pallas kernels for 8% -> 15%
where the time goes in v2:
time: 163 us; the launch traced here: 162 us
  starting transfers between devices  78.4 us (48%)
  Pallas kernels  48.8 us (30%)
  waiting for transfers between devices  30.6 us (19%)
  local copies, waits for them, and re-layouts  2.92 us (2%)
    ppermute x24, starting transfers between devices, shift(): return lax.ppermute(value, axis, pairs)  59.7 us
    pallas_call x17, Pallas kernels, kernel_call(): pl.pallas_call(run, out_shape=outs, in_specs=[HBM if isinstance(q, Load)...  48.8 us
    ppermute x24, waiting for transfers between devices, shift(): return lax.ppermute(value, axis, pairs)  21.9 us
    ppermute x9, starting transfers between devices, four(): return [value] + [lax.ppermute(value, axis, pairs_of(s)) for s in (1, 2, 3)]  13.1 us
    ppermute x9, waiting for transfers between devices, four(): return [value] + [lax.ppermute(value, axis, pairs_of(s)) for s in (1, 2, 3)]  5.84 us
    ppermute x1, starting transfers between devices, per_device(): lax.ppermute(coarse_list, both, [(t, (t + tiles // 2) % tiles) for t in r...  4.55 us
  transfers between devices with their start and end apart: 39, of which 11 were waited for; matrix products, arithmetic and copies ran while one was open for 1% of the time, Pallas kernels for 15%

profile of v2, /device:TPU:4, one launch (start us, length us, event | category | flops | bytes accessed | tf_op | source)
XLA Modules:
  0.0 162.0 jit_solution(13317696191383903812)
XLA Ops:
  1.8 3.8 %collective-permute-start.4 = (bf16[192,512]{1,0:T(8,128)(2,1)S(1)}, bf16[192,512]{1,0:T(8,128)(2,1)S(1)}, u32[]{:S(2)}, u32[]{:S(2)}) collective-permute-start(bf16[192,512]{1,0:T(8,128)(2,1)S(1)} %get-tuple-element.32.refs_0_), channel_id=1, source_target_pairs={{0,16},{16,32},{32,48},{48,64},{64,80},{80,96},{96,112},{1,17},{17... | collective-permute-start | bytes 589832 | tf_op jit(solution)/shard_map/ppermute | solution.py:488
  5.5 3.6 %collective-permute-start.5 = (bf16[192,512]{1,0:T(8,128)(2,1)S(1)}, bf16[192,512]{1,0:T(8,128)(2,1)S(1)}, u32[]{:S(2)}, u32[]{:S(2)}) collective-permute-start(bf16[192,512]{1,0:T(8,128)(2,1)S(1)} %get-tuple-element.32.refs_0_), channel_id=1, source_target_pairs={{16,0},{32,16},{48,32},{64,48},{80,64},{96,80},{112,96},{17,1},{33... | collective-permute-start | bytes 589832 | tf_op jit(solution)/shard_map/ppermute | solution.py:488
  10.6 3.8 %embed.1 = (bf16[1024,512]{1,0:T(8,128)(2,1)S(1)}, bf16[1024,512]{1,0:T(8,128)(2,1)S(1)}) custom-call(bf16[1024,474]{1,0:T(8,128)(2,1)S(1)} %bitcast.11, bf16[474,512]{1,0:T(8,128)(2,1)} %refs_1_.6, bf16[512,512]{1,0:T(8,128)(2,1)} %refs_2_.7, bf16[3,3,512,512]{3,2,1,0:T(8,128)(2,1)} %refs_5_.5), custom_call_target="tpu_custom_call" | custom-call | flops 1610612736 | bytes 5242880 | tf_op jit(solution)/shard_map/embed/pallas_call | solution.py:126
  14.4 2.9 %collective-permute-done.5.refs_1_ = bf16[192,512]{1,0:T(8,128)(2,1)S(1)} collective-permute-done((bf16[192,512]{1,0:T(8,128)(2,1)S(1)}, bf16[192,512]{1,0:T(8,128)(2,1)S(1)}, u32[]{:S(2)}, u32[]{:S(2)}) %collective-permute-start.5) | collective-permute-done | bytes 196640 | tf_op jit(solution)/shard_map/ppermute | solution.py:488
  17.5 3.8 %collective-permute-start.7 = (bf16[2,192,512]{2,1,0:T(8,128)(2,1)S(1)}, bf16[2,192,512]{2,1,0:T(8,128)(2,1)S(1)}, u32[]{:S(2)}, u32[]{:S(2)}) collective-permute-start(bf16[2,192,512]{2,1,0:T(8,128)(2,1)S(1)} %pair.2.refs_2_), channel_id=1, source_target_pairs={{0,15},{1,0},{2,1},{3,2},{4,3},{5,4},{6,5},{7,6},{8,7},{9,8},{10,9... | collective-permute-start | bytes 1179656 | tf_op jit(solution)/shard_map/ppermute | solution.py:488
  21.3 3.9 %collective-permute-start.3 = (bf16[192,512]{1,0:T(8,128)(2,1)S(1)}, bf16[192,512]{1,0:T(8,128)(2,1)S(1)}, u32[]{:S(2)}, u32[]{:S(2)}) collective-permute-start(bf16[192,512]{1,0:T(8,128)(2,1)S(1)} %get-tuple-element.32.refs_0_), channel_id=1, source_target_pairs={{0,15},{1,0},{2,1},{3,2},{4,3},{5,4},{6,5},{7,6},{8,7},{9,8},{10,9... | collective-permute-start | bytes 589832 | tf_op jit(solution)/shard_map/ppermute | solution.py:488
  26.9 8.3 %own.1.refs_8_.refs_0_ = f32[128,512]{1,0:T(8,128)S(1)} custom-call(bf16[192,512]{1,0:T(8,128)(2,1)S(1)} %get-tuple-element.32.refs_0_, bf16[1024,512]{1,0:T(8,128)(2,1)S(1)} %get-tuple-element.33.refs_1_.refs_2_.refs_5_, bf16[3,3,512,512]{3,2,1,0:T(8,128)(2,1)} %refs_5_.5, bf16[3,16,512]{2,1,0:T(8,128)(2,1)S(1)} %get-tuple-element.34.refs_3_.refs_7_.refs_8_.refs_13_.refs_6_), custom_call_target="tpu_custom_call" | custom-call | flops 2684354560 | bytes 3145728 | tf_op jit(solution)/shard_map/own/pallas_call | solution.py:126
  35.2 8.2 %near.1 = (bf16[128,512]{1,0:T(8,128)(2,1)}, bf16[128,512]{1,0:T(8,128)(2,1)}, bf16[2,128,512]{2,1,0:T(8,128)(2,1)S(1)}, bf16[2,128,512]{2,1,0:T(8,128)(2,1)S(1)}, bf16[2,128,512]{2,1,0:T(8,128)(2,1)S(1)}) custom-call(bf16[192,512]{1,0:T(8,128)(2,1)S(1)} %collective-permute-done.2.refs_0_, bf16[192,512]{1,0:T(8,128)(2,1)S(1)} %collective-permute-done.3.refs_1_, ...), custom_call_target="tpu_custom_call" | custom-call | flops 2147483648 | bytes 5242880 | tf_op jit(solution)/shard_map/near/pallas_call | solution.py:126
  43.5 3.8 %collective-permute-start.11 = (bf16[2,128,512]{2,1,0:T(8,128)(2,1)S(1)}, bf16[2,128,512]{2,1,0:T(8,128)(2,1)S(1)}, u32[]{:S(2)}, u32[]{:S(2)}) collective-permute-start(bf16[2,128,512]{2,1,0:T(8,128)(2,1)S(1)} %get-tuple-element.39), channel_id=1, source_target_pairs={{0,15},{1,0},{2,1},{3,2},{4,3},{5,4},{6,5},{7,6},{8,7},{9,8},{10,9... | collective-permute-start | bytes 786440 | tf_op jit(solution)/shard_map/ppermute | solution.py:488
  47.3 2.5 %grid.1 = (bf16[1024,512]{1,0:T(8,128)(2,1)S(1)}, f32[1024,512]{1,0:T(8,128)S(1)}) custom-call(bf16[1024,512]{1,0:T(8,128)(2,1)S(1)} %get-tuple-element.40.refs_0_, bf16[3,3,512,512]{3,2,1,0:T(8,128)(2,1)} %refs_5_.5, bf16[3,1024,512]{2,1,0:T(8,128)(2,1)} %refs_6_.7), custom_call_target="tpu_custom_call" | custom-call | flops 1073741824 | bytes 5242880 | tf_op jit(solution)/shard_map/grid/pallas_call | solution.py:126
  51.2 3.9 %collective-permute-start.9 = (bf16[128,512]{1,0:T(8,128)(2,1)}, bf16[128,512]{1,0:T(8,128)(2,1)S(1)}, u32[]{:S(2)}, u32[]{:S(2)}) collective-permute-start(bf16[128,512]{1,0:T(8,128)(2,1)} %get-tuple-element.36), channel_id=1, source_target_pairs={{0,15},{1,0},{2,1},{3,2},{4,3},{5,4},{6,5},{7,6},{8,7},{9,8},{10,9... | collective-permute-start | bytes 393224 | tf_op jit(solution)/shard_map/ppermute | solution.py:488
  55.8 3.7 %collective-permute-start.12 = (bf16[128,512]{1,0:T(8,128)(2,1)}, bf16[128,512]{1,0:T(8,128)(2,1)S(1)}, u32[]{:S(2)}, u32[]{:S(2)}) collective-permute-start(bf16[128,512]{1,0:T(8,128)(2,1)} %get-tuple-element.42), channel_id=1, source_target_pairs={{0,16},{16,32},{32,48},{48,64},{64,80},{80,96},{96,112},{1,17},{17... | collective-permute-start | bytes 393224 | tf_op jit(solution)/shard_map/ppermute | solution.py:488
  59.5 3.6 %collective-permute-start.13 = (bf16[128,512]{1,0:T(8,128)(2,1)}, bf16[128,512]{1,0:T(8,128)(2,1)S(1)}, u32[]{:S(2)}, u32[]{:S(2)}) collective-permute-start(bf16[128,512]{1,0:T(8,128)(2,1)} %get-tuple-element.43), channel_id=1, source_target_pairs={{16,0},{32,16},{48,32},{64,48},{80,64},{96,80},{112,96},{17,1},{33... | collective-permute-start | bytes 393224 | tf_op jit(solution)/shard_map/ppermute | solution.py:488
  64.6 4.5 %collective-permute-start.1 = (bf16[16,256]{1,0:T(8,128)(2,1)S(1)}, bf16[16,256]{1,0:T(8,128)(2,1)S(1)}, u32[]{:S(2)}, u32[]{:S(2)}) collective-permute-start(bf16[16,256]{1,0:T(8,128)(2,1)S(1)} %get-tuple-element.29.refs_1_), channel_id=1, source_target_pairs={{0,64},{1,65},{2,66},{3,67},{4,68},{5,69},{6,70},{7,71},{8,72},{9,... | collective-permute-start | bytes 24584 | tf_op jit(solution)/shard_map/ppermute | solution.py:635
  72.5 2.9 %node.1 = (bf16[128,512]{1,0:T(8,128)(2,1)S(1)}, bf16[128,512]{1,0:T(8,128)(2,1)S(1)}, bf16[128,512]{1,0:T(8,128)(2,1)S(1)}) custom-call(f32[128,512]{1,0:T(8,128)S(1)} %own.1.refs_8_.refs_0_, bf16[128,512]{1,0:T(8,128)(2,1)S(1)} %collective-permute-done.8.refs_1_, bf16[128,512]{1,0:T(8,128)(2,1)S(1)} %collective-permute-done.9.refs_2_, ...), custom_call_target="tpu_custom_call" | custom-call | flops 469762048 | bytes 4194304 | tf_op jit(solution)/shard_map/node/pallas_call | solution.py:126
  77.4 2.7 %collective-permute-start.17 = (bf16[16,512]{1,0:T(8,128)(2,1)S(1)}, bf16[16,512]{1,0:T(8,128)(2,1)S(1)}, u32[]{:S(2)}, u32[]{:S(2)}) collective-permute-start(bf16[16,512]{1,0:T(8,128)(2,1)S(1)} %slice.3.refs_0_), channel_id=1, source_target_pairs={{0,64},{16,80},{32,96},{48,112},{64,0},{80,16},{96,32},{112,48},{1... | collective-permute-start | bytes 49160 | tf_op jit(solution)/shard_map/ppermute | solution.py:521
  83.8 3.8 %collective-permute-start.22 = (bf16[128,512]{1,0:T(8,128)(2,1)S(1)}, bf16[128,512]{1,0:T(8,128)(2,1)S(1)}, u32[]{:S(2)}, u32[]{:S(2)}) collective-permute-start(bf16[128,512]{1,0:T(8,128)(2,1)S(1)} %get-tuple-element.45.refs_2_), channel_id=1, source_target_pairs={{0,16},{16,32},{32,48},{48,64},{64,80},{80,96},{96,112},{1,17},{17... | collective-permute-start | bytes 393224 | tf_op jit(solution)/shard_map/ppermute | solution.py:488
  87.7 3.5 %collective-permute-start.23 = (bf16[128,512]{1,0:T(8,128)(2,1)S(1)}, bf16[128,512]{1,0:T(8,128)(2,1)S(1)}, u32[]{:S(2)}, u32[]{:S(2)}) collective-permute-start(bf16[128,512]{1,0:T(8,128)(2,1)S(1)} %get-tuple-element.45.refs_2_), channel_id=1, source_target_pairs={{16,0},{32,16},{48,32},{64,48},{80,64},{96,80},{112,96},{17,1},{33... | collective-permute-start | bytes 393224 | tf_op jit(solution)/shard_map/ppermute | solution.py:488
  91.5 3.2 %collective-permute-start.21 = (bf16[64,512]{1,0:T(8,128)(2,1)S(1)}, bf16[64,512]{1,0:T(8,128)(2,1)S(1)}, u32[]{:S(2)}, u32[]{:S(2)}) collective-permute-start(bf16[64,512]{1,0:T(8,128)(2,1)S(1)} %join_z.1.refs_0_), channel_id=1, source_target_pairs={{0,12},{1,13},{2,14},{3,15},{4,0},{5,1},{6,2},{7,3},{8,4},{9,5},{1... | collective-permute-start | bytes 196616 | tf_op jit(solution)/shard_map/ppermute | solution.py:521
  94.7 3.2 %collective-permute-done.20.refs_2_ = bf16[64,512]{1,0:T(8,128)(2,1)S(1)} collective-permute-done((bf16[64,512]{1,0:T(8,128)(2,1)S(1)}, bf16[64,512]{1,0:T(8,128)(2,1)S(1)}, u32[]{:S(2)}, u32[]{:S(2)}) %collective-permute-start.20) | collective-permute-done | bytes 65568 | tf_op jit(solution)/shard_map/ppermute | solution.py:521
  102.0 2.7 %collective-permute-start.15 = (bf16[128,512]{1,0:T(8,128)(2,1)S(1)}, bf16[128,512]{1,0:T(8,128)(2,1)S(1)}, u32[]{:S(2)}, u32[]{:S(2)}) collective-permute-start(bf16[128,512]{1,0:T(8,128)(2,1)S(1)} %get-tuple-element.45.refs_2_), channel_id=1, source_target_pairs={{0,15},{1,0},{2,1},{3,2},{4,3},{5,4},{6,5},{7,6},{8,7},{9,8},{10,9... | collective-permute-start | bytes 393224 | tf_op jit(solution)/shard_map/ppermute | solution.py:488
  104.7 10.9 %collective-permute-done.15.refs_3_ = bf16[128,512]{1,0:T(8,128)(2,1)S(1)} collective-permute-done((bf16[128,512]{1,0:T(8,128)(2,1)S(1)}, bf16[128,512]{1,0:T(8,128)(2,1)S(1)}, u32[]{:S(2)}, u32[]{:S(2)}) %collective-permute-start.15) | collective-permute-done | bytes 131104 | tf_op jit(solution)/shard_map/ppermute | solution.py:488
  115.6 4.0 %collective-permute-start.25 = (bf16[2,128,512]{2,1,0:T(8,128)(2,1)S(1)}, bf16[2,128,512]{2,1,0:T(8,128)(2,1)S(1)}, u32[]{:S(2)}, u32[]{:S(2)}) collective-permute-start(bf16[2,128,512]{2,1,0:T(8,128)(2,1)S(1)} %get-tuple-element.46.refs_4_), channel_id=1, source_target_pairs={{0,15},{1,0},{2,1},{3,2},{4,3},{5,4},{6,5},{7,6},{8,7},{9,8},{10,9... | collective-permute-start | bytes 786440 | tf_op jit(solution)/shard_map/ppermute | solution.py:488
  120.7 2.9 %collective-permute-done.25.refs_6_ = bf16[2,128,512]{2,1,0:T(8,128)(2,1)S(1)} collective-permute-done((bf16[2,128,512]{2,1,0:T(8,128)(2,1)S(1)}, bf16[2,128,512]{2,1,0:T(8,128)(2,1)S(1)}, u32[]{:S(2)}, u32[]{:S(2)}) %collective-permute-start.25) | collective-permute-done | bytes 262176 | tf_op jit(solution)/shard_map/ppermute | solution.py:488
  125.4 3.6 %mesh.1.refs_2_ = bf16[128,512]{1,0:T(8,128)(2,1)S(1)} custom-call(s32[1,1]{1,0:T(1,128)} %get-tuple-element.30.refs_0_, f32[128,512]{1,0:T(8,128)S(1)} %fine.1.refs_1_, f32[768,16]{1,0:T(8,128)S(1)} %get-tuple-element.44.refs_12_.refs_2_, bf16[256,512]{1,0:T(8,128)(2,1)S(1)} %get-tuple-element.48.refs_3_, ...), custom_call_target="tpu_custom_call" | custom-call | flops 2147483648 | bytes 6291456 | tf_op jit(solution)/shard_map/mesh/pallas_call | solution.py:126
  128.9 3.4 %collective-permute-start.35 = (bf16[128,512]{1,0:T(8,128)(2,1)S(1)}, bf16[128,512]{1,0:T(8,128)(2,1)S(1)}, u32[]{:S(2)}, u32[]{:S(2)}) collective-permute-start(bf16[128,512]{1,0:T(8,128)(2,1)S(1)} %mesh.1.refs_2_), channel_id=1, source_target_pairs={{0,16},{16,32},{32,48},{48,64},{64,80},{80,96},{96,112},{1,17},{17... | collective-permute-start | bytes 393224 | tf_op jit(solution)/shard_map/ppermute | solution.py:488
  132.3 4.0 %collective-permute-start.36 = (bf16[128,512]{1,0:T(8,128)(2,1)S(1)}, bf16[128,512]{1,0:T(8,128)(2,1)S(1)}, u32[]{:S(2)}, u32[]{:S(2)}) collective-permute-start(bf16[128,512]{1,0:T(8,128)(2,1)S(1)} %mesh.1.refs_2_), channel_id=1, source_target_pairs={{16,0},{32,16},{48,32},{64,48},{80,64},{96,80},{112,96},{17,1},{33... | collective-permute-start | bytes 393224 | tf_op jit(solution)/shard_map/ppermute | solution.py:488
  136.4 3.8 %collective-permute-start.34 = (bf16[128,512]{1,0:T(8,128)(2,1)S(1)}, bf16[128,512]{1,0:T(8,128)(2,1)S(1)}, u32[]{:S(2)}, u32[]{:S(2)}) collective-permute-start(bf16[128,512]{1,0:T(8,128)(2,1)S(1)} %mesh.1.refs_2_), channel_id=1, source_target_pairs={{0,15},{1,0},{2,1},{3,2},{4,3},{5,4},{6,5},{7,6},{8,7},{9,8},{10,9... | collective-permute-start | bytes 393224 | tf_op jit(solution)/shard_map/ppermute | solution.py:488
  140.2 2.8 %collective-permute-done.36.refs_1_ = bf16[128,512]{1,0:T(8,128)(2,1)S(1)} collective-permute-done((bf16[128,512]{1,0:T(8,128)(2,1)S(1)}, bf16[128,512]{1,0:T(8,128)(2,1)S(1)}, u32[]{:S(2)}, u32[]{:S(2)}) %collective-permute-start.36) | collective-permute-done | bytes 131104 | tf_op jit(solution)/shard_map/ppermute | solution.py:488
  143.1 3.8 %collective-permute-start.38 = (bf16[2,128,512]{2,1,0:T(8,128)(2,1)S(1)}, bf16[2,128,512]{2,1,0:T(8,128)(2,1)S(1)}, u32[]{:S(2)}, u32[]{:S(2)}) collective-permute-start(bf16[2,128,512]{2,1,0:T(8,128)(2,1)S(1)} %pair.3.refs_4_), channel_id=1, source_target_pairs={{0,15},{1,0},{2,1},{3,2},{4,3},{5,4},{6,5},{7,6},{8,7},{9,8},{10,9... | collective-permute-start | bytes 786440 | tf_op jit(solution)/shard_map/ppermute | solution.py:488
  147.0 4.5 %early.1.refs_1_ = f32[3,1024,512]{2,1,0:T(8,128)S(1)} custom-call(f32[3,1024,16]{2,1,0:T(8,128)S(1)} %get-tuple-element.28.refs_0_, bf16[128,512]{1,0:T(8,128)(2,1)S(1)} %collective-permute-done.33.refs_1_, bf16[128,512]{1,0:T(8,128)(2,1)S(1)} %mesh.1.refs_2_, bf16[128,512]{1,0:T(8,128)(2,1)S(1)} %collective-permute-done.34.refs_3_, ...), custom_call_target="tpu_custom_call" | custom-call | flops 2147483648 | bytes 8388608 | tf_op jit(solution)/shard_map/early/pallas_call | solution.py:126
  153.8 8.0 %decode.1 = bf16[227,1024]{1,0:T(8,128)(2,1)} custom-call(f32[3,1024,16]{2,1,0:T(8,128)S(1)} %get-tuple-element.28.refs_0_, f32[3,1024,512]{2,1,0:T(8,128)S(1)} %early.1.refs_1_, bf16[2,128,512]{2,1,0:T(8,128)(2,1)S(1)} %collective-permute-done.37.refs_2_, bf16[2,128,512]{2,1,0:T(8,128)(2,1)S(1)} %collective-permute-done.38.refs_3_, ...), custom_call_target="tpu_custom_call" | custom-call | flops 2684354560 | bytes 8388608 | tf_op jit(solution)/shard_map/decode/pallas_call | solution.py:126
  (76 shorter events, 26.8 us)
Async XLA Ops:
  1.8 12.7 %collective-permute-start.4 = (bf16[192,512]{1,0:T(8,128)(2,1)S(1)}, bf16[192,512]{1,0:T(8,128)(2,1)S(1)}, u32[]{:S(2)}, u32[]{:S(2)}) collective-permute-start(bf16[192,512]{1,0:T(8,128)(2,1)S(1)} %get-tuple-element.32.refs_0_), channel_id=1, source_target_pairs={{0,16},{16,32},{32,48},{48,64},{64,80},{80,96},{96,112},{1,17},{17... | collective-permute-start | bytes 589832 | tf_op jit(solution)/shard_map/ppermute | solution.py:488
  5.5 11.8 %collective-permute-start.5 = (bf16[192,512]{1,0:T(8,128)(2,1)S(1)}, bf16[192,512]{1,0:T(8,128)(2,1)S(1)}, u32[]{:S(2)}, u32[]{:S(2)}) collective-permute-start(bf16[192,512]{1,0:T(8,128)(2,1)S(1)} %get-tuple-element.32.refs_0_), channel_id=1, source_target_pairs={{16,0},{32,16},{48,32},{64,48},{80,64},{96,80},{112,96},{17,1},{33... | collective-permute-start | bytes 589832 | tf_op jit(solution)/shard_map/ppermute | solution.py:488
  17.4 17.8 %collective-permute-start.6 = (bf16[2,192,512]{2,1,0:T(8,128)(2,1)S(1)}, bf16[2,192,512]{2,1,0:T(8,128)(2,1)S(1)}, u32[]{:S(2)}, u32[]{:S(2)}) collective-permute-start(bf16[2,192,512]{2,1,0:T(8,128)(2,1)S(1)} %pair.2.refs_2_), channel_id=1, source_target_pairs={{0,1},{1,2},{2,3},{3,4},{4,5},{5,6},{6,7},{7,8},{8,9},{9,10},{10,1... | collective-permute-start | bytes 1179656 | tf_op jit(solution)/shard_map/ppermute | solution.py:488
  17.5 17.7 %collective-permute-start.7 = (bf16[2,192,512]{2,1,0:T(8,128)(2,1)S(1)}, bf16[2,192,512]{2,1,0:T(8,128)(2,1)S(1)}, u32[]{:S(2)}, u32[]{:S(2)}) collective-permute-start(bf16[2,192,512]{2,1,0:T(8,128)(2,1)S(1)} %pair.2.refs_2_), channel_id=1, source_target_pairs={{0,15},{1,0},{2,1},{3,2},{4,3},{5,4},{6,5},{7,6},{8,7},{9,8},{10,9... | collective-permute-start | bytes 1179656 | tf_op jit(solution)/shard_map/ppermute | solution.py:488
  21.3 13.8 %collective-permute-start.2 = (bf16[192,512]{1,0:T(8,128)(2,1)S(1)}, bf16[192,512]{1,0:T(8,128)(2,1)S(1)}, u32[]{:S(2)}, u32[]{:S(2)}) collective-permute-start(bf16[192,512]{1,0:T(8,128)(2,1)S(1)} %get-tuple-element.32.refs_0_), channel_id=1, source_target_pairs={{0,1},{1,2},{2,3},{3,4},{4,5},{5,6},{6,7},{7,8},{8,9},{9,10},{10,1... | collective-permute-start | bytes 589832 | tf_op jit(solution)/shard_map/ppermute | solution.py:488
  21.3 13.8 %collective-permute-start.3 = (bf16[192,512]{1,0:T(8,128)(2,1)S(1)}, bf16[192,512]{1,0:T(8,128)(2,1)S(1)}, u32[]{:S(2)}, u32[]{:S(2)}) collective-permute-start(bf16[192,512]{1,0:T(8,128)(2,1)S(1)} %get-tuple-element.32.refs_0_), channel_id=1, source_target_pairs={{0,15},{1,0},{2,1},{3,2},{4,3},{5,4},{6,5},{7,6},{8,7},{9,8},{10,9... | collective-permute-start | bytes 589832 | tf_op jit(solution)/shard_map/ppermute | solution.py:488
  43.4 11.6 %collective-permute-start.10 = (bf16[2,128,512]{2,1,0:T(8,128)(2,1)S(1)}, bf16[2,128,512]{2,1,0:T(8,128)(2,1)S(1)}, u32[]{:S(2)}, u32[]{:S(2)}) collective-permute-start(bf16[2,128,512]{2,1,0:T(8,128)(2,1)S(1)} %get-tuple-element.38), channel_id=1, source_target_pairs={{0,1},{1,2},{2,3},{3,4},{4,5},{5,6},{6,7},{7,8},{8,9},{9,10},{10,1... | collective-permute-start | bytes 786440 | tf_op jit(solution)/shard_map/ppermute | solution.py:488
  43.5 11.5 %collective-permute-start.11 = (bf16[2,128,512]{2,1,0:T(8,128)(2,1)S(1)}, bf16[2,128,512]{2,1,0:T(8,128)(2,1)S(1)}, u32[]{:S(2)}, u32[]{:S(2)}) collective-permute-start(bf16[2,128,512]{2,1,0:T(8,128)(2,1)S(1)} %get-tuple-element.39), channel_id=1, source_target_pairs={{0,15},{1,0},{2,1},{3,2},{4,3},{5,4},{6,5},{7,6},{8,7},{9,8},{10,9... | collective-permute-start | bytes 786440 | tf_op jit(solution)/shard_map/ppermute | solution.py:488
  51.2 21.3 %collective-permute-start.8 = (bf16[128,512]{1,0:T(8,128)(2,1)}, bf16[128,512]{1,0:T(8,128)(2,1)S(1)}, u32[]{:S(2)}, u32[]{:S(2)}) collective-permute-start(bf16[128,512]{1,0:T(8,128)(2,1)} %get-tuple-element.35), channel_id=1, source_target_pairs={{0,1},{1,2},{2,3},{3,4},{4,5},{5,6},{6,7},{7,8},{8,9},{9,10},{10,1... | collective-permute-start | bytes 393224 | tf_op jit(solution)/shard_map/ppermute | solution.py:488
  51.2 21.3 %collective-permute-start.9 = (bf16[128,512]{1,0:T(8,128)(2,1)}, bf16[128,512]{1,0:T(8,128)(2,1)S(1)}, u32[]{:S(2)}, u32[]{:S(2)}) collective-permute-start(bf16[128,512]{1,0:T(8,128)(2,1)} %get-tuple-element.36), channel_id=1, source_target_pairs={{0,15},{1,0},{2,1},{3,2},{4,3},{5,4},{6,5},{7,6},{8,7},{9,8},{10,9... | collective-permute-start | bytes 393224 | tf_op jit(solution)/shard_map/ppermute | solution.py:488
  55.8 16.7 %collective-permute-start.12 = (bf16[128,512]{1,0:T(8,128)(2,1)}, bf16[128,512]{1,0:T(8,128)(2,1)S(1)}, u32[]{:S(2)}, u32[]{:S(2)}) collective-permute-start(bf16[128,512]{1,0:T(8,128)(2,1)} %get-tuple-element.42), channel_id=1, source_target_pairs={{0,16},{16,32},{32,48},{48,64},{64,80},{80,96},{96,112},{1,17},{17... | collective-permute-start | bytes 393224 | tf_op jit(solution)/shard_map/ppermute | solution.py:488
  59.5 13.0 %collective-permute-start.13 = (bf16[128,512]{1,0:T(8,128)(2,1)}, bf16[128,512]{1,0:T(8,128)(2,1)S(1)}, u32[]{:S(2)}, u32[]{:S(2)}) collective-permute-start(bf16[128,512]{1,0:T(8,128)(2,1)} %get-tuple-element.43), channel_id=1, source_target_pairs={{16,0},{32,16},{48,32},{64,48},{80,64},{96,80},{112,96},{17,1},{33... | collective-permute-start | bytes 393224 | tf_op jit(solution)/shard_map/ppermute | solution.py:488
  64.6 6.2 %collective-permute-start.1 = (bf16[16,256]{1,0:T(8,128)(2,1)S(1)}, bf16[16,256]{1,0:T(8,128)(2,1)S(1)}, u32[]{:S(2)}, u32[]{:S(2)}) collective-permute-start(bf16[16,256]{1,0:T(8,128)(2,1)S(1)} %get-tuple-element.29.refs_1_), channel_id=1, source_target_pairs={{0,64},{1,65},{2,66},{3,67},{4,68},{5,69},{6,70},{7,71},{8,72},{9,... | collective-permute-start | bytes 24584 | tf_op jit(solution)/shard_map/ppermute | solution.py:635
  75.5 6.2 %collective-permute-start.16 = (bf16[16,512]{1,0:T(8,128)(2,1)S(1)}, bf16[16,512]{1,0:T(8,128)(2,1)S(1)}, u32[]{:S(2)}, u32[]{:S(2)}) collective-permute-start(bf16[16,512]{1,0:T(8,128)(2,1)S(1)} %slice.3.refs_0_), channel_id=1, source_target_pairs={{0,32},{16,48},{32,64},{48,80},{64,96},{80,112},{96,0},{112,16},{1... | collective-permute-start | bytes 49160 | tf_op jit(solution)/shard_map/ppermute | solution.py:521
  83.8 7.7 %collective-permute-start.19 = (bf16[64,512]{1,0:T(8,128)(2,1)S(1)}, bf16[64,512]{1,0:T(8,128)(2,1)S(1)}, u32[]{:S(2)}, u32[]{:S(2)}) collective-permute-start(bf16[64,512]{1,0:T(8,128)(2,1)S(1)} %join_z.1.refs_0_), channel_id=1, source_target_pairs={{0,4},{1,5},{2,6},{3,7},{4,8},{5,9},{6,10},{7,11},{8,12},{9,13},{1... | collective-permute-start | bytes 196616 | tf_op jit(solution)/shard_map/ppermute | solution.py:521
  83.8 14.5 %collective-permute-start.22 = (bf16[128,512]{1,0:T(8,128)(2,1)S(1)}, bf16[128,512]{1,0:T(8,128)(2,1)S(1)}, u32[]{:S(2)}, u32[]{:S(2)}) collective-permute-start(bf16[128,512]{1,0:T(8,128)(2,1)S(1)} %get-tuple-element.45.refs_2_), channel_id=1, source_target_pairs={{0,16},{16,32},{32,48},{48,64},{64,80},{80,96},{96,112},{1,17},{17... | collective-permute-start | bytes 393224 | tf_op jit(solution)/shard_map/ppermute | solution.py:488
  87.7 10.7 %collective-permute-start.23 = (bf16[128,512]{1,0:T(8,128)(2,1)S(1)}, bf16[128,512]{1,0:T(8,128)(2,1)S(1)}, u32[]{:S(2)}, u32[]{:S(2)}) collective-permute-start(bf16[128,512]{1,0:T(8,128)(2,1)S(1)} %get-tuple-element.45.refs_2_), channel_id=1, source_target_pairs={{16,0},{32,16},{48,32},{64,48},{80,64},{96,80},{112,96},{17,1},{33... | collective-permute-start | bytes 393224 | tf_op jit(solution)/shard_map/ppermute | solution.py:488
  91.2 10.8 %collective-permute-start.14 = (bf16[128,512]{1,0:T(8,128)(2,1)S(1)}, bf16[128,512]{1,0:T(8,128)(2,1)S(1)}, u32[]{:S(2)}, u32[]{:S(2)}) collective-permute-start(bf16[128,512]{1,0:T(8,128)(2,1)S(1)} %get-tuple-element.45.refs_2_), channel_id=1, source_target_pairs={{0,1},{1,2},{2,3},{3,4},{4,5},{5,6},{6,7},{7,8},{8,9},{9,10},{10,1... | collective-permute-start | bytes 393224 | tf_op jit(solution)/shard_map/ppermute | solution.py:488
  91.3 6.5 %collective-permute-start.20 = (bf16[64,512]{1,0:T(8,128)(2,1)S(1)}, bf16[64,512]{1,0:T(8,128)(2,1)S(1)}, u32[]{:S(2)}, u32[]{:S(2)}) collective-permute-start(bf16[64,512]{1,0:T(8,128)(2,1)S(1)} %join_z.1.refs_0_), channel_id=1, source_target_pairs={{0,8},{1,9},{2,10},{3,11},{4,12},{5,13},{6,14},{7,15},{8,0},{9,1},... | collective-permute-start | bytes 196616 | tf_op jit(solution)/shard_map/ppermute | solution.py:521
  91.5 6.9 %collective-permute-start.21 = (bf16[64,512]{1,0:T(8,128)(2,1)S(1)}, bf16[64,512]{1,0:T(8,128)(2,1)S(1)}, u32[]{:S(2)}, u32[]{:S(2)}) collective-permute-start(bf16[64,512]{1,0:T(8,128)(2,1)S(1)} %join_z.1.refs_0_), channel_id=1, source_target_pairs={{0,12},{1,13},{2,14},{3,15},{4,0},{5,1},{6,2},{7,3},{8,4},{9,5},{1... | collective-permute-start | bytes 196616 | tf_op jit(solution)/shard_map/ppermute | solution.py:521
  98.4 21.2 %collective-permute-start.24 = (bf16[2,128,512]{2,1,0:T(8,128)(2,1)S(1)}, bf16[2,128,512]{2,1,0:T(8,128)(2,1)S(1)}, u32[]{:S(2)}, u32[]{:S(2)}) collective-permute-start(bf16[2,128,512]{2,1,0:T(8,128)(2,1)S(1)} %get-tuple-element.46.refs_4_), channel_id=1, source_target_pairs={{0,1},{1,2},{2,3},{3,4},{4,5},{5,6},{6,7},{7,8},{8,9},{9,10},{10,1... | collective-permute-start | bytes 786440 | tf_op jit(solution)/shard_map/ppermute | solution.py:488
  98.5 21.2 %collective-permute-start.26 = (bf16[256,512]{1,0:T(8,128)(2,1)S(1)}, bf16[256,512]{1,0:T(8,128)(2,1)S(1)}, u32[]{:S(2)}, u32[]{:S(2)}) collective-permute-start(bf16[256,512]{1,0:T(8,128)(2,1)S(1)} %get-tuple-element.48.refs_3_), channel_id=1, source_target_pairs={{0,2},{1,3},{2,16},{3,17},{4,6},{5,7},{6,20},{7,21},{8,10},{9,11},... | collective-permute-start | bytes 786440 | tf_op jit(solution)/shard_map/ppermute | solution.py:521
  100.5 19.7 %collective-permute-start.27 = (bf16[256,512]{1,0:T(8,128)(2,1)S(1)}, bf16[256,512]{1,0:T(8,128)(2,1)S(1)}, u32[]{:S(2)}, u32[]{:S(2)}) collective-permute-start(bf16[256,512]{1,0:T(8,128)(2,1)S(1)} %get-tuple-element.48.refs_3_), channel_id=1, source_target_pairs={{0,16},{1,17},{2,18},{3,19},{4,20},{5,21},{6,22},{7,23},{8,24},{9,... | collective-permute-start | bytes 786440 | tf_op jit(solution)/shard_map/ppermute | solution.py:521
  100.5 19.7 %collective-permute-start.28 = (bf16[256,512]{1,0:T(8,128)(2,1)S(1)}, bf16[256,512]{1,0:T(8,128)(2,1)S(1)}, u32[]{:S(2)}, u32[]{:S(2)}) collective-permute-start(bf16[256,512]{1,0:T(8,128)(2,1)S(1)} %get-tuple-element.48.refs_3_), channel_id=1, source_target_pairs={{0,18},{1,19},{2,0},{3,1},{4,22},{5,23},{6,4},{7,5},{8,26},{9,27},... | collective-permute-start | bytes 786440 | tf_op jit(solution)/shard_map/ppermute | solution.py:521
  102.0 13.7 %collective-permute-start.15 = (bf16[128,512]{1,0:T(8,128)(2,1)S(1)}, bf16[128,512]{1,0:T(8,128)(2,1)S(1)}, u32[]{:S(2)}, u32[]{:S(2)}) collective-permute-start(bf16[128,512]{1,0:T(8,128)(2,1)S(1)} %get-tuple-element.45.refs_2_), channel_id=1, source_target_pairs={{0,15},{1,0},{2,1},{3,2},{4,3},{5,4},{6,5},{7,6},{8,7},{9,8},{10,9... | collective-permute-start | bytes 393224 | tf_op jit(solution)/shard_map/ppermute | solution.py:488
  115.6 7.9 %collective-permute-start.25 = (bf16[2,128,512]{2,1,0:T(8,128)(2,1)S(1)}, bf16[2,128,512]{2,1,0:T(8,128)(2,1)S(1)}, u32[]{:S(2)}, u32[]{:S(2)}) collective-permute-start(bf16[2,128,512]{2,1,0:T(8,128)(2,1)S(1)} %get-tuple-element.46.refs_4_), channel_id=1, source_target_pairs={{0,15},{1,0},{2,1},{3,2},{4,3},{5,4},{6,5},{7,6},{8,7},{9,8},{10,9... | collective-permute-start | bytes 786440 | tf_op jit(solution)/shard_map/ppermute | solution.py:488
  128.9 11.3 %collective-permute-start.35 = (bf16[128,512]{1,0:T(8,128)(2,1)S(1)}, bf16[128,512]{1,0:T(8,128)(2,1)S(1)}, u32[]{:S(2)}, u32[]{:S(2)}) collective-permute-start(bf16[128,512]{1,0:T(8,128)(2,1)S(1)} %mesh.1.refs_2_), channel_id=1, source_target_pairs={{0,16},{16,32},{32,48},{48,64},{64,80},{80,96},{96,112},{1,17},{17... | collective-permute-start | bytes 393224 | tf_op jit(solution)/shard_map/ppermute | solution.py:488
  132.3 10.7 %collective-permute-start.36 = (bf16[128,512]{1,0:T(8,128)(2,1)S(1)}, bf16[128,512]{1,0:T(8,128)(2,1)S(1)}, u32[]{:S(2)}, u32[]{:S(2)}) collective-permute-start(bf16[128,512]{1,0:T(8,128)(2,1)S(1)} %mesh.1.refs_2_), channel_id=1, source_target_pairs={{16,0},{32,16},{48,32},{64,48},{80,64},{96,80},{112,96},{17,1},{33... | collective-permute-start | bytes 393224 | tf_op jit(solution)/shard_map/ppermute | solution.py:488
  136.3 10.7 %collective-permute-start.33 = (bf16[128,512]{1,0:T(8,128)(2,1)S(1)}, bf16[128,512]{1,0:T(8,128)(2,1)S(1)}, u32[]{:S(2)}, u32[]{:S(2)}) collective-permute-start(bf16[128,512]{1,0:T(8,128)(2,1)S(1)} %mesh.1.refs_2_), channel_id=1, source_target_pairs={{0,1},{1,2},{2,3},{3,4},{4,5},{5,6},{6,7},{7,8},{8,9},{9,10},{10,1... | collective-permute-start | bytes 393224 | tf_op jit(solution)/shard_map/ppermute | solution.py:488
  136.4 10.6 %collective-permute-start.34 = (bf16[128,512]{1,0:T(8,128)(2,1)S(1)}, bf16[128,512]{1,0:T(8,128)(2,1)S(1)}, u32[]{:S(2)}, u32[]{:S(2)}) collective-permute-start(bf16[128,512]{1,0:T(8,128)(2,1)S(1)} %mesh.1.refs_2_), channel_id=1, source_target_pairs={{0,15},{1,0},{2,1},{3,2},{4,3},{5,4},{6,5},{7,6},{8,7},{9,8},{10,9... | collective-permute-start | bytes 393224 | tf_op jit(solution)/shard_map/ppermute | solution.py:488
  143.0 10.7 %collective-permute-start.37 = (bf16[2,128,512]{2,1,0:T(8,128)(2,1)S(1)}, bf16[2,128,512]{2,1,0:T(8,128)(2,1)S(1)}, u32[]{:S(2)}, u32[]{:S(2)}) collective-permute-start(bf16[2,128,512]{2,1,0:T(8,128)(2,1)S(1)} %pair.3.refs_4_), channel_id=1, source_target_pairs={{0,1},{1,2},{2,3},{3,4},{4,5},{5,6},{6,7},{7,8},{8,9},{9,10},{10,1... | collective-permute-start | bytes 786440 | tf_op jit(solution)/shard_map/ppermute | solution.py:488
  143.1 10.7 %collective-permute-start.38 = (bf16[2,128,512]{2,1,0:T(8,128)(2,1)S(1)}, bf16[2,128,512]{2,1,0:T(8,128)(2,1)S(1)}, u32[]{:S(2)}, u32[]{:S(2)}) collective-permute-start(bf16[2,128,512]{2,1,0:T(8,128)(2,1)S(1)} %pair.3.refs_4_), channel_id=1, source_target_pairs={{0,15},{1,0},{2,1},{3,2},{4,3},{5,4},{6,5},{7,6},{8,7},{9,8},{10,9... | collective-permute-start | bytes 786440 | tf_op jit(solution)/shard_map/ppermute | solution.py:488
  (12 other events, 106.3 us)

commit v3 on v2

v3 whole, which is shorter than its diff:
```python
import functools

import jax
import jax.numpy as jnp
from jax import lax
from jax.experimental import pallas as pl
from jax.experimental.pallas import tpu as pltpu
from jax.sharding import PartitionSpec as P

BF = jnp.bfloat16
F32 = jnp.float32
I32 = jnp.int32
WIDTH = 512
GRID_NODES = 1024
MESH_NODES = 128
MESH_DEGREE = 6
GRID_DEGREE = 3
COARSE_DEV = 16
SLOTS = 2048
CHUNK = 512
CHUNKS = SLOTS // CHUNK
LISTED = MESH_NODES + 8 * CHUNKS
PAYLOAD = LISTED + 16
COARSE_EDGES = 256
LON = 16
NEAR_SLOTS = 160
COARSE_SLOTS = 320
GROUPS = (5, 3, 7, 0, 1, 2, 6, 4, 8)
VMEM_BYTES = 14 * 1024 * 1024


def mm(left, right):
    return jnp.dot(left, right, preferred_element_type=F32)


def mm_t(left, right):
    return lax.dot_general(left, right, (((0,), (0,)), ((), ())), preferred_element_type=F32)


def mm_nt(left, right):
    return lax.dot_general(left, right, (((1,), (1,)), ((), ())), preferred_element_type=F32)


def silu(v):
    half = 0.5 * v
    return half + half * jnp.tanh(half)


def one_hot(column, width):
    spots = lax.broadcasted_iota(I32, (column.shape[0], width), 1)
    return jnp.where(spots == column, 1.0, 0.0).astype(BF)


class Load:
    def __init__(self, index, shape):
        self.index, self.shape = index, shape


class View:
    def __init__(self, index):
        self.index = index


class Arriving:
    def __init__(self, copy, ref):
        self.copy, self.ref = copy, ref
        self.shape = ref.shape

    def ready(self):
        if self.copy is not None:
            self.copy.wait()
            self.copy = None
        return self.ref

    def __getitem__(self, index):
        return self.ready()[index]


V = pl.BlockSpec(memory_space=pltpu.VMEM)
SMEM = pl.BlockSpec(memory_space=pltpu.SMEM)
ANY = pl.BlockSpec(memory_space=pl.ANY)
HBM = pl.BlockSpec(memory_space=pltpu.HBM)


def square(block, kind):
    return Load((block, kind), (WIDTH, WIDTH))


def first_half(block, half):
    return Load((block, slice(WIDTH * half, WIDTH * (half + 1))), (WIDTH, WIDTH))


def second_of(block):
    return Load((block,), (WIDTH, WIDTH))


KEPT = (
    ("square", square(0, 2)), ("first", first_half(0, 0)), ("first", first_half(0, 1)), ("second", second_of(0)),
    ("square", square(1, 0)), ("square", square(1, 1)), ("square", square(1, 2)), ("first", first_half(1, 0)),
    ("first", first_half(1, 1)), ("second", second_of(1)), ("square", square(2, 0)), ("square", square(2, 2)),
    ("first", first_half(2, 1)),
)
ENCODER = (square(0, 0), square(0, 1))


def kernel_call(body, outs, specs, args, scratch=(), flops=0, moved=0, name=None, out_specs=None):
    loads = [(k, spec, args[k].dtype) for k, spec in enumerate(specs) if isinstance(spec, Load)]
    n_in, n_loads = len(specs), len(loads)

    def run(*refs):
        given, rest = list(refs[:n_in]), list(refs[n_in:])
        if n_loads:
            sems = rest[-1]
            buffers = rest[-1 - n_loads : -1]
            rest = rest[: -1 - n_loads]
            for at, ((k, spec, _), buffer) in enumerate(zip(loads, buffers)):
                source = given[k].at[spec.index] if spec.index else given[k]
                copy = pltpu.make_async_copy(source, buffer, sems.at[at])
                copy.start()
                given[k] = Arriving(copy, buffer)
        for k, spec in enumerate(specs):
            if isinstance(spec, View):
                given[k] = given[k].at[spec.index]
        body(*given, *rest)
        for part in given:
            if isinstance(part, Arriving):
                part.ready()

    extra = [pltpu.VMEM(spec.shape, dtype) for _, spec, dtype in loads]
    if loads:
        extra.append(pltpu.SemaphoreType.DMA((n_loads,)))
    many = isinstance(outs, tuple)
    args = [
        pltpu.with_memory_space_constraint(arg, pltpu.HBM) if spec is HBM or isinstance(spec, Load) else arg
        for spec, arg in zip(specs, args)
    ]
    return pl.pallas_call(
        run,
        out_shape=outs,
        in_specs=[HBM if isinstance(q, Load) else V if isinstance(q, View) else q for q in specs],
        out_specs=out_specs if out_specs is not None else (V,) * len(outs) if many else V,
        scratch_shapes=list(scratch) + extra,
        compiler_params=pltpu.CompilerParams(vmem_limit_bytes=VMEM_BYTES),
        cost_estimate=pl.CostEstimate(flops=flops, bytes_accessed=moved, transcendentals=0),
        name=name,
    )(*args)


def shaped(shape, dtype):
    return jax.ShapeDtypeStruct(shape, dtype)


def fill_list(scr, width, indices, geometry):
    for row, value in enumerate(indices):
        scr[row : row + 1, 0:width] = value.astype(F32)
    high = geometry.astype(BF).astype(F32)
    scr[4:8, 0:width] = high
    scr[8:12, 0:width] = geometry - high
    scr[12:16, 0:width] = high


def pack_body(
    count, senders, receivers, geometry, state, c_senders, c_receivers, c_geometry, weight,
    out, own, coarse, w_out, scr, short,
):
    for c in range(CHUNKS):
        cols = slice(c * CHUNK, (c + 1) * CHUNK)
        s = senders[:, cols]
        edge = lax.broadcasted_iota(I32, (1, CHUNK), 1) + c * CHUNK
        code = jnp.where(edge < count[0, 0], lax.shift_right_logical(s, 10) + 1, 0)
        local = s & (GRID_NODES - 1)
        fill_list(
            scr, CHUNK, (code, lax.shift_right_logical(local, 8), local & 255, receivers[:, cols]), geometry[:, cols]
        )
        own[16 * c : 16 * (c + 1), :] = scr[...].astype(BF)
        short[8 * c : 8 * (c + 1), :] = scr[0:8, :]
    out[MESH_NODES:LISTED, :] = short[...].astype(BF)
    s = c_senders[...]
    r = c_receivers[...]
    n = s.shape[1]
    fill_list(
        scr, n, (lax.shift_right_logical(s, 8), s & 255, lax.shift_right_logical(r, 4), r & 15), c_geometry[...]
    )
    out[LISTED:PAYLOAD, :] = scr[...].astype(BF)
    coarse[...] = scr[:, 0:n].astype(BF)
    zero = jnp.zeros((4, WIDTH), F32)
    for k in range(3):
        w = weight[k]
        high = w.astype(BF).astype(F32)
        scr[0:4, :] = zero
        scr[4:8, :] = high
        scr[8:12, :] = high
        scr[12:16, :] = w - high
        w_out[k] = scr[...].astype(BF)
        if k == 0:
            scr[8:12, :] = zero
            w_out[3] = scr[...].astype(BF)
    out[0:MESH_NODES, :] = state[...]


def prep_body(m_senders, m_geometry, d_senders, d_geometry, order, *refs):
    n = len(KEPT)
    sources, (m_out, d_out), kept, (scr, turned, sems) = refs[:n], refs[n : n + 2], refs[n + 2 : -3], refs[-3:]
    copies = bring(sources, [load for _, load in KEPT], kept, sems)
    for senders, geometry, degree, out in (
        (m_senders, m_geometry, MESH_DEGREE, m_out),
        (d_senders, d_geometry, GRID_DEGREE, d_out),
    ):
        n = senders.shape[1]
        s = senders[...]
        near = lax.shift_right_logical(s, 7)
        spot = jnp.zeros_like(near)
        for place, group in enumerate(GROUPS):
            spot = jnp.where(near == place, group, spot)
        spot = spot * MESH_NODES + (s & (MESH_NODES - 1))
        zero = jnp.zeros((1, n), F32)
        fill_list(scr, n, (spot, zero, zero, zero), geometry[...])
        turned[0:n, :] = scr[:, 0:n].T
        for t in range(degree):
            out[t] = turned[pl.ds(t, n // degree, stride=degree), :]
    for copy in copies:
        copy.wait()


def embed_body(x, w_in, w_out, source, source_too, latent, w_send, w_recv, sems):
    copies = bring((source, source_too), ENCODER, (w_send, w_recv), sems)
    for b in range(4):
        rows = slice(256 * b, 256 * (b + 1))
        hidden = silu(mm(x[rows, :], w_in[...])).astype(BF)
        latent[rows, :] = mm(hidden, w_out[...]).astype(BF)
    for copy in copies:
        copy.wait()


def send_body(latent, w_send, order, order_too, send):
    for b in range(4):
        rows = slice(256 * b, 256 * (b + 1))
        send[rows, :] = mm(latent[rows, :], w_send[...]).astype(BF)


def grid_body(latent, w_recv, w_first, order, recv, base):
    for b in range(4):
        rows = slice(256 * b, 256 * (b + 1))
        recv[rows, :] = mm(latent[rows, :], w_recv[...]).astype(BF)
        base[rows, :] = mm(latent[rows, :], w_first[...])


def bring(sources, loads, outs, sems):
    copies = []
    for k, load in enumerate(loads):
        copies.append(pltpu.make_async_copy(sources[k].at[load.index], outs[k], sems.at[k]))
        copies[-1].start()
    return copies


def self_body(state, listed, send, w_recv, w_geom, out):
    total = jnp.zeros((MESH_NODES, WIDTH), F32)
    q = None
    for c in range(CHUNKS):
        d = listed[16 * c : 16 * (c + 1), :].astype(F32).T
        s = (d[:, 1:2] * 256.0 + d[:, 2:3]).astype(I32)
        r = jnp.where(d[:, 0:1] == 5.0, d[:, 3:4], -1.0).astype(I32)
        pick = one_hot(r, MESH_NODES)
        pre = mm(one_hot(s, GRID_NODES), send[...]) + mm(d.astype(BF), w_geom[...])
        if q is None:
            q = mm(state[...], w_recv[...]).astype(BF)
        total += mm_t(pick, silu(pre + mm(pick, q)).astype(BF))
    out[...] = total


def near_body(buckets, place, *refs):
    sources, refs = refs[: len(buckets)], refs[len(buckets) :]
    if len(refs) == 16:
        beside, order_first, order_last, *refs = refs
    send, w_recv, w_geom, *refs = refs
    outs, refs = refs[: len(buckets)], refs[len(buckets) :]
    if len(refs) == 6 and buckets[0] != 5:
        following, *refs = refs
        n = COARSE_EDGES
        last = (place[0, 4] & (LON - 1)) == LON - 1
        following[...] = jnp.where(
            last, sources[-1][LISTED:PAYLOAD, 0:n].astype(F32), beside[...].astype(F32)
        ).astype(BF)
    if len(buckets) == 4 and buckets[0] == 5:
        following, *refs = refs
        following[...] = sources[1][LISTED:PAYLOAD, 0:COARSE_EDGES]
    masks, ranks, q, edges, sums = refs
    last = lax.shift_right_logical(place[0, 4], 4) == 7
    lists = tuple(zip(sources, buckets, outs))
    q[...] = jnp.zeros_like(q)

    def listed(src, c):
        return src[MESH_NODES:LISTED, :].astype(F32)[8 * c : 8 * (c + 1), :]

    def geometry_part(d):
        return mm(jnp.concatenate([d, d], axis=1).astype(BF), w_geom[...])

    for i, (src, bucket, _) in enumerate(lists):
        for c in range(CHUNKS):
            row = i * CHUNKS + c
            code = listed(src, c)[0:1, :]
            wanted = jnp.where(last, -1.0, float(bucket + 1)) if bucket < 3 else float(bucket + 1)
            masks[row : row + 1, :] = jnp.where(code == wanted, 1.0, 0.0)
    n = masks.shape[0]
    mask = masks[...]
    before = lax.broadcasted_iota(I32, (CHUNK, CHUNK), 0) < lax.broadcasted_iota(I32, (CHUNK, CHUNK), 1)
    inside = mm(mask.astype(BF), jnp.where(before, 1.0, 0.0).astype(BF))
    mine = lax.broadcasted_iota(I32, (n, n), 0)
    other = lax.broadcasted_iota(I32, (n, n), 1)
    same = mine // CHUNKS == other // CHUNKS
    earlier = jnp.where((other < mine) & same, 1.0, 0.0).astype(BF)
    carried = mm(earlier, mask.astype(BF)).sum(axis=1, keepdims=True)
    ranks[...] = jnp.where(mask > 0.5, inside + carried, -1.0).astype(I32)

    slot = lax.broadcasted_iota(I32, (NEAR_SLOTS, CHUNK), 0)
    for i, (src, _, _) in enumerate(lists):
        d = jnp.zeros((NEAR_SLOTS, 8), F32)
        for c in range(CHUNKS):
            row = i * CHUNKS + c
            d += mm_nt(jnp.where(slot == ranks[row : row + 1, :], 1.0, 0.0).astype(BF), listed(src, c).astype(BF))
        edges[NEAR_SLOTS * i : NEAR_SLOTS * (i + 1), :] = d
    for src, bucket, _ in lists:
        q[MESH_NODES * bucket : MESH_NODES * (bucket + 1), :] = mm(src[0:MESH_NODES, :], w_recv[...]).astype(BF)
    for j in range(len(lists) // 2):
        d = edges[2 * NEAR_SLOTS * j : 2 * NEAR_SLOTS * (j + 1), :]
        s = (d[:, 1:2] * 256.0 + d[:, 2:3]).astype(I32)
        pre = mm(one_hot(s, GRID_NODES), send[...]) + geometry_part(d)
        r = jnp.where(d[:, 0:1] > 0.5, d[:, 3:4], -1.0).astype(I32)
        for h in range(2):
            bucket = lists[2 * j + h][1]
            part = slice(NEAR_SLOTS * h, NEAR_SLOTS * (h + 1))
            rows = slice(MESH_NODES * bucket, MESH_NODES * (bucket + 1))
            pick = one_hot(r[part, :], MESH_NODES)
            sums[rows, :] = mm_t(pick, silu(pre[part, :] + mm(pick, q[rows, :])).astype(BF))

    count = mm(jnp.where(same, 1.0, 0.0).astype(BF), mask.astype(BF)).sum(axis=1, keepdims=True)
    over = jnp.maximum(count - NEAR_SLOTS, 0.0)
    total = lax.shift_right_logical(jnp.sum(over).astype(I32), 2)

    @pl.when(total > 0)
    def _():
        across = lax.broadcasted_iota(I32, (n, 1), 0) // CHUNKS
        base = jnp.zeros((n, 1), F32)
        for i in range(len(lists) - 1):
            base += jnp.where(across > i, over[i * CHUNKS : i * CHUNKS + 1, :], 0.0)
        rank = ranks[...]
        ranks[...] = jnp.where(rank >= NEAR_SLOTS, rank - NEAR_SLOTS + base.astype(I32), -1)

        @pl.loop(0, lax.shift_right_logical(total + 127, 7))
        def _(k):
            late = lax.broadcasted_iota(I32, (128, CHUNK), 0) + k * 128
            d = jnp.zeros((128, 8), F32)
            for i, (src, _, _) in enumerate(lists):
                for c in range(CHUNKS):
                    row = i * CHUNKS + c
                    d += mm_nt(jnp.where(late == ranks[row : row + 1, :], 1.0, 0.0).astype(BF), listed(src, c).astype(BF))
            s = (d[:, 1:2] * 256.0 + d[:, 2:3]).astype(I32)
            code = d[:, 0:1]
            r = jnp.where(code > 0.5, (code - 1.0) * float(MESH_NODES) + d[:, 3:4], -1.0).astype(I32)
            pick = one_hot(r, 9 * MESH_NODES)
            pre = mm(one_hot(s, GRID_NODES), send[...]) + mm(pick, q[...]) + geometry_part(d)
            sums[...] += mm_t(pick, silu(pre).astype(BF))

    for _, bucket, dst in lists:
        dst[...] = sums[MESH_NODES * bucket : MESH_NODES * (bucket + 1), :].astype(BF)


def corner_body(a, b, c, d, left, right):
    left[0] = a[...]
    left[1] = b[...]
    right[0] = c[...]
    right[1] = d[...]


def side_sum_body(above, below, from_left, from_right, left, right, order, up, down, o_left, o_right):
    for k, middle, out in ((0, above, up), (1, below, down)):
        total = middle[...].astype(F32) + from_left[k].astype(F32) + from_right[k].astype(F32)
        out[...] = total.astype(BF)
    o_left[...] = left[...]
    o_right[...] = right[...]


def join_body(parts, out):
    n = parts[0].shape[0]
    for k, part in enumerate(parts):
        out[n * k : n * (k + 1), :] = part[...]


def pair_body(up, down, order, out):
    out[0] = up[...]
    out[1] = down[...]


def partner_body(own, partner, coarse, order, near, far):
    near[0:MESH_NODES, :] = partner[...]
    near[MESH_NODES : MESH_NODES + COARSE_DEV, :] = own[0:COARSE_DEV, :]
    far[0:COARSE_DEV, :] = own[0:COARSE_DEV, :]
    far[COARSE_DEV : 2 * COARSE_DEV, :] = partner[0:COARSE_DEV, :]
    far[2 * COARSE_DEV : 3 * COARSE_DEV, :] = jnp.zeros((COARSE_DEV, WIDTH), BF)
    far[2 * COARSE_DEV : 3 * COARSE_DEV, 0:COARSE_EDGES] = coarse[...]


def bands_body(own, partner, below, across, above, coarse):
    n = COARSE_DEV
    coarse[0:n, :] = own[0:n, :]
    coarse[n : 2 * n, :] = partner[0:n, :]
    coarse[2 * n : 3 * n, :] = below[MESH_NODES : MESH_NODES + n, :]
    coarse[3 * n : 4 * n, :] = below[0:n, :]
    coarse[4 * n : 6 * n, :] = across[0 : 2 * n, :]
    coarse[6 * n : 7 * n, :] = above[MESH_NODES : MESH_NODES + n, :]
    coarse[7 * n : 8 * n, :] = above[0:n, :]


def both_body(place, a, b, own, partner, below, above, out, triple):
    join_body((a, b), out)
    triple[1] = own[...]
    odd = place[0, 2] >= 2

    @pl.when(odd)
    def _():
        triple[0] = partner[...]
        triple[2] = above[0:MESH_NODES, :]

    @pl.when(jnp.logical_not(odd))
    def _():
        triple[0] = below[0:MESH_NODES, :]
        triple[2] = partner[...]


def split_mm(value, weight):
    high = value.astype(BF)
    low = (value - high.astype(F32)).astype(BF)
    return mm(high, weight) + mm(low, weight)


def node_rows(v, hidden_total, w_second, first_node, first_sum, second):
    m = split_mm(hidden_total, w_second).astype(BF)
    u = silu(mm(v, first_node) + mm(m, first_sum)).astype(BF)
    return (v.astype(F32) + mm(u, second)).astype(BF)


def node_body(
    own, from_left, from_right, up, down, state, w_second, first_node, first_sum, second, w_send, w_recv,
    mesh_one, send, recv,
):
    total = own[...] + from_left[...].astype(F32) + from_right[...].astype(F32)
    total = total + up[...].astype(F32) + down[...].astype(F32)
    one = node_rows(state[...], total, w_second[...], first_node[...], first_sum[...], second[...])
    mesh_one[...] = one
    send[...] = mm(one, w_send[...]).astype(BF)
    recv[...] = mm(one, w_recv[...]).astype(BF)


def fine_body(edges, left, own, right, recv, w_geom, order, order_too, out, rows):
    parts = (left[1], own[1], right[1], own[0], own[2], left[0], left[2], right[0], right[2])
    for k, part in enumerate(parts):
        rows[MESH_NODES * k : MESH_NODES * (k + 1), :] = part
    q = recv[...].astype(F32)
    total = jnp.zeros((MESH_NODES, WIDTH), F32)
    for t in range(MESH_DEGREE):
        d = edges[t]
        spread = one_hot(d[:, 0:1].astype(I32), 9 * MESH_NODES)
        pre = q + mm(spread, rows[...]) + mm(d.astype(BF), w_geom[...])
        total += silu(pre)
    out[...] = total


def coarse_prep_body(place, own, following, far, out, count, row):
    z, y, x, core, tile = (place[0, k] for k in range(5))
    n = COARSE_EDGES
    lists = (own[...], following[...], far[2 * COARSE_DEV : 3 * COARSE_DEV, 0:n])
    for k, edges in enumerate(lists):
        owner = edges.astype(F32)[2:3, :].astype(I32)
        row[k : k + 1, :] = jnp.where(owner == tile, 1.0, 0.0)
    row[3:8, :] = jnp.zeros((5, n), F32)
    mask = row[...]
    before = lax.broadcasted_iota(I32, (n, n), 0) < lax.broadcasted_iota(I32, (n, n), 1)
    inside = mm(mask.astype(BF), jnp.where(before, 1.0, 0.0).astype(BF))
    earlier = lax.broadcasted_iota(I32, (8, 8), 1) < lax.broadcasted_iota(I32, (8, 8), 0)
    carried = mm(jnp.where(earlier, 1.0, 0.0).astype(BF), mask.astype(BF)).sum(axis=1, keepdims=True)
    rank = jnp.where(mask > 0.5, inside + carried, -1.0).astype(I32)
    slot = lax.broadcasted_iota(I32, (3 * n, n), 0)
    d = jnp.zeros((3 * n, 16), F32)
    for k, edges in enumerate(lists):
        d += mm_nt(jnp.where(slot == rank[k : k + 1, :], 1.0, 0.0).astype(BF), edges)
    s = (d[:, 0:1] * 256.0 + d[:, 1:2]).astype(I32)
    t = lax.shift_right_logical(s, 4)
    lat = lax.shift_right_logical(t, 4)
    lon = t & 15
    gz = (z - lax.shift_right_logical(lat, 1)) & 3
    gy = (y - lax.shift_right_logical(lon, 2)) & 3
    g_high = (lax.shift_right_logical(x, 1) + lat) & 1
    g_low = (x + lax.shift_right_logical(lon, 1)) & 1
    gc = (core + lon) & 1
    spot = ((((gc * 4 + gy) * 2 + g_low) * 4 + gz) * 2 + g_high) * 16 + (s & 15)
    total = jnp.sum(mask).astype(I32)
    used = lax.broadcasted_iota(I32, (3 * n, 1), 0) < total
    r = jnp.where(used, d[:, 3:4], -1.0)
    lane = lax.broadcasted_iota(I32, (3 * n, 16), 1)
    out[...] = jnp.where(lane == 0, spot.astype(F32), jnp.where(lane == 1, r, d))
    count[0, 0] = total


def mesh_body(
    count, fine, edges, a0, a1, a2, a3, b0, b1, b2, b3, recv, mesh_one, w_geom, w_second, first_node, first_sum,
    second, w_send, send, rows, total,
):
    parts = (a0, a1, a2, a3, b0, b1, b2, b3)
    n = a0.shape[0]
    for k, part in enumerate(parts):
        rows[n * k : n * (k + 1), :] = part[...]
    q = recv[0:COARSE_DEV, :]

    def hidden_sum(d):
        pick = one_hot(d[:, 1:2].astype(I32), MESH_NODES)
        pre = mm(one_hot(d[:, 0:1].astype(I32), len(parts) * n), rows[...])
        pre += mm(pick[:, 0:COARSE_DEV], q) + mm(d.astype(BF), w_geom[...])
        return mm_t(pick, silu(pre).astype(BF))

    total[...] = fine[...] + hidden_sum(edges[0:COARSE_SLOTS, :])

    @pl.loop(COARSE_SLOTS // 64, lax.shift_right_logical(count[0, 0] + 63, 6))
    def _(k):
        total[...] += hidden_sum(edges[pl.ds(pl.multiple_of(64 * k, 64), 64), :])

    two = node_rows(mesh_one[...], total[...], w_second[...], first_node[...], first_sum[...], second[...])
    send[...] = mm(two, w_send[...]).astype(BF)


def decode_early_body(edges, left, own, right, pair, recv, w_geom, out, rows):
    for k, part in enumerate((left, own, right, pair.at[0], pair.at[1])):
        rows[MESH_NODES * k : MESH_NODES * (k + 1), :] = part[...]
    n = 5 * MESH_NODES

    @pl.loop(0, 4)
    def _(b):
        span = pl.ds(pl.multiple_of(256 * b, 256), 256)
        q = recv[span, :].astype(F32)
        for t in range(GRID_DEGREE):
            d = edges[t, span, :]
            spread = one_hot(d[:, 0:1].astype(I32), n)
            out[t, span, :] = q + mm(spread, rows[0:n, :]) + mm(d.astype(BF), w_geom[...])


def decode_body(edges, early, left_pair, right_pair, base, w_second, first_sum, head, out, rows, totals):
    for k, part in enumerate((left_pair.at[0], left_pair.at[1], right_pair.at[0], right_pair.at[1])):
        rows[MESH_NODES * k : MESH_NODES * (k + 1), :] = part[...]
    for b in range(4):
        span = slice(256 * b, 256 * (b + 1))
        total = jnp.zeros((256, WIDTH), F32)
        for t in range(GRID_DEGREE):
            spot = edges[t, span, :][:, 0:1].astype(I32) - 5 * MESH_NODES
            total += silu(early[t, span, :] + mm(one_hot(spot, 4 * MESH_NODES), rows[...]))
        totals[span, :] = total.astype(BF)
    for b in range(2):
        span = slice(512 * b, 512 * (b + 1))
        summed = mm(totals[span, :], w_second[...]).astype(BF)
        hidden = silu(base[span, :] + mm(summed, first_sum[...])).astype(BF)
        out[:, span] = mm_nt(head[...], hidden).astype(BF)


def shift(value, axis, step, periodic):
    n = lax.axis_size(axis)
    pairs = [(i, (i + step) % n) for i in range(n) if periodic or 0 <= i + step < n]
    return lax.ppermute(value, axis, pairs)


def first_stage(value, round_down=False):
    up = shift(value, "lat", 1, False)
    down = shift(value, "lat", -1, round_down)
    return up, down, shift(value, "lon", 1, True), shift(value, "lon", -1, True)


def second_stage(pair):
    return shift(pair, "lon", 1, True), shift(pair, "lon", -1, True)


def along_z(s):
    return [(i, ((i // 2 + s) % 4) * 2 + i % 2) for i in range(8)]


def along_y(s):
    return [(i, ((i // 4 + s) % 4) * 4 + i % 4) for i in range(16)]


def four(value, axis, pairs_of):
    return [value] + [lax.ppermute(value, axis, pairs_of(s)) for s in (1, 2, 3)]


def per_device(
    grid_inputs,
    mesh_state,
    embed_in,
    embed_out,
    edge_square,
    edge_geom_weight,
    node_first,
    node_second,
    head,
    g2m_senders,
    g2m_receivers,
    g2m_counts,
    g2m_geom,
    mesh_senders,
    mesh_geom,
    coarse_senders,
    coarse_receivers,
    coarse_geom,
    m2g_senders,
    m2g_geom,
):
    mesh_rows = (MESH_NODES, WIDTH)
    grid_rows = (GRID_NODES, WIDTH)
    pair_rows = (2,) + mesh_rows
    grid_flops = 2 * GRID_NODES * WIDTH * WIDTH
    mesh_flops = grid_flops // 8
    both = ("lat", "lon")
    tiles = lax.axis_size(both)
    lat, lon = lax.axis_index("lat"), lax.axis_index("lon")
    place = jnp.stack([lat // 2, lon // 4, (lat % 2) * 2 + (lon // 2) % 2, lon % 2, lat * LON + lon])[None]
    place = place.astype(I32)

    pack_args = (
        g2m_senders, g2m_receivers, g2m_geom, mesh_state, coarse_senders, coarse_receivers, coarse_geom
    )

    def part_of(array):
        n = array.ndim - 2
        return Load((0,) if n == 1 else (0, 0), array.shape[1:] if n == 1 else array.shape[2:])

    payload, own_list, coarse_list, geom = kernel_call(
        pack_body,
        (
            shaped((PAYLOAD, WIDTH), BF), shaped((16 * CHUNKS, WIDTH), BF), shaped((16, COARSE_EDGES), BF),
            shaped((4, 16, WIDTH), BF),
        ),
        [SMEM] + [part_of(a) for a in pack_args] + [Load((), edge_geom_weight.shape)],
        (g2m_counts,) + pack_args + (edge_geom_weight,),
        [pltpu.VMEM((16, CHUNK), F32), pltpu.VMEM((8 * CHUNKS, CHUNK), F32)],
        name="pack",
    )
    up, down, near_left, near_right = first_stage(payload, True)
    latent, w_send, w_recv = kernel_call(
        embed_body,
        (shaped(grid_rows, BF),) + (shaped((WIDTH, WIDTH), BF),) * 2,
        [V, Load((), embed_in.shape), Load((), embed_out.shape), HBM, HBM],
        (grid_inputs[0, 0], embed_in, embed_out, edge_square, edge_square),
        [pltpu.SemaphoreType.DMA((2,))],
        flops=2 * grid_flops,
        moved=4 << 20,
        name="embed",
    )
    grid_send = kernel_call(
        send_body,
        shaped(grid_rows, BF),
        [V, V, ANY, ANY],
        (latent, w_send, near_left, near_right),
        flops=grid_flops,
        moved=3 << 20,
        name="send",
    )

    def geom_of(k):
        return View(k)

    def paired(up, down, order):
        shape = (2,) + up.shape
        return kernel_call(pair_body, shaped(shape, BF), [V, V, ANY], (up, down, order), name="pair")

    near_middle = paired(up, down, grid_send)
    near_left_pair, near_right_pair = second_stage(near_middle)
    own_sum = kernel_call(
        self_body,
        shaped(mesh_rows, F32),
        [part_of(mesh_state), V, V, V, geom_of(0)],
        (mesh_state, own_list, grid_send, w_recv, geom),
        flops=5 * grid_flops,
        moved=3 << 20,
        name="own",
    )
    near_scratch = [
        pltpu.VMEM((4 * CHUNKS, CHUNK), F32),
        pltpu.VMEM((4 * CHUNKS, CHUNK), I32),
        pltpu.VMEM((9 * MESH_NODES, WIDTH), BF),
        pltpu.VMEM((4 * NEAR_SLOTS, 8), F32),
        pltpu.VMEM((9 * MESH_NODES, WIDTH), F32),
    ]
    near_weights = [V, V, geom_of(3)]
    to_left, to_right, to_above, to_below, right_list = kernel_call(
        functools.partial(near_body, (5, 3, 7, 1)),
        (shaped(mesh_rows, BF),) * 4 + (shaped((16, COARSE_EDGES), BF),),
        [SMEM, V, V, View(0), View(1)] + near_weights,
        (place, near_left, near_right, near_middle, near_middle, grid_send, w_recv, geom),
        near_scratch,
        flops=2 * grid_flops,
        moved=5 << 20,
        name="beside",
    )
    *to_corners, coarse_next = kernel_call(
        functools.partial(near_body, (8, 2, 6, 0)),
        (shaped(mesh_rows, BF),) * 4 + (shaped((16, COARSE_EDGES), BF),),
        [SMEM, View(0), View(1), View(0), View(1), V, ANY, ANY] + near_weights,
        (
            place, near_left_pair, near_left_pair, near_right_pair, near_right_pair, right_list, own_sum, to_left,
            grid_send, w_recv, geom,
        ),
        near_scratch,
        flops=2 * grid_flops,
        moved=5 << 20,
        name="corners",
    )
    to_left_pair, to_right_pair = kernel_call(
        corner_body, (shaped(pair_rows, BF),) * 2, [V] * 4, tuple(to_corners), name="corner_pairs"
    )
    pair_left = shift(to_right_pair, "lon", 1, True)
    pair_right = shift(to_left_pair, "lon", -1, True)
    prep_args = (mesh_senders, mesh_geom, m2g_senders, m2g_geom)
    stored = {"square": edge_square, "first": node_first, "second": node_second}
    m_edges, d_edges, *kept = kernel_call(
        prep_body,
        (
            shaped((MESH_DEGREE, MESH_NODES, 16), F32),
            shaped((GRID_DEGREE, GRID_NODES, 16), F32),
        ) + (shaped((WIDTH, WIDTH), BF),) * len(KEPT),
        [part_of(a) for a in prep_args] + [ANY] + [HBM] * len(KEPT),
        prep_args + (to_left_pair,) + tuple(stored[name] for name, _ in KEPT),
        [pltpu.VMEM((16, 3072), F32), pltpu.VMEM((3072, 16), F32), pltpu.SemaphoreType.DMA((len(KEPT),))],
        flops=grid_flops,
        name="prep",
    )
    to_up, to_down, to_left, to_right = kernel_call(
        side_sum_body,
        (shaped(mesh_rows, BF),) * 4,
        [V, V, V, V, V, V, ANY],
        (to_above, to_below, pair_left, pair_right, to_left, to_right, m_edges),
        name="sides",
    )
    down = shift(to_up, "lat", -1, False)
    up = shift(to_down, "lat", 1, False)
    from_left = shift(to_right, "lon", 1, True)
    from_right = shift(to_left, "lon", -1, True)
    mesh_one, proc_send, proc_recv = kernel_call(
        node_body,
        (shaped(mesh_rows, BF),) * 3,
        [V] * 5 + [part_of(mesh_state)] + [V] * 6,
        (own_sum, from_left, from_right, up, down, mesh_state, *kept[0:6]),
        flops=7 * mesh_flops,
        moved=4 << 20,
        name="node",
    )
    grid_recv, grid_base = kernel_call(
        grid_body,
        (shaped(grid_rows, BF), shaped(grid_rows, F32)),
        [V, square(2, 1), first_half(2, 0), ANY],
        (latent, edge_square, node_first, proc_send),
        flops=2 * grid_flops,
        moved=5 << 20,
        name="grid",
    )
    partner = lax.ppermute(proc_send, "lat", [(i, i ^ 1) for i in range(8)])
    beside, apart = kernel_call(
        partner_body,
        (shaped((MESH_NODES + COARSE_DEV, WIDTH), BF), shaped((3 * COARSE_DEV, WIDTH), BF)),
        [V, V, V, ANY],
        (proc_send, partner, coarse_list, grid_recv),
        name="partner",
    )
    below = lax.ppermute(beside, "lat", along_z(1))
    above = lax.ppermute(beside, "lat", along_z(3))
    across = lax.ppermute(apart, "lat", along_z(2))
    rows = kernel_call(
        bands_body,
        shaped((8 * COARSE_DEV, WIDTH), BF),
        [V] * 5,
        (proc_send, partner, below, across, above),
        name="bands",
    )
    other = lax.ppermute(rows, "lon", [(i, i ^ 2) for i in range(LON)])
    rows, triple = kernel_call(
        both_body,
        (shaped((16 * COARSE_DEV, WIDTH), BF), shaped((3,) + mesh_rows, BF)),
        [SMEM] + [V] * 6,
        (place, rows, other, proc_send, partner, below, above),
        name="join_x",
    )
    left, right = second_stage(triple)
    quarter = four(rows, "lon", along_y)
    swapped = [lax.ppermute(part, "lon", [(i, i ^ 1) for i in range(LON)]) for part in quarter]
    edge_total = 3 * COARSE_EDGES
    c_edges, c_count = kernel_call(
        coarse_prep_body,
        (shaped((edge_total, 16), F32), shaped((1, 1), I32)),
        [SMEM, V, V, V],
        (place, coarse_list, coarse_next, across),
        [pltpu.VMEM((8, COARSE_EDGES), F32)],
        flops=mesh_flops,
        name="coarse_edges",
        out_specs=(V, SMEM),
    )
    fine = kernel_call(
        fine_body,
        shaped(mesh_rows, F32),
        [V] * 5 + [geom_of(1), ANY, ANY],
        (m_edges, left, triple, right, proc_recv, geom, quarter[1], c_edges),
        [pltpu.VMEM((9 * MESH_NODES, WIDTH), BF)],
        flops=2 * grid_flops,
        moved=3 << 20,
        name="fine",
    )
    dec_send = kernel_call(
        mesh_body,
        shaped(mesh_rows, BF),
        [SMEM] + [V] * 12 + [geom_of(1)] + [V] * 5,
        (c_count, fine, c_edges, *quarter, *swapped, proc_recv, mesh_one, geom, *kept[6:11]),
        [pltpu.VMEM((128 * COARSE_DEV, WIDTH), BF), pltpu.VMEM(mesh_rows, F32)],
        flops=4 * grid_flops,
        moved=6 << 20,
        name="mesh",
    )
    up, down, left, right = first_stage(dec_send)
    pair = paired(up, down, dec_send)
    left_pair, right_pair = second_stage(pair)
    early = kernel_call(
        decode_early_body,
        shaped((GRID_DEGREE,) + grid_rows, F32),
        [V, V, V, V, V, V, geom_of(2)],
        (d_edges, left, dec_send, right, pair, grid_recv, geom),
        [pltpu.VMEM((5 * MESH_NODES, WIDTH), BF)],
        flops=4 * grid_flops,
        moved=8 << 20,
        name="early",
    )
    outputs = kernel_call(
        decode_body,
        shaped((head.shape[1], GRID_NODES), BF),
        [V] * 8,
        (d_edges, early, left_pair, right_pair, grid_base, *kept[11:13], head.T),
        [pltpu.VMEM((4 * MESH_NODES, WIDTH), BF), pltpu.VMEM(grid_rows, BF)],
        flops=5 * grid_flops,
        moved=8 << 20,
        name="decode",
    )
    return outputs.T[None, None]


def solution(mesh):
    return jax.shard_map(
        per_device,
        mesh=mesh,
        in_specs=(
            P("lat", "lon", None, None),
            P("lat", "lon", None, None),
            P(),
            P(),
            P(),
            P(),
            P(),
            P(),
            P(),
            P("lat", "lon", None),
            P("lat", "lon", None),
            P("lat", "lon"),
            P("lat", "lon", None, None),
            P("lat", "lon", None),
            P("lat", "lon", None, None),
            P("lat", "lon", None),
            P("lat", "lon", None),
            P("lat", "lon", None, None),
            P("lat", "lon", None),
            P("lat", "lon", None, None),
        ),
        out_specs=P("lat", "lon", None, None),
        check_vma=False,
    )
```

time: 163 us -> 143 us (0.88)
  starting transfers between devices: 78.4 us -> 55.8 us
  waiting for transfers between devices: 30.6 us -> 38.6 us
  Pallas kernels: 48.8 us -> 43.2 us
    ppermute x24 -> x20, starting transfers between devices: 59.7 us -> 45.3 us  [shift(): return lax.ppermute(value, axis, pairs)]
    ppermute x24 -> x20, waiting for transfers between devices: 21.9 us -> 12 us  [shift(): return lax.ppermute(value, axis, pairs)]
    ppermute x2 -> x5, waiting for transfers between devices: 2.9 us -> 12.5 us  [the longest x1 4.95 us: per_device(): other = lax.ppermute(rows, 'lon', [(i, i ^ 2) for i in range(LON)])]
    ppermute x9 -> x3, starting transfers between devices: 13.1 us -> 3.75 us  [four(): return [value] + [lax.ppermute(value, axis, pairs_of(s)) for s in (1, 2, 3)]]
    ppermute x9 -> x3, waiting for transfers between devices: 5.84 us -> 14.1 us  [four(): return [value] + [lax.ppermute(value, axis, pairs_of(s)) for s in (1, 2, 3)]]
    pallas_call x17 -> x21, Pallas kernels: 48.8 us -> 43.2 us  [kernel_call(): pl.pallas_call(run, out_shape=outs, in_specs=[HBM if isinstance(q, Load)...]
    ppermute x2 -> x5, starting transfers between devices: 4.62 us -> 5.68 us  [the longest x1 1.99 us: per_device(): below = lax.ppermute(beside, 'lat', along_z(1))]
  transfers between devices with their start and end apart: 39 -> 32, of which waited for: 11 -> 10; matrix products, arithmetic and copies ran while one was open for 1% -> 1% of each run, Pallas kernels for 15% -> 18%
where the time goes in v3:
time: 143 us; the launch traced here: 141 us
  starting transfers between devices  55.8 us (39%)
  Pallas kernels  43.2 us (30%)
  waiting for transfers between devices  38.6 us (27%)
  local copies, waits for them, and re-layouts  2.62 us (2%)
    ppermute x20, starting transfers between devices, shift(): return lax.ppermute(value, axis, pairs)  45.3 us
    pallas_call x21, Pallas kernels, kernel_call(): pl.pallas_call(run, out_shape=outs, in_specs=[HBM if isinstance(q, Load)...  43.2 us
    ppermute x3, waiting for transfers between devices, four(): return [value] + [lax.ppermute(value, axis, pairs_of(s)) for s in (1, 2, 3)]  14.1 us
    ppermute x20, waiting for transfers between devices, shift(): return lax.ppermute(value, axis, pairs)  12 us
    ppermute x1, waiting for transfers between devices, per_device(): other = lax.ppermute(rows, 'lon', [(i, i ^ 2) for i in range(LON)])  4.95 us
    ppermute x1, waiting for transfers between devices, per_device(): partner = lax.ppermute(proc_send, 'lat', [(i, i ^ 1) for i in range(8)])  3.95 us
    ppermute x3, starting transfers between devices, four(): return [value] + [lax.ppermute(value, axis, pairs_of(s)) for s in (1, 2, 3)]  3.75 us
    ppermute x1, waiting for transfers between devices, per_device(): across = lax.ppermute(apart, 'lat', along_z(2))  3.62 us
  transfers between devices with their start and end apart: 32, of which 10 were waited for; matrix products, arithmetic and copies ran while one was open for 1% of the time, Pallas kernels for 18%

profile of v3, /device:TPU:4, one launch (start us, length us, event | category | flops | bytes accessed | tf_op | source)
XLA Modules:
  0.0 141.3 jit_solution(1260434962697275703)
XLA Ops:
  1.8 3.8 %collective-permute-start.3 = (bf16[176,512]{1,0:T(8,128)(2,1)S(1)}, bf16[176,512]{1,0:T(8,128)(2,1)S(1)}, u32[]{:S(2)}, u32[]{:S(2)}) collective-permute-start(bf16[176,512]{1,0:T(8,128)(2,1)S(1)} %get-tuple-element.54), channel_id=1, source_target_pairs={{0,15},{1,0},{2,1},{3,2},{4,3},{5,4},{6,5},{7,6},{8,7},{9,8},{10,9... | collective-permute-start | bytes 540680 | tf_op jit(solution)/shard_map/ppermute | solution.py:565
  5.6 3.8 %collective-permute-start = (bf16[176,512]{1,0:T(8,128)(2,1)S(1)}, bf16[176,512]{1,0:T(8,128)(2,1)S(1)}, u32[]{:S(2)}, u32[]{:S(2)}) collective-permute-start(bf16[176,512]{1,0:T(8,128)(2,1)S(1)} %get-tuple-element.54), channel_id=1, source_target_pairs={{0,16},{16,32},{32,48},{48,64},{64,80},{80,96},{96,112},{1,17},{17... | collective-permute-start | bytes 540680 | tf_op jit(solution)/shard_map/ppermute | solution.py:565
  12.6 2.9 %embed.1 = (bf16[1024,512]{1,0:T(8,128)(2,1)S(1)}, bf16[512,512]{1,0:T(8,128)(2,1)S(1)}, bf16[512,512]{1,0:T(8,128)(2,1)S(1)}) custom-call(bf16[1024,474]{1,0:T(8,128)(2,1)S(1)} %bitcast.11, bf16[474,512]{1,0:T(8,128)(2,1)} %refs_1_.5, bf16[512,512]{1,0:T(8,128)(2,1)} %refs_2_.5, bf16[3,3,512,512]{3,2,1,0:T(8,128)(2,1)} %refs_1_.7, ...), custom_call_target="tpu_custom_call" | custom-call | flops 1073741824 | bytes 4194304 | tf_op jit(solution)/shard_map/embed/pallas_call | solution.py:137
  16.3 2.4 %collective-permute-done.1.refs_1_ = bf16[176,512]{1,0:T(8,128)(2,1)S(1)} collective-permute-done((bf16[176,512]{1,0:T(8,128)(2,1)S(1)}, bf16[176,512]{1,0:T(8,128)(2,1)S(1)}, u32[]{:S(2)}, u32[]{:S(2)}) %collective-permute-start.1) | collective-permute-done | bytes 180256 | tf_op jit(solution)/shard_map/ppermute | solution.py:565
  18.8 3.8 %collective-permute-start.5 = (bf16[2,176,512]{2,1,0:T(8,128)(2,1)S(1)}, bf16[2,176,512]{2,1,0:T(8,128)(2,1)}, u32[]{:S(2)}, u32[]{:S(2)}) collective-permute-start(bf16[2,176,512]{2,1,0:T(8,128)(2,1)S(1)} %pair.2.refs_3_.refs_4_), channel_id=1, source_target_pairs={{0,15},{1,0},{2,1},{3,2},{4,3},{5,4},{6,5},{7,6},{8,7},{9,8},{10,9... | collective-permute-start | bytes 1081352 | tf_op jit(solution)/shard_map/ppermute | solution.py:565
  23.8 4.1 %beside.1 = (bf16[128,512]{1,0:T(8,128)(2,1)S(1)}, bf16[128,512]{1,0:T(8,128)(2,1)S(1)}, bf16[128,512]{1,0:T(8,128)(2,1)S(1)}, bf16[128,512]{1,0:T(8,128)(2,1)S(1)}, bf16[16,256]{1,0:T(8,128)(2,1)S(1)}) custom-call(s32[1,5]{1,0:T(1,128)S(1)} %bitcast.13, bf16[176,512]{1,0:T(8,128)(2,1)S(1)} %collective-permute-done.2.refs_2_.refs_1_, ...), custom_call_target="tpu_custom_call" | custom-call | flops 1073741824 | bytes 5242880 | tf_op jit(solution)/shard_map/beside/pallas_call | solution.py:137
  27.9 5.1 %own.1.refs_6_.refs_0_ = f32[128,512]{1,0:T(8,128)S(1)} custom-call(bf16[1,1,128,512]{3,2,1,0:T(8,128)(2,1)} %refs_5_.5, bf16[64,512]{1,0:T(8,128)(2,1)S(1)} %get-tuple-element.60.refs_1_, bf16[1024,512]{1,0:T(8,128)(2,1)S(1)} %send.1.refs_2_.refs_5_.refs_8_, bf16[512,512]{1,0:T(8,128)(2,1)S(1)} %copy-done.3, ...), custom_call_target="tpu_custom_call" | custom-call | flops 2684354560 | bytes 3145728 | tf_op jit(solution)/shard_map/own/pallas_call | solution.py:137
  33.1 4.8 %corners.1 = (bf16[128,512]{1,0:T(8,128)(2,1)S(1)}, bf16[128,512]{1,0:T(8,128)(2,1)S(1)}, bf16[128,512]{1,0:T(8,128)(2,1)S(1)}, bf16[128,512]{1,0:T(8,128)(2,1)S(1)}, bf16[16,256]{1,0:T(8,128)(2,1)S(1)}) custom-call(s32[1,5]{1,0:T(1,128)S(1)} %bitcast.14, bf16[2,176,512]{2,1,0:T(8,128)(2,1)} %collective-permute-done.4.refs_1_.refs_2_, ...), custom_call_target="tpu_custom_call" | custom-call | flops 1073741824 | bytes 5242880 | tf_op jit(solution)/shard_map/corners/pallas_call | solution.py:137
  38.0 3.8 %collective-permute-start.7 = (bf16[2,128,512]{2,1,0:T(8,128)(2,1)S(1)}, bf16[2,128,512]{2,1,0:T(8,128)(2,1)S(1)}, u32[]{:S(2)}, u32[]{:S(2)}) collective-permute-start(bf16[2,128,512]{2,1,0:T(8,128)(2,1)S(1)} %get-tuple-element.66.refs_4_), channel_id=1, source_target_pairs={{0,15},{1,0},{2,1},{3,2},{4,3},{5,4},{6,5},{7,6},{8,7},{9,8},{10,9... | collective-permute-start | bytes 786440 | tf_op jit(solution)/shard_map/ppermute | solution.py:565
  41.8 3.5 %prep.1 = (f32[6,128,16]{2,1,0:T(8,128)S(1)}, f32[3,1024,16]{2,1,0:T(8,128)S(1)}, bf16[512,512]{1,0:T(8,128)(2,1)S(1)}, bf16[512,512]{1,0:T(8,128)(2,1)S(1)}, bf...) custom-call(s32[1,1,768]{2,1,0:T(1,128)} %refs_0_.4, ...), custom_call_target="tpu_custom_call" | custom-call | flops 536870912 | tf_op jit(solution)/shard_map/prep/pallas_call | solution.py:137
  45.3 2.0 %collective-permute-done.6.refs_2_ = bf16[2,128,512]{2,1,0:T(8,128)(2,1)S(1)} collective-permute-done((bf16[2,128,512]{2,1,0:T(8,128)(2,1)S(1)}, bf16[2,128,512]{2,1,0:T(8,128)(2,1)S(1)}, u32[]{:S(2)}, u32[]{:S(2)}) %collective-permute-start.6) | collective-permute-done | bytes 262176 | tf_op jit(solution)/shard_map/ppermute | solution.py:565
  47.4 3.9 %collective-permute-start.10 = (bf16[128,512]{1,0:T(8,128)(2,1)S(1)}, bf16[128,512]{1,0:T(8,128)(2,1)S(1)}, u32[]{:S(2)}, u32[]{:S(2)}) collective-permute-start(bf16[128,512]{1,0:T(8,128)(2,1)S(1)} %get-tuple-element.77), channel_id=1, source_target_pairs={{0,16},{16,32},{32,48},{48,64},{64,80},{80,96},{96,112},{1,17},{17... | collective-permute-start | bytes 393224 | tf_op jit(solution)/shard_map/ppermute | solution.py:565
  51.3 3.5 %collective-permute-start.11 = (bf16[128,512]{1,0:T(8,128)(2,1)S(1)}, bf16[128,512]{1,0:T(8,128)(2,1)S(1)}, u32[]{:S(2)}, u32[]{:S(2)}) collective-permute-start(bf16[128,512]{1,0:T(8,128)(2,1)S(1)} %get-tuple-element.78), channel_id=1, source_target_pairs={{16,0},{32,16},{48,32},{64,48},{80,64},{96,80},{112,96},{17,1},{33... | collective-permute-start | bytes 393224 | tf_op jit(solution)/shard_map/ppermute | solution.py:565
  54.9 3.8 %collective-permute-start.9 = (bf16[128,512]{1,0:T(8,128)(2,1)S(1)}, bf16[128,512]{1,0:T(8,128)(2,1)S(1)}, u32[]{:S(2)}, u32[]{:S(2)}) collective-permute-start(bf16[128,512]{1,0:T(8,128)(2,1)S(1)} %get-tuple-element.76), channel_id=1, source_target_pairs={{0,15},{1,0},{2,1},{3,2},{4,3},{5,4},{6,5},{7,6},{8,7},{9,8},{10,9... | collective-permute-start | bytes 393224 | tf_op jit(solution)/shard_map/ppermute | solution.py:565
  58.7 2.6 %collective-permute-done.11.refs_4_ = bf16[128,512]{1,0:T(8,128)(2,1)S(1)} collective-permute-done((bf16[128,512]{1,0:T(8,128)(2,1)S(1)}, bf16[128,512]{1,0:T(8,128)(2,1)S(1)}, u32[]{:S(2)}, u32[]{:S(2)}) %collective-permute-start.11) | collective-permute-done | bytes 131104 | tf_op jit(solution)/shard_map/ppermute | solution.py:565
  62.5 1.9 %node.1 = (bf16[128,512]{1,0:T(8,128)(2,1)S(1)}, bf16[128,512]{1,0:T(8,128)(2,1)S(1)}, bf16[128,512]{1,0:T(8,128)(2,1)S(1)}) custom-call(f32[128,512]{1,0:T(8,128)S(1)} %own.1.refs_6_.refs_0_, bf16[128,512]{1,0:T(8,128)(2,1)S(1)} %collective-permute-done.8.refs_1_, bf16[128,512]{1,0:T(8,128)(2,1)S(1)} %collective-permute-done.9.refs_2_, ...), custom_call_target="tpu_custom_call" | custom-call | flops 469762048 | bytes 4194304 | tf_op jit(solution)/shard_map/node/pallas_call | solution.py:137
  64.7 2.5 %grid.1 = (bf16[1024,512]{1,0:T(8,128)(2,1)S(1)}, f32[1024,512]{1,0:T(8,128)S(1)}) custom-call(bf16[1024,512]{1,0:T(8,128)(2,1)S(1)} %get-tuple-element.55.refs_0_, bf16[3,3,512,512]{3,2,1,0:T(8,128)(2,1)} %refs_1_.7, bf16[3,1024,512]{2,1,0:T(8,128)(2,1)} %refs_2_.7, bf16[128,512]{1,0:T(8,128)(2,1)S(1)} %get-tuple-element.85.refs_3_.refs_0_), custom_call_target="tpu_custom_call" | custom-call | flops 1073741824 | bytes 5242880 | tf_op jit(solution)/shard_map/grid/pallas_call | solution.py:137
  67.2 3.9 %collective-permute-done.12.refs_1_.refs_4_ = bf16[128,512]{1,0:T(8,128)(2,1)S(1)} collective-permute-done((bf16[128,512]{1,0:T(8,128)(2,1)S(1)}, bf16[128,512]{1,0:T(8,128)(2,1)S(1)}, u32[]{:S(2)}, u32[]{:S(2)}) %collective-permute-start.12) | collective-permute-done | bytes 131104 | tf_op jit(solution)/shard_map/ppermute | solution.py:760
  71.2 2.0 %collective-permute-start.14 = (bf16[144,512]{1,0:T(8,128)(2,1)S(1)}, bf16[144,512]{1,0:T(8,128)(2,1)S(1)}, u32[]{:S(2)}, u32[]{:S(2)}) collective-permute-start(bf16[144,512]{1,0:T(8,128)(2,1)S(1)} %get-tuple-element.89), channel_id=1, source_target_pairs={{0,32},{16,48},{32,64},{48,80},{64,96},{80,112},{96,0},{112,16},{1... | collective-permute-start | bytes 442376 | tf_op jit(solution)/shard_map/ppermute | solution.py:768
  74.5 2.0 %collective-permute-start.13 = (bf16[48,512]{1,0:T(8,128)(2,1)S(1)}, bf16[48,512]{1,0:T(8,128)(2,1)S(1)}, u32[]{:S(2)}, u32[]{:S(2)}) collective-permute-start(bf16[48,512]{1,0:T(8,128)(2,1)S(1)} %get-tuple-element.87), channel_id=1, source_target_pairs={{0,64},{16,80},{32,96},{48,112},{64,0},{80,16},{96,32},{112,48},{1... | collective-permute-start | bytes 147464 | tf_op jit(solution)/shard_map/ppermute | solution.py:770
  76.5 3.6 %collective-permute-done.13.refs_3_ = bf16[48,512]{1,0:T(8,128)(2,1)S(1)} collective-permute-done((bf16[48,512]{1,0:T(8,128)(2,1)S(1)}, bf16[48,512]{1,0:T(8,128)(2,1)S(1)}, u32[]{:S(2)}, u32[]{:S(2)}) %collective-permute-start.13) | collective-permute-done | bytes 49184 | tf_op jit(solution)/shard_map/ppermute | solution.py:770
  80.2 5.0 %collective-permute-done.16.refs_2_ = bf16[128,512]{1,0:T(8,128)(2,1)S(1)} collective-permute-done((bf16[128,512]{1,0:T(8,128)(2,1)S(1)}, bf16[128,512]{1,0:T(8,128)(2,1)S(1)}, u32[]{:S(2)}, u32[]{:S(2)}) %collective-permute-start.16) | collective-permute-done | bytes 131104 | tf_op jit(solution)/shard_map/ppermute | solution.py:778
  85.9 1.9 %collective-permute-start.20 = (bf16[256,512]{1,0:T(8,128)(2,1)S(1)}, bf16[256,512]{1,0:T(8,128)(2,1)S(1)}, u32[]{:S(2)}, u32[]{:S(2)}) collective-permute-start(bf16[256,512]{1,0:T(8,128)(2,1)S(1)} %get-tuple-element.92.refs_3_), channel_id=1, source_target_pairs={{0,8},{1,9},{2,10},{3,11},{4,12},{5,13},{6,14},{7,15},{8,0},{9,1},... | collective-permute-start | bytes 786440 | tf_op jit(solution)/shard_map/ppermute | solution.py:587
  91.1 14.0 %collective-permute-done.19.refs_6_.refs_4_ = bf16[256,512]{1,0:T(8,128)(2,1)S(1)} collective-permute-done((bf16[256,512]{1,0:T(8,128)(2,1)S(1)}, bf16[256,512]{1,0:T(8,128)(2,1)S(1)}, u32[]{:S(2)}, u32[]{:S(2)}) %collective-permute-start.19) | collective-permute-done | bytes 262176 | tf_op jit(solution)/shard_map/ppermute | solution.py:587
  109.8 2.8 %mesh.1.refs_2_ = bf16[128,512]{1,0:T(8,128)(2,1)S(1)} custom-call(s32[1,1]{1,0:T(1,128)} %get-tuple-element.88.refs_0_, f32[128,512]{1,0:T(8,128)S(1)} %fine.1.refs_1_, f32[768,16]{1,0:T(8,128)S(1)} %get-tuple-element.93.refs_7_.refs_2_, bf16[256,512]{1,0:T(8,128)(2,1)S(1)} %get-tuple-element.92.refs_3_, ...), custom_call_target="tpu_custom_call" | custom-call | flops 2147483648 | bytes 6291456 | tf_op jit(solution)/shard_map/mesh/pallas_call | solution.py:137
  112.5 4.2 %collective-permute-start.28 = (bf16[128,512]{1,0:T(8,128)(2,1)S(1)}, bf16[128,512]{1,0:T(8,128)(2,1)S(1)}, u32[]{:S(2)}, u32[]{:S(2)}) collective-permute-start(bf16[128,512]{1,0:T(8,128)(2,1)S(1)} %mesh.1.refs_2_), channel_id=1, source_target_pairs={{0,16},{16,32},{32,48},{48,64},{64,80},{80,96},{96,112},{1,17},{17... | collective-permute-start | bytes 393224 | tf_op jit(solution)/shard_map/ppermute | solution.py:565
  116.8 3.1 %collective-permute-start.29 = (bf16[128,512]{1,0:T(8,128)(2,1)S(1)}, bf16[128,512]{1,0:T(8,128)(2,1)S(1)}, u32[]{:S(2)}, u32[]{:S(2)}) collective-permute-start(bf16[128,512]{1,0:T(8,128)(2,1)S(1)} %mesh.1.refs_2_), channel_id=1, source_target_pairs={{16,0},{32,16},{48,32},{64,48},{80,64},{96,80},{112,96},{17,1},{33... | collective-permute-start | bytes 393224 | tf_op jit(solution)/shard_map/ppermute | solution.py:565
  120.0 3.8 %collective-permute-start.27 = (bf16[128,512]{1,0:T(8,128)(2,1)S(1)}, bf16[128,512]{1,0:T(8,128)(2,1)S(1)}, u32[]{:S(2)}, u32[]{:S(2)}) collective-permute-start(bf16[128,512]{1,0:T(8,128)(2,1)S(1)} %mesh.1.refs_2_), channel_id=1, source_target_pairs={{0,15},{1,0},{2,1},{3,2},{4,3},{5,4},{6,5},{7,6},{8,7},{9,8},{10,9... | collective-permute-start | bytes 393224 | tf_op jit(solution)/shard_map/ppermute | solution.py:565
  123.8 3.6 %collective-permute-done.29.refs_1_ = bf16[128,512]{1,0:T(8,128)(2,1)S(1)} collective-permute-done((bf16[128,512]{1,0:T(8,128)(2,1)S(1)}, bf16[128,512]{1,0:T(8,128)(2,1)S(1)}, u32[]{:S(2)}, u32[]{:S(2)}) %collective-permute-start.29) | collective-permute-done | bytes 131104 | tf_op jit(solution)/shard_map/ppermute | solution.py:565
  127.5 3.8 %collective-permute-start.31 = (bf16[2,128,512]{2,1,0:T(8,128)(2,1)S(1)}, bf16[2,128,512]{2,1,0:T(8,128)(2,1)S(1)}, u32[]{:S(2)}, u32[]{:S(2)}) collective-permute-start(bf16[2,128,512]{2,1,0:T(8,128)(2,1)S(1)} %pair.3.refs_4_), channel_id=1, source_target_pairs={{0,15},{1,0},{2,1},{3,2},{4,3},{5,4},{6,5},{7,6},{8,7},{9,8},{10,9... | collective-permute-start | bytes 786440 | tf_op jit(solution)/shard_map/ppermute | solution.py:565
  131.4 4.5 %early.1.refs_1_ = f32[3,1024,512]{2,1,0:T(8,128)S(1)} custom-call(f32[3,1024,16]{2,1,0:T(8,128)S(1)} %get-tuple-element.67.refs_0_, bf16[128,512]{1,0:T(8,128)(2,1)S(1)} %collective-permute-done.26.refs_1_, bf16[128,512]{1,0:T(8,128)(2,1)S(1)} %mesh.1.refs_2_, bf16[128,512]{1,0:T(8,128)(2,1)S(1)} %collective-permute-done.27.refs_3_, ...), custom_call_target="tpu_custom_call" | custom-call | flops 2147483648 | bytes 8388608 | tf_op jit(solution)/shard_map/early/pallas_call | solution.py:137
  136.1 5.2 %decode.1 = bf16[227,1024]{1,0:T(8,128)(2,1)} custom-call(f32[3,1024,16]{2,1,0:T(8,128)S(1)} %get-tuple-element.67.refs_0_, f32[3,1024,512]{2,1,0:T(8,128)S(1)} %early.1.refs_1_, bf16[2,128,512]{2,1,0:T(8,128)(2,1)S(1)} %collective-permute-done.30.refs_2_, bf16[2,128,512]{2,1,0:T(8,128)(2,1)S(1)} %collective-permute-done.31.refs_3_, ...), custom_call_target="tpu_custom_call" | custom-call | flops 2684354560 | bytes 8388608 | tf_op jit(solution)/shard_map/decode/pallas_call | solution.py:137
  (63 shorter events, 18.4 us)
Async XLA Ops:
  1.7 13.8 %collective-permute-start.2 = (bf16[176,512]{1,0:T(8,128)(2,1)S(1)}, bf16[176,512]{1,0:T(8,128)(2,1)S(1)}, u32[]{:S(2)}, u32[]{:S(2)}) collective-permute-start(bf16[176,512]{1,0:T(8,128)(2,1)S(1)} %get-tuple-element.54), channel_id=1, source_target_pairs={{0,1},{1,2},{2,3},{3,4},{4,5},{5,6},{6,7},{7,8},{8,9},{9,10},{10,1... | collective-permute-start | bytes 540680 | tf_op jit(solution)/shard_map/ppermute | solution.py:565
  1.8 13.7 %collective-permute-start.3 = (bf16[176,512]{1,0:T(8,128)(2,1)S(1)}, bf16[176,512]{1,0:T(8,128)(2,1)S(1)}, u32[]{:S(2)}, u32[]{:S(2)}) collective-permute-start(bf16[176,512]{1,0:T(8,128)(2,1)S(1)} %get-tuple-element.54), channel_id=1, source_target_pairs={{0,15},{1,0},{2,1},{3,2},{4,3},{5,4},{6,5},{7,6},{8,7},{9,8},{10,9... | collective-permute-start | bytes 540680 | tf_op jit(solution)/shard_map/ppermute | solution.py:565
  5.6 10.6 %collective-permute-start = (bf16[176,512]{1,0:T(8,128)(2,1)S(1)}, bf16[176,512]{1,0:T(8,128)(2,1)S(1)}, u32[]{:S(2)}, u32[]{:S(2)}) collective-permute-start(bf16[176,512]{1,0:T(8,128)(2,1)S(1)} %get-tuple-element.54), channel_id=1, source_target_pairs={{0,16},{16,32},{32,48},{48,64},{64,80},{80,96},{96,112},{1,17},{17... | collective-permute-start | bytes 540680 | tf_op jit(solution)/shard_map/ppermute | solution.py:565
  9.4 9.3 %collective-permute-start.1 = (bf16[176,512]{1,0:T(8,128)(2,1)S(1)}, bf16[176,512]{1,0:T(8,128)(2,1)S(1)}, u32[]{:S(2)}, u32[]{:S(2)}) collective-permute-start(bf16[176,512]{1,0:T(8,128)(2,1)S(1)} %get-tuple-element.54), channel_id=1, source_target_pairs={{0,112},{16,0},{32,16},{48,32},{64,48},{80,64},{96,80},{112,96},{1... | collective-permute-start | bytes 540680 | tf_op jit(solution)/shard_map/ppermute | solution.py:565
  18.7 14.3 %collective-permute-start.4 = (bf16[2,176,512]{2,1,0:T(8,128)(2,1)S(1)}, bf16[2,176,512]{2,1,0:T(8,128)(2,1)}, u32[]{:S(2)}, u32[]{:S(2)}) collective-permute-start(bf16[2,176,512]{2,1,0:T(8,128)(2,1)S(1)} %pair.2.refs_3_.refs_4_), channel_id=1, source_target_pairs={{0,1},{1,2},{2,3},{3,4},{4,5},{5,6},{6,7},{7,8},{8,9},{9,10},{10,1... | collective-permute-start | bytes 1081352 | tf_op jit(solution)/shard_map/ppermute | solution.py:565
  18.8 14.3 %collective-permute-start.5 = (bf16[2,176,512]{2,1,0:T(8,128)(2,1)S(1)}, bf16[2,176,512]{2,1,0:T(8,128)(2,1)}, u32[]{:S(2)}, u32[]{:S(2)}) collective-permute-start(bf16[2,176,512]{2,1,0:T(8,128)(2,1)S(1)} %pair.2.refs_3_.refs_4_), channel_id=1, source_target_pairs={{0,15},{1,0},{2,1},{3,2},{4,3},{5,4},{6,5},{7,6},{8,7},{9,8},{10,9... | collective-permute-start | bytes 1081352 | tf_op jit(solution)/shard_map/ppermute | solution.py:565
  37.9 9.4 %collective-permute-start.6 = (bf16[2,128,512]{2,1,0:T(8,128)(2,1)S(1)}, bf16[2,128,512]{2,1,0:T(8,128)(2,1)S(1)}, u32[]{:S(2)}, u32[]{:S(2)}) collective-permute-start(bf16[2,128,512]{2,1,0:T(8,128)(2,1)S(1)} %get-tuple-element.72), channel_id=1, source_target_pairs={{0,1},{1,2},{2,3},{3,4},{4,5},{5,6},{6,7},{7,8},{8,9},{9,10},{10,1... | collective-permute-start | bytes 786440 | tf_op jit(solution)/shard_map/ppermute | solution.py:565
  38.0 9.4 %collective-permute-start.7 = (bf16[2,128,512]{2,1,0:T(8,128)(2,1)S(1)}, bf16[2,128,512]{2,1,0:T(8,128)(2,1)S(1)}, u32[]{:S(2)}, u32[]{:S(2)}) collective-permute-start(bf16[2,128,512]{2,1,0:T(8,128)(2,1)S(1)} %get-tuple-element.66.refs_4_), channel_id=1, source_target_pairs={{0,15},{1,0},{2,1},{3,2},{4,3},{5,4},{6,5},{7,6},{8,7},{9,8},{10,9... | collective-permute-start | bytes 786440 | tf_op jit(solution)/shard_map/ppermute | solution.py:565
  47.4 11.3 %collective-permute-start.10 = (bf16[128,512]{1,0:T(8,128)(2,1)S(1)}, bf16[128,512]{1,0:T(8,128)(2,1)S(1)}, u32[]{:S(2)}, u32[]{:S(2)}) collective-permute-start(bf16[128,512]{1,0:T(8,128)(2,1)S(1)} %get-tuple-element.77), channel_id=1, source_target_pairs={{0,16},{16,32},{32,48},{48,64},{64,80},{80,96},{96,112},{1,17},{17... | collective-permute-start | bytes 393224 | tf_op jit(solution)/shard_map/ppermute | solution.py:565
  51.3 10.0 %collective-permute-start.11 = (bf16[128,512]{1,0:T(8,128)(2,1)S(1)}, bf16[128,512]{1,0:T(8,128)(2,1)S(1)}, u32[]{:S(2)}, u32[]{:S(2)}) collective-permute-start(bf16[128,512]{1,0:T(8,128)(2,1)S(1)} %get-tuple-element.78), channel_id=1, source_target_pairs={{16,0},{32,16},{48,32},{64,48},{80,64},{96,80},{112,96},{17,1},{33... | collective-permute-start | bytes 393224 | tf_op jit(solution)/shard_map/ppermute | solution.py:565
  54.8 7.7 %collective-permute-start.8 = (bf16[128,512]{1,0:T(8,128)(2,1)S(1)}, bf16[128,512]{1,0:T(8,128)(2,1)S(1)}, u32[]{:S(2)}, u32[]{:S(2)}) collective-permute-start(bf16[128,512]{1,0:T(8,128)(2,1)S(1)} %get-tuple-element.75), channel_id=1, source_target_pairs={{0,1},{1,2},{2,3},{3,4},{4,5},{5,6},{6,7},{7,8},{8,9},{9,10},{10,1... | collective-permute-start | bytes 393224 | tf_op jit(solution)/shard_map/ppermute | solution.py:565
  54.9 7.6 %collective-permute-start.9 = (bf16[128,512]{1,0:T(8,128)(2,1)S(1)}, bf16[128,512]{1,0:T(8,128)(2,1)S(1)}, u32[]{:S(2)}, u32[]{:S(2)}) collective-permute-start(bf16[128,512]{1,0:T(8,128)(2,1)S(1)} %get-tuple-element.76), channel_id=1, source_target_pairs={{0,15},{1,0},{2,1},{3,2},{4,3},{5,4},{6,5},{7,6},{8,7},{9,8},{10,9... | collective-permute-start | bytes 393224 | tf_op jit(solution)/shard_map/ppermute | solution.py:565
  64.4 6.8 %collective-permute-start.12 = (bf16[128,512]{1,0:T(8,128)(2,1)S(1)}, bf16[128,512]{1,0:T(8,128)(2,1)S(1)}, u32[]{:S(2)}, u32[]{:S(2)}) collective-permute-start(bf16[128,512]{1,0:T(8,128)(2,1)S(1)} %get-tuple-element.85.refs_3_.refs_0_), channel_id=1, source_target_pairs={{0,16},{16,0},{32,48},{48,32},{64,80},{80,64},{96,112},{112,96},{1... | collective-permute-start | bytes 393224 | tf_op jit(solution)/shard_map/ppermute | solution.py:760
  71.2 8.9 %collective-permute-start.14 = (bf16[144,512]{1,0:T(8,128)(2,1)S(1)}, bf16[144,512]{1,0:T(8,128)(2,1)S(1)}, u32[]{:S(2)}, u32[]{:S(2)}) collective-permute-start(bf16[144,512]{1,0:T(8,128)(2,1)S(1)} %get-tuple-element.89), channel_id=1, source_target_pairs={{0,32},{16,48},{32,64},{48,80},{64,96},{80,112},{96,0},{112,16},{1... | collective-permute-start | bytes 442376 | tf_op jit(solution)/shard_map/ppermute | solution.py:768
  73.2 6.9 %collective-permute-start.15 = (bf16[144,512]{1,0:T(8,128)(2,1)S(1)}, bf16[144,512]{1,0:T(8,128)(2,1)S(1)}, u32[]{:S(2)}, u32[]{:S(2)}) collective-permute-start(bf16[144,512]{1,0:T(8,128)(2,1)S(1)} %get-tuple-element.89), channel_id=1, source_target_pairs={{0,96},{16,112},{32,0},{48,16},{64,32},{80,48},{96,64},{112,80},{1... | collective-permute-start | bytes 442376 | tf_op jit(solution)/shard_map/ppermute | solution.py:769
  74.5 5.6 %collective-permute-start.13 = (bf16[48,512]{1,0:T(8,128)(2,1)S(1)}, bf16[48,512]{1,0:T(8,128)(2,1)S(1)}, u32[]{:S(2)}, u32[]{:S(2)}) collective-permute-start(bf16[48,512]{1,0:T(8,128)(2,1)S(1)} %get-tuple-element.87), channel_id=1, source_target_pairs={{0,64},{16,80},{32,96},{48,112},{64,0},{80,16},{96,32},{112,48},{1... | collective-permute-start | bytes 147464 | tf_op jit(solution)/shard_map/ppermute | solution.py:770
  80.1 5.0 %collective-permute-start.16 = (bf16[128,512]{1,0:T(8,128)(2,1)S(1)}, bf16[128,512]{1,0:T(8,128)(2,1)S(1)}, u32[]{:S(2)}, u32[]{:S(2)}) collective-permute-start(bf16[128,512]{1,0:T(8,128)(2,1)S(1)} %bands.1.refs_1_), channel_id=1, source_target_pairs={{0,2},{1,3},{2,0},{3,1},{4,6},{5,7},{6,4},{7,5},{8,10},{9,11},{10,... | collective-permute-start | bytes 393224 | tf_op jit(solution)/shard_map/ppermute | solution.py:778
  85.7 20.0 %collective-permute-start.17 = (bf16[3,128,512]{2,1,0:T(8,128)(2,1)S(1)}, bf16[3,128,512]{2,1,0:T(8,128)(2,1)S(1)}, u32[]{:S(2)}, u32[]{:S(2)}) collective-permute-start(bf16[3,128,512]{2,1,0:T(8,128)(2,1)S(1)} %get-tuple-element.90.refs_2_), channel_id=1, source_target_pairs={{0,1},{1,2},{2,3},{3,4},{4,5},{5,6},{6,7},{7,8},{8,9},{9,10},{10,1... | collective-permute-start | bytes 1179656 | tf_op jit(solution)/shard_map/ppermute | solution.py:565
  85.8 19.4 %collective-permute-start.19 = (bf16[256,512]{1,0:T(8,128)(2,1)S(1)}, bf16[256,512]{1,0:T(8,128)(2,1)S(1)}, u32[]{:S(2)}, u32[]{:S(2)}) collective-permute-start(bf16[256,512]{1,0:T(8,128)(2,1)S(1)} %get-tuple-element.92.refs_3_), channel_id=1, source_target_pairs={{0,4},{1,5},{2,6},{3,7},{4,8},{5,9},{6,10},{7,11},{8,12},{9,13},{1... | collective-permute-start | bytes 786440 | tf_op jit(solution)/shard_map/ppermute | solution.py:587
  85.9 19.3 %collective-permute-start.20 = (bf16[256,512]{1,0:T(8,128)(2,1)S(1)}, bf16[256,512]{1,0:T(8,128)(2,1)S(1)}, u32[]{:S(2)}, u32[]{:S(2)}) collective-permute-start(bf16[256,512]{1,0:T(8,128)(2,1)S(1)} %get-tuple-element.92.refs_3_), channel_id=1, source_target_pairs={{0,8},{1,9},{2,10},{3,11},{4,12},{5,13},{6,14},{7,15},{8,0},{9,1},... | collective-permute-start | bytes 786440 | tf_op jit(solution)/shard_map/ppermute | solution.py:587
  87.8 17.9 %collective-permute-start.21 = (bf16[256,512]{1,0:T(8,128)(2,1)S(1)}, bf16[256,512]{1,0:T(8,128)(2,1)S(1)}, u32[]{:S(2)}, u32[]{:S(2)}) collective-permute-start(bf16[256,512]{1,0:T(8,128)(2,1)S(1)} %get-tuple-element.92.refs_3_), channel_id=1, source_target_pairs={{0,12},{1,13},{2,14},{3,15},{4,0},{5,1},{6,2},{7,3},{8,4},{9,5},{1... | collective-permute-start | bytes 786440 | tf_op jit(solution)/shard_map/ppermute | solution.py:587
  89.6 18.4 %collective-permute-start.18 = (bf16[3,128,512]{2,1,0:T(8,128)(2,1)S(1)}, bf16[3,128,512]{2,1,0:T(8,128)(2,1)S(1)}, u32[]{:S(2)}, u32[]{:S(2)}) collective-permute-start(bf16[3,128,512]{2,1,0:T(8,128)(2,1)S(1)} %get-tuple-element.90.refs_2_), channel_id=1, source_target_pairs={{0,15},{1,0},{2,1},{3,2},{4,3},{5,4},{6,5},{7,6},{8,7},{9,8},{10,9... | collective-permute-start | bytes 1179656 | tf_op jit(solution)/shard_map/ppermute | solution.py:565
  105.2 4.5 %collective-permute-start.22 = (bf16[256,512]{1,0:T(8,128)(2,1)S(1)}, bf16[256,512]{1,0:T(8,128)(2,1)S(1)}, u32[]{:S(2)}, u32[]{:S(2)}) collective-permute-start(bf16[256,512]{1,0:T(8,128)(2,1)S(1)} %get-tuple-element.92.refs_3_), channel_id=1, source_target_pairs={{0,1},{1,0},{2,3},{3,2},{4,5},{5,4},{6,7},{7,6},{8,9},{9,8},{10,11... | collective-permute-start | bytes 786440 | tf_op jit(solution)/shard_map/ppermute | solution.py:788
  105.2 4.5 %collective-permute-start.23 = (bf16[256,512]{1,0:T(8,128)(2,1)S(1)}, bf16[256,512]{1,0:T(8,128)(2,1)S(1)}, u32[]{:S(2)}, u32[]{:S(2)}) collective-permute-start(bf16[256,512]{1,0:T(8,128)(2,1)S(1)} %collective-permute-done.19.refs_6_.refs_4_), channel_id=1, source_target_pairs={{0,1},{1,0},{2,3},{3,2},{4,5},{5,4},{6,7},{7,6},{8,9},{9,8},{10,11... | collective-permute-start | bytes 786440 | tf_op jit(solution)/shard_map/ppermute | solution.py:788
  105.7 4.0 %collective-permute-start.24 = (bf16[256,512]{1,0:T(8,128)(2,1)S(1)}, bf16[256,512]{1,0:T(8,128)(2,1)S(1)}, u32[]{:S(2)}, u32[]{:S(2)}) collective-permute-start(bf16[256,512]{1,0:T(8,128)(2,1)S(1)} %collective-permute-done.20.refs_5_), channel_id=1, source_target_pairs={{0,1},{1,0},{2,3},{3,2},{4,5},{5,4},{6,7},{7,6},{8,9},{9,8},{10,11... | collective-permute-start | bytes 786440 | tf_op jit(solution)/shard_map/ppermute | solution.py:788
  105.8 4.0 %collective-permute-start.25 = (bf16[256,512]{1,0:T(8,128)(2,1)S(1)}, bf16[256,512]{1,0:T(8,128)(2,1)S(1)}, u32[]{:S(2)}, u32[]{:S(2)}) collective-permute-start(bf16[256,512]{1,0:T(8,128)(2,1)S(1)} %collective-permute-done.21.refs_6_), channel_id=1, source_target_pairs={{0,1},{1,0},{2,3},{3,2},{4,5},{5,4},{6,7},{7,6},{8,9},{9,8},{10,11... | collective-permute-start | bytes 786440 | tf_op jit(solution)/shard_map/ppermute | solution.py:788
  112.5 11.3 %collective-permute-start.28 = (bf16[128,512]{1,0:T(8,128)(2,1)S(1)}, bf16[128,512]{1,0:T(8,128)(2,1)S(1)}, u32[]{:S(2)}, u32[]{:S(2)}) collective-permute-start(bf16[128,512]{1,0:T(8,128)(2,1)S(1)} %mesh.1.refs_2_), channel_id=1, source_target_pairs={{0,16},{16,32},{32,48},{48,64},{64,80},{80,96},{96,112},{1,17},{17... | collective-permute-start | bytes 393224 | tf_op jit(solution)/shard_map/ppermute | solution.py:565
  116.8 10.7 %collective-permute-start.29 = (bf16[128,512]{1,0:T(8,128)(2,1)S(1)}, bf16[128,512]{1,0:T(8,128)(2,1)S(1)}, u32[]{:S(2)}, u32[]{:S(2)}) collective-permute-start(bf16[128,512]{1,0:T(8,128)(2,1)S(1)} %mesh.1.refs_2_), channel_id=1, source_target_pairs={{16,0},{32,16},{48,32},{64,48},{80,64},{96,80},{112,96},{17,1},{33... | collective-permute-start | bytes 393224 | tf_op jit(solution)/shard_map/ppermute | solution.py:565
  119.9 11.5 %collective-permute-start.26 = (bf16[128,512]{1,0:T(8,128)(2,1)S(1)}, bf16[128,512]{1,0:T(8,128)(2,1)S(1)}, u32[]{:S(2)}, u32[]{:S(2)}) collective-permute-start(bf16[128,512]{1,0:T(8,128)(2,1)S(1)} %mesh.1.refs_2_), channel_id=1, source_target_pairs={{0,1},{1,2},{2,3},{3,4},{4,5},{5,6},{6,7},{7,8},{8,9},{9,10},{10,1... | collective-permute-start | bytes 393224 | tf_op jit(solution)/shard_map/ppermute | solution.py:565
  120.0 11.4 %collective-permute-start.27 = (bf16[128,512]{1,0:T(8,128)(2,1)S(1)}, bf16[128,512]{1,0:T(8,128)(2,1)S(1)}, u32[]{:S(2)}, u32[]{:S(2)}) collective-permute-start(bf16[128,512]{1,0:T(8,128)(2,1)S(1)} %mesh.1.refs_2_), channel_id=1, source_target_pairs={{0,15},{1,0},{2,1},{3,2},{4,3},{5,4},{6,5},{7,6},{8,7},{9,8},{10,9... | collective-permute-start | bytes 393224 | tf_op jit(solution)/shard_map/ppermute | solution.py:565
  127.5 8.6 %collective-permute-start.30 = (bf16[2,128,512]{2,1,0:T(8,128)(2,1)S(1)}, bf16[2,128,512]{2,1,0:T(8,128)(2,1)S(1)}, u32[]{:S(2)}, u32[]{:S(2)}) collective-permute-start(bf16[2,128,512]{2,1,0:T(8,128)(2,1)S(1)} %pair.3.refs_4_), channel_id=1, source_target_pairs={{0,1},{1,2},{2,3},{3,4},{4,5},{5,6},{6,7},{7,8},{8,9},{9,10},{10,1... | collective-permute-start | bytes 786440 | tf_op jit(solution)/shard_map/ppermute | solution.py:565
  127.5 8.5 %collective-permute-start.31 = (bf16[2,128,512]{2,1,0:T(8,128)(2,1)S(1)}, bf16[2,128,512]{2,1,0:T(8,128)(2,1)S(1)}, u32[]{:S(2)}, u32[]{:S(2)}) collective-permute-start(bf16[2,128,512]{2,1,0:T(8,128)(2,1)S(1)} %pair.3.refs_4_), channel_id=1, source_target_pairs={{0,15},{1,0},{2,1},{3,2},{4,3},{5,4},{6,5},{7,6},{8,7},{9,8},{10,9... | collective-permute-start | bytes 786440 | tf_op jit(solution)/shard_map/ppermute | solution.py:565
  (4 other events, 13.1 us)
